TPU v7x, 32 devices: a whole 2x2x4 slice. The times are simulated.
32 devices in a mesh: groups: 2 (over x), mp: 16 (over z, y, core).
Axes of the slice: x: 2, y: 2, z: 4, core: 2. Of those that a mesh axis runs over, the one named last changes fastest.
Arguments:
- features: bfloat16 [32, 256, 128, 128], P(None, ('groups', 'mp')), parts along dimension 1, may hold values from -6 to 6
- cotangent: bfloat16 [32, 256, 128, 128], P(None, ('groups', 'mp')), parts along dimension 1, may hold values from -9 to 9
- spectral_weight: float32 [256, 2, 16, 32, 32], P('mp'), may hold values from -9 to 9
- pointwise_weight: bfloat16 [32, 32], replicated, may hold values from -1 to 1
- biases: float32 [32], replicated, may hold values from -3 to 3
Outputs:
- features_grad: bfloat16 [32, 256, 128, 128], P(None, ('groups', 'mp')), parts along dimension 1
- spectral_grad: float32 [512, 2, 16, 32, 32], P(('groups', 'mp')), parts along dimension 0
- pointwise_grad: float32 [64, 32], P('groups'), parts along dimension 0
- biases_grad: float32 [64], P('groups'), parts along dimension 0
There are 2 independent parts, one for each index of `groups`. A program takes and returns all parts, laid end to end along the dimension named above; an argument that names none is the same for every part. Nothing has to cross between parts.
All inputs are finite; a program needn't handle non-finite values.
Results may differ from a plain program's by a relative error of at most 0.007.
Values sent between devices are 32-bit elements; how exact they have to be, the bound alone decides.
No kernel may reach another device: no remote copies, remote signals or barrier semaphores. Data moves between devices by JAX's collectives and lax.ppermute only.
A program may use at most 128 MiB of HBM per device.

v0:
```python
import math

import jax
import jax.numpy as jnp
from jax import lax
from jax.sharding import PartitionSpec as P

NX = 128
NY = 128
NZ = 128
KX = 16
KY = 16
KZ = 16


precise = lax.Precision.HIGHEST


def axis_tables(length, mode_count, signed):
    freqs = jnp.arange(mode_count, dtype=jnp.int32) - (mode_count // 2 if signed else 0)
    spots = jnp.arange(length, dtype=jnp.int32)
    phases = (spots[:, None] * freqs[None, :] % length).astype(jnp.float32) * (
        2.0 * math.pi / length
    )
    return (jnp.cos(phases), jnp.sin(phases))


def spectrum_plane(data, z_cos, z_sin, y_cos, y_sin, z_scale):
    z_real = (
        jnp.einsum("cxyz,zk->kcxy", data, z_cos, preferred_element_type=jnp.float32)
        * z_scale[:, None, None, None]
    )
    z_imag = (
        -jnp.einsum("cxyz,zk->kcxy", data, z_sin, preferred_element_type=jnp.float32)
        * z_scale[:, None, None, None]
    )
    y_real = jnp.einsum("kcxy,yj->jkcx", z_real, y_cos, precision=precise) + jnp.einsum(
        "kcxy,yj->jkcx", z_imag, y_sin, precision=precise
    )
    y_imag = jnp.einsum("kcxy,yj->jkcx", z_imag, y_cos, precision=precise) - jnp.einsum(
        "kcxy,yj->jkcx", z_real, y_sin, precision=precise
    )
    stacked = jnp.stack([y_real, y_imag], axis=2)
    return stacked.reshape(KY * KZ, 2, stacked.shape[3], stacked.shape[4])


def spectrum_lines(part, x_cos, x_sin):
    a_real = part[:, 0]
    a_imag = part[:, 1]
    v_real = jnp.einsum("pcx,xk->pck", a_real, x_cos, precision=precise) + jnp.einsum(
        "pcx,xk->pck", a_imag, x_sin, precision=precise
    )
    v_imag = jnp.einsum("pcx,xk->pck", a_imag, x_cos, precision=precise) - jnp.einsum(
        "pcx,xk->pck", a_real, x_sin, precision=precise
    )
    return jnp.stack([v_real, v_imag], axis=1)


def space_lines(spec, x_cos, x_sin):
    u_real = spec[:, 0]
    u_imag = spec[:, 1]
    b_real = jnp.einsum("pck,xk->pcx", u_real, x_cos, precision=precise) - jnp.einsum(
        "pck,xk->pcx", u_imag, x_sin, precision=precise
    )
    b_imag = jnp.einsum("pck,xk->pcx", u_imag, x_cos, precision=precise) + jnp.einsum(
        "pck,xk->pcx", u_real, x_sin, precision=precise
    )
    return jnp.stack([b_real, b_imag], axis=1)


def space_plane(stacked, y_cos, y_sin, z_cos, z_sin):
    grid = stacked.reshape(KY, KZ, 2, stacked.shape[2], stacked.shape[3])
    q_real = grid[:, :, 0]
    q_imag = grid[:, :, 1]
    b_real = jnp.einsum("jkcx,yj->kcxy", q_real, y_cos, precision=precise) - jnp.einsum(
        "jkcx,yj->kcxy", q_imag, y_sin, precision=precise
    )
    b_imag = jnp.einsum("jkcx,yj->kcxy", q_imag, y_cos, precision=precise) + jnp.einsum(
        "jkcx,yj->kcxy", q_real, y_sin, precision=precise
    )
    return jnp.einsum("kcxy,zk->cxyz", b_real, z_cos, precision=precise) - jnp.einsum(
        "kcxy,zk->cxyz", b_imag, z_sin, precision=precise
    )


def modes_product(spec, weight):
    v_real, v_imag = (spec[:, 0], spec[:, 1])
    r_real, r_imag = (weight[:, 0], weight[:, 1])
    u_real = jnp.einsum("pck,pkco->pok", v_real, r_real, precision=precise) - jnp.einsum(
        "pck,pkco->pok", v_imag, r_imag, precision=precise
    )
    u_imag = jnp.einsum("pck,pkco->pok", v_real, r_imag, precision=precise) + jnp.einsum(
        "pck,pkco->pok", v_imag, r_real, precision=precise
    )
    return jnp.stack([u_real, u_imag], axis=1)


def modes_adjoint(dspec, weight):
    d_real, d_imag = (dspec[:, 0], dspec[:, 1])
    r_real, r_imag = (weight[:, 0], weight[:, 1])
    g_real = jnp.einsum("pok,pkco->pck", d_real, r_real, precision=precise) + jnp.einsum(
        "pok,pkco->pck", d_imag, r_imag, precision=precise
    )
    g_imag = jnp.einsum("pok,pkco->pck", d_imag, r_real, precision=precise) - jnp.einsum(
        "pok,pkco->pck", d_real, r_imag, precision=precise
    )
    return jnp.stack([g_real, g_imag], axis=1)


def modes_gradient(spec, dspec):
    v_real, v_imag = (spec[:, 0], spec[:, 1])
    d_real, d_imag = (dspec[:, 0], dspec[:, 1])
    w_real = jnp.einsum("pck,pok->pkco", v_real, d_real, precision=precise) + jnp.einsum(
        "pck,pok->pkco", v_imag, d_imag, precision=precise
    )
    w_imag = jnp.einsum("pck,pok->pkco", v_real, d_imag, precision=precise) - jnp.einsum(
        "pck,pok->pkco", v_imag, d_real, precision=precise
    )
    return jnp.stack([w_real, w_imag], axis=1)


def to_modes(partial_value, x_cos_mine, x_sin_mine):
    return lax.psum_scatter(
        spectrum_lines(partial_value, x_cos_mine, x_sin_mine), "mp", scatter_dimension=0, tiled=True
    )


def to_space(spec, x_cos_mine, x_sin_mine):
    return space_lines(lax.all_gather(spec, "mp", axis=0, tiled=True), x_cos_mine, x_sin_mine)


def shards(features, cotangent, spectral_weight, pointwise_weight, biases):
    blocks = lax.axis_size("mp")
    rows_mine = NX // blocks
    first_cell = lax.axis_index("mp") * rows_mine
    z_cos, z_sin = axis_tables(NZ, KZ, False)
    z_cos_low = z_cos.astype(jnp.bfloat16)
    z_sin_low = z_sin.astype(jnp.bfloat16)
    y_cos, y_sin = axis_tables(NY, KY, True)
    x_cos, x_sin = axis_tables(NX, KX, True)
    x_cos_mine = lax.dynamic_slice_in_dim(x_cos, first_cell, rows_mine, 0)
    x_sin_mine = lax.dynamic_slice_in_dim(x_sin, first_cell, rows_mine, 0)
    z_weight = jnp.where(jnp.arange(KZ) == 0, 1.0, 2.0).astype(jnp.float32) / float(NX * NY * NZ)
    unit_weight = jnp.ones((KZ,), jnp.float32)
    partial_value = spectrum_plane(features, z_cos_low, z_sin_low, y_cos, y_sin, unit_weight)
    spec = to_modes(partial_value, x_cos_mine, x_sin_mine)
    mixed = modes_product(spec, spectral_weight)
    spectral = space_plane(
        to_space(mixed, x_cos_mine, x_sin_mine),
        y_cos,
        y_sin,
        z_cos * z_weight[None, :],
        z_sin * z_weight[None, :],
    )
    local_mix = jnp.einsum(
        "oc,cxyz->oxyz", pointwise_weight, features, preferred_element_type=jnp.float32
    )
    preact = spectral + local_mix + biases[:, None, None, None]
    _, pullback = jax.vjp(jax.nn.gelu, preact)
    pre_grad = pullback(cotangent.astype(jnp.float32))[0].astype(jnp.bfloat16)
    dpartial = spectrum_plane(pre_grad, z_cos_low, z_sin_low, y_cos, y_sin, z_weight)
    dspec = to_modes(dpartial, x_cos_mine, x_sin_mine)
    spectral_grad = modes_gradient(spec, dspec)
    dmixed = modes_adjoint(dspec, spectral_weight)
    back = space_plane(to_space(dmixed, x_cos_mine, x_sin_mine), y_cos, y_sin, z_cos, z_sin)
    local_back = jnp.einsum(
        "oc,oxyz->cxyz", pointwise_weight, pre_grad, preferred_element_type=jnp.float32
    )
    features_grad = (back + local_back).astype(jnp.bfloat16)
    factor = float(NX * NY * NZ) ** (-0.5)
    mix_local = jnp.einsum("oxyz,cxyz->oc", pre_grad, features, preferred_element_type=jnp.float32)
    bias_local = jnp.sum(pre_grad, axis=(1, 2, 3), dtype=jnp.float32)
    mix_total, bias_total = lax.psum((mix_local, bias_local), "mp")
    return (features_grad, spectral_grad, mix_total * factor, bias_total * factor)


def solution(mesh):
    return jax.shard_map(
        shards,
        mesh=mesh,
        in_specs=(
            P(None, ("groups", "mp"), None, None),
            P(None, ("groups", "mp"), None, None),
            P("mp", None, None, None, None),
            P(),
            P(),
        ),
        out_specs=(
            P(None, ("groups", "mp"), None, None),
            P(("groups", "mp"), None, None, None, None),
            P("groups", None),
            P("groups"),
        ),
        check_vma=False,
    )
```

profile of v0, /device:TPU:0, one launch (start us, length us, event | category | flops | bytes accessed | tf_op | source)
XLA Modules:
  0.0 625.8 jit_solution(12048591459338722951)
XLA Ops:
  7.3 5.8 fusion.165
  15.6 8.9 %fusion.57 = f32[16,16,32,8]{2,0,3,1:T(8,128)S(1)} fusion(f32[16,32,8,128]{3,0,2,1:T(8,128)S(1)} %convolution_negate_fusion, s32[16]{0:T(128)S(1)} %iota_add_fusion), kind=kOutput, calls=%fused_computation.68 | convolution fusion | flops 100691968 | bytes 2359360 | tf_op jit(solution)/shard_map/kcxy,yj->jkcx/dot_general | solution.py:40
  24.4 10.1 %fusion.59 = f32[16,16,32,8]{2,0,3,1:T(8,128)} fusion(f32[16,32,8,128]{3,0,2,1:T(8,128)S(1)} %convolution_negate_fusion, s32[16]{0:T(128)S(1)} %iota_add_fusion), kind=kOutput, calls=%fused_computation.70 | convolution fusion | flops 100691968 | bytes 2359360 | tf_op jit(solution)/shard_map/kcxy,yj->jkcx/dot_general | solution.py:37
  34.5 11.1 %fusion.65 = f32[16,16,32,8]{2,0,3,1:T(8,128)} fusion(f32[16,16,32,8]{2,0,3,1:T(8,128)} %fusion.59, f32[16,32,8,128]{3,0,2,1:T(8,128)S(1)} %fusion.165, s32[16]{0:T(128)S(1)} %iota_add_fusion), kind=kOutput, calls=%fused_computation.78 | convolution fusion | flops 100757504 | bytes 2621504 | tf_op jit(solution)/shard_map/kcxy,yj->jkcx/dot_general | solution.py:37
  45.6 20.3 %fusion.68 = f32[16,16,32,8]{2,0,3,1:T(8,128)S(1)} fusion(f32[16,16,32,8]{2,0,3,1:T(8,128)S(1)} %fusion.57, f32[16,32,8,128]{3,0,2,1:T(8,128)S(1)} %fusion.165, s32[16]{0:T(128)S(1)} %iota_add_fusion), kind=kOutput, calls=%fused_computation.79 | convolution fusion | flops 100757504 | bytes 2621504 | tf_op jit(solution)/shard_map/kcxy,yj->jkcx/dot_general | solution.py:40
  75.7 75.4 %reduce-scatter.3.cloned.1.call-done = f32[16,2,32,16]{2,3,1,0:T(8,128)} async-done(((f32[256,2,32,16]{2,3,1,0:T(8,128)}), f32[16,2,32,16]{2,3,1,0:T(8,128)}) %reduce-scatter.3.cloned.1.call-update) | async-done | bytes 65552 | tf_op jit(solution)/shard_map/reduce_scatter | solution.py:123
  174.8 14.1 %fusion.17 = f32[32,8,128,128]{3,0,2,1:T(8,128)} fusion(bf16[32,8,128,128]{3,2,1,0:T(8,128)(2,1)} %param.5, bf16[32,32]{1,0:T(8,128)(2,1)S(1)} %copy-done), kind=kOutput, calls=%fused_computation.25 | convolution fusion | flops 268435456 | bytes 25167872 | tf_op jit(solution)/shard_map/oc,cxyz->oxyz/dot_general | solution.py:155
  188.9 35.2 %all-gather.3.cloned.1.call-done = f32[256,2,32,16]{2,3,1,0:T(8,128)} async-done(((f32[16,2,32,16]{2,3,1,0:T(8,128)}), f32[256,2,32,16]{2,3,1,0:T(8,128)}) %all-gather.3.cloned.1.call-update) | async-done | bytes 1048592 | tf_op jit(solution)/shard_map/all_gather | solution.py:129
  251.0 28.8 %fusion.47 = f32[32,8,128,128]{3,2,1,0:T(8,128)} fusion(f32[16,32,8,128]{3,0,2,1:T(8,128)S(1)} %copy-done.4, f32[16,32,8,128]{3,0,2,1:T(8,128)S(1)} %fusion.126, f32[16]{0:T(128)S(1)} %fusion.215), kind=kOutput, calls=%fused_computation.58 | convolution fusion | flops 805861376 | bytes 20971584 | tf_op jit(solution)/shard_map/kcxy,zk->cxyz/dot_general | solution.py:81
  279.8 43.8 %convert_reduce_fusion = (f32[32]{0:T(128)S(1)}, bf16[32,8,128,128]{3,2,1,0:T(8,128)(2,1)S(1)}) fusion(f32[32]{0:T(128)S(1)} %copy-done.9, f32[32,8,128,128]{3,0,2,1:T(8,128)} %fusion.17, f32[32,8,128,128]{3,2,1,0:T(8,128)} %fusion.47, f32[16]{0:T(128)S(1)} %fusion.215, f32[16,32,8,128]{3,0,2,1:T(8,128)S(1)} %fusion.148, ...), kind=kOutput, calls=%fused_computation.18 | convolution fusion | flops 914913280 | bytes 54526272 | tf_op jit(solution)/shard_map/kcxy,zk->cxyz/dot_general | solution.py:81
  326.0 8.9 %fusion.49 = f32[16,16,32,8]{2,0,3,1:T(8,128)S(1)} fusion(f32[16,32,8,128]{3,0,2,1:T(8,128)S(1)} %negate_multiply_fusion, s32[16]{0:T(128)S(1)} %iota_add_fusion), kind=kOutput, calls=%fused_computation.60 | convolution fusion | flops 100691968 | bytes 2359360 | tf_op jit(solution)/shard_map/kcxy,yj->jkcx/dot_general | solution.py:40
  334.9 9.1 %fusion.51 = f32[16,16,32,8]{2,0,3,1:T(8,128)S(1)} fusion(f32[16,32,8,128]{3,0,2,1:T(8,128)S(1)} %negate_multiply_fusion, s32[16]{0:T(128)S(1)} %iota_add_fusion), kind=kOutput, calls=%fused_computation.62 | convolution fusion | flops 100691968 | bytes 2359360 | tf_op jit(solution)/shard_map/kcxy,yj->jkcx/dot_general | solution.py:37
  346.3 8.9 %fusion.74 = f32[16,16,32,8]{2,0,3,1:T(8,128)S(1)} fusion(f32[16,16,32,8]{2,0,3,1:T(8,128)S(1)} %fusion.49, f32[16,32,8,128]{3,0,2,1:T(8,128)S(1)} %convolution_multiply_fusion, s32[16]{0:T(128)S(1)} %iota_add_fusion), kind=kOutput, calls=%fused_computation.81 | convolution fusion | flops 100757504 | bytes 2621504 | tf_op jit(solution)/shard_map/kcxy,yj->jkcx/dot_general | solution.py:40
  355.2 9.3 %fusion.71 = f32[16,16,32,8]{2,0,3,1:T(8,128)S(1)} fusion(f32[16,16,32,8]{2,0,3,1:T(8,128)S(1)} %fusion.51, f32[16,32,8,128]{3,0,2,1:T(8,128)S(1)} %convolution_multiply_fusion, s32[16]{0:T(128)S(1)} %iota_add_fusion), kind=kOutput, calls=%fused_computation.80 | convolution fusion | flops 100757504 | bytes 2621504 | tf_op jit(solution)/shard_map/kcxy,yj->jkcx/dot_general | solution.py:37
  373.2 15.4 %fusion.81 = f32[32,32]{1,0:T(8,128)S(1)} fusion(bf16[32,8,128,128]{3,2,1,0:T(8,128)(2,1)} %param.5, bf16[32,8,128,128]{3,2,1,0:T(8,128)(2,1)} %copy-done.1), kind=kOutput, calls=%fused_computation.94 | convolution fusion | flops 268435456 | bytes 16781312 | tf_op jit(solution)/shard_map/oxyz,cxyz->oc/dot_general | solution.py:171
  388.6 60.2 %all-reduce = (f32[32,32]{1,0:T(8,128)S(1)}, f32[32]{0:T(128)S(1)}) all-reduce(f32[32,32]{1,0:T(8,128)S(1)} %fusion.81, f32[32]{0:T(128)S(1)} %get-tuple-element.22), channel_id=1, replica_groups=mesh['groups'=2,'mp'=16] {'mp'}, use_global_device_ids=true, to_apply=%region_2.3 | all-reduce | flops 1056 | bytes 8448 | tf_op jit(solution)/shard_map/psum | solution.py:173
  449.9 8.3 %fusion.27 = f32[16,16,1,32]{3,2,1,0:T(1,128)S(1)} fusion(f32[16,32,16,1]{1,3,2,0:T(1,128)S(1)} %bitcast.300, f32[16,2,16,32,32]{4,3,2,1,0:T(8,128)} %param.7), kind=kOutput, calls=%fused_computation.35 | convolution fusion | flops 3145728 | bytes 4259840 | tf_op jit(solution)/shard_map/pok,pkco->pck/dot_general | solution.py:104
  458.2 8.3 %fusion.21 = f32[16,16,1,32]{3,2,1,0:T(1,128)S(1)} fusion(f32[16,32,16,1]{1,3,2,0:T(1,128)S(1)} %bitcast.301, f32[16,2,16,32,32]{4,3,2,1,0:T(8,128)} %param.7), kind=kOutput, calls=%fused_computation.29 | convolution fusion | flops 3145728 | bytes 4259840 | tf_op jit(solution)/shard_map/pok,pkco->pck/dot_general | solution.py:101
  466.6 8.3 %fusion.19 = f32[16,16,1,32]{3,2,1,0:T(1,128)S(1)} fusion(f32[16,32,16,1]{1,3,2,0:T(1,128)S(1)} %bitcast.296, f32[16,2,16,32,32]{4,3,2,1,0:T(8,128)} %param.7), kind=kOutput, calls=%fused_computation.27 | convolution fusion | flops 3145728 | bytes 4259840 | tf_op jit(solution)/shard_map/pok,pkco->pck/dot_general | solution.py:104
  474.9 8.7 %fusion.29 = f32[16,16,1,32]{3,2,1,0:T(1,128)S(1)} fusion(f32[16,32,16,1]{1,3,2,0:T(1,128)S(1)} %bitcast.297, f32[16,2,16,32,32]{4,3,2,1,0:T(8,128)} %param.7), kind=kOutput, calls=%fused_computation.37 | convolution fusion | flops 3145728 | bytes 4259840 | tf_op jit(solution)/shard_map/pok,pkco->pck/dot_general | solution.py:101
  485.6 14.3 %fusion.14 = f32[8,128,128,32]{2,3,1,0:T(8,128)} fusion(bf16[32,8,128,128]{3,2,1,0:T(8,128)(2,1)} %copy-done.1, bf16[32,32]{1,0:T(8,128)(2,1)S(1)} %copy-done), kind=kOutput, calls=%fused_computation.22 | convolution fusion | flops 268435456 | bytes 25167872 | tf_op jit(solution)/shard_map/oc,oxyz->cxyz/dot_general | solution.py:166
  506.8 25.6 %all-gather.5.cloned.1.call-done = f32[256,2,32,16]{2,3,1,0:T(8,128)} async-done(((f32[16,2,32,16]{2,3,1,0:T(8,128)}), f32[256,2,32,16]{2,3,1,0:T(8,128)}) %all-gather.5.cloned.1.call-update) | async-done | bytes 1048592 | tf_op jit(solution)/shard_map/all_gather | solution.py:129
  559.3 26.8 %fusion.44 = f32[32,8,128,128]{3,2,1,0:T(8,128)S(1)} fusion(f32[16,32,8,128]{3,0,2,1:T(8,128)S(1)} %copy-done.5, f32[16,32,8,128]{3,0,2,1:T(8,128)S(1)} %fusion.120), kind=kOutput, calls=%fused_computation.54 | convolution fusion | flops 805859328 | bytes 20971520 | tf_op jit(solution)/shard_map/kcxy,zk->cxyz/dot_general | solution.py:81
  586.2 32.6 %fusion.10 = bf16[32,8,128,128]{3,2,1,0:T(8,128)(2,1)} fusion(f32[8,128,128,32]{2,3,1,0:T(8,128)} %fusion.14, f32[32,8,128,128]{3,2,1,0:T(8,128)S(1)} %fusion.44, f32[16,32,8,128]{3,0,2,1:T(8,128)S(1)} %fusion.142, f32[16,32,8,128]{3,0,2,1:T(8,128)S(1)} %copy-done.3), kind=kOutput, calls=%fused_computation.15 | convolution fusion | flops 818442240 | bytes 46137344 | tf_op jit(solution)/shard_map/kcxy,zk->cxyz/dot_general | solution.py:81
  (105 shorter events, 112.5 us)
Async XLA Ops:
  7.2 167.6 %copy-start = (bf16[32,32]{1,0:T(8,128)(2,1)S(1)}, bf16[32,32]{1,0:T(8,128)(2,1)}, u32[]{:S(2)}) copy-start(bf16[32,32]{1,0:T(8,128)(2,1)} %param.8) | copy-start | bytes 6148
  7.2 144.0 %reduce-scatter.3.cloned.1.call-start = ((), (), s32[]{:S(2)}) async-start(), calls=%async_computation.2 | async-start | bytes 4456448 | tf_op jit(solution)/shard_map/reduce_scatter | solution.py:123
  7.2 5.8 copy-start.2
  75.7 148.5 %all-gather.3.cloned.1.call-start = ((), (), s32[]{:S(2)}) async-start(), calls=%async_computation.3 | async-start | bytes 4456448 | tf_op jit(solution)/shard_map/all_gather | solution.py:129
  174.3 274.6 %reduce-scatter.5.cloned.1.call-start = ((), (), s32[]{:S(2)}) async-start(), calls=%async_computation.4 | async-start | bytes 4456448 | tf_op jit(solution)/shard_map/reduce_scatter | solution.py:123
  247.0 3.9 copy-start.4
  249.0 30.8 %slice-start = ((s8[8388608]{0:T(1024)(128)(4,1)}), s8[4194304]{0:T(1024)(128)(4,1)S(1)}, s32[]{:S(2)}) async-start(s8[8388608]{0:T(1024)(128)(4,1)} %bitcast.310), calls=%async_computation.6 | async-start | bytes 8388608
  250.9 28.8 %copy-start.6 = (f32[16,32,8,128]{3,0,2,1:T(8,128)S(1)}, f32[16,32,8,128]{3,0,2,1:T(8,128)}, u32[]{:S(2)}) copy-start(f32[16,32,8,128]{3,0,2,1:T(8,128)} %fusion.124) | copy-start | bytes 6291460
  250.9 28.8 %slice-start.1 = ((s8[8388608]{0:T(1024)(128)(4,1)}), s8[4194304]{0:T(1024)(128)(4,1)S(1)}, s32[]{:S(2)}) async-start(s8[8388608]{0:T(1024)(128)(4,1)} %bitcast.310), calls=%async_computation.7 | async-start | bytes 8388608
  251.0 28.8 %copy-start.9 = (f32[32]{0:T(128)S(1)}, f32[32]{0:T(128)}, u32[]{:S(2)}) copy-start(f32[32]{0:T(128)} %param.9) | copy-start | bytes 388
  323.7 20.3 %copy-start.1 = (bf16[32,8,128,128]{3,2,1,0:T(8,128)(2,1)}, bf16[32,8,128,128]{3,2,1,0:T(8,128)(2,1)S(1)}, u32[]{:S(2)}) copy-start(bf16[32,8,128,128]{3,2,1,0:T(8,128)(2,1)S(1)} %get-tuple-element.23) | copy-start | bytes 25165828
  373.0 159.4 %all-gather.5.cloned.1.call-start = ((), (), s32[]{:S(2)}) async-start(), calls=%async_computation.5 | async-start | bytes 4456448 | tf_op jit(solution)/shard_map/all_gather | solution.py:129
  485.6 14.3 %copy-start.7 = (f32[16,16,32]{2,1,0:T(8,128)S(1)}, f32[16,16,32]{2,1,0:T(8,128)}, u32[]{:S(2)}) copy-start(f32[16,16,32]{2,1,0:T(8,128)} %get-tuple-element.12) | copy-start | bytes 98308
  485.6 14.3 %copy-start.8 = (f32[16,16,32]{2,1,0:T(8,128)S(1)}, f32[16,16,32]{2,1,0:T(8,128)}, u32[]{:S(2)}) copy-start(f32[16,16,32]{2,1,0:T(8,128)} %get-tuple-element.13) | copy-start | bytes 98308
  555.3 4.0 copy-start.5
  559.3 26.8 %copy-start.3 = (f32[16,32,8,128]{3,0,2,1:T(8,128)S(1)}, f32[16,32,8,128]{3,0,2,1:T(8,128)}, u32[]{:S(2)}) copy-start(f32[16,32,8,128]{3,0,2,1:T(8,128)} %fusion.118) | copy-start | bytes 6291460
Sparse Core Ops, SparseCore 0:
  75.8 75.3 reduce-scatter.2
  174.4 49.6 all-gather.2
  373.1 71.8 reduce-scatter.4
  484.6 47.7 all-gather.4
where the time goes:
time: 635 us; the launch traced here: 626 us
  matrix products  359 us (57%)
  waiting for transfers between devices  136 us (21%)
  blocking collectives  60.2 us (9%)
  local copies, waits for them, and re-layouts  44.5 us (7%)
  between operations  14.8 us (2%)
  other arithmetic  9.88 us (2%)
    dot_general x2, matrix products, space_plane(): jnp.einsum('kcxy,zk->cxyz', b_imag, z_sin, precision=precise)  76.5 us
    reduce_scatter x2, waiting for transfers between devices, to_modes(): lax.psum_scatter(spectrum_lines(partial_value, x_cos_mine, x_sin_mine), '...  75.4 us
    all_gather x2, waiting for transfers between devices, to_space(): lax.all_gather(spec, 'mp', axis=0, tiled=True)  60.8 us
    psum x1, blocking collectives, shards(): mix_total, bias_total = lax.psum((mix_local, bias_local), 'mp')  60.2 us
    dot_general x2, matrix products, space_plane(): jnp.einsum('kcxy,zk->cxyz', b_real, z_cos, precision=precise)  55.6 us
    dot_general x2, matrix products, spectrum_plane(): jnp.einsum('kcxy,yj->jkcx', z_real, y_sin, precision=precise)  29.2 us
    dot_general x2, matrix products, spectrum_plane(): jnp.einsum('kcxy,yj->jkcx', z_real, y_cos, precision=precise)  20.3 us
    dot_general x2, matrix products, spectrum_plane(): jnp.einsum('kcxy,yj->jkcx', z_imag, y_sin, precision=precise)  19.2 us
  transfers between devices with their start and end apart: 4, of which 3 were waited for; matrix products, arithmetic and copies ran while one was open for 8% of the time, Pallas kernels for 0%

commit v1 on v0

v1 whole, which is shorter than its diff:
```python
import functools
import math

import jax
import jax.numpy as jnp
import ml_dtypes
import numpy as np
from jax import lax
from jax.experimental import pallas as pl
from jax.experimental.pallas import tpu as pltpu
from jax.sharding import PartitionSpec as P

KX = 16
KY = 16
KZ = 16
XB = 4
CB = 8
YB = 16
VMEM = 56 << 20

F32 = jnp.float32
BF16 = jnp.bfloat16


def angles(length, modes, signed):
    freqs = np.arange(modes) - (modes // 2 if signed else 0)
    theta = (np.arange(length)[:, None] * freqs[None, :] % length) * (2.0 * math.pi / length)
    return np.cos(theta), np.sin(theta)


def bf16(table):
    return np.asarray(table, np.float32).astype(ml_dtypes.bfloat16)


@functools.cache
def plane_tables(ny, nz):
    yc, ys = angles(ny, KY, True)
    zc, zs = angles(nz, KZ, False)
    eye_x = np.eye(XB)
    rows = np.stack([np.stack([yc, -ys], 0), np.stack([-ys, -yc], 0)], 0)
    y_in = np.einsum("mryj,xw->mjrxwy", rows, eye_x).reshape(2 * KY * 2 * XB, XB * ny)
    z_in = np.einsum("mzk,cd->cmzkd", np.stack([zc, zs], 0), np.eye(CB)).reshape(CB, 2 * nz, KZ * CB)
    mix = np.stack([np.stack([yc, -ys], 0), np.stack([ys, yc], 0)], 0)
    y_out = np.einsum("qryj,xw->xqyjrw", mix, eye_x).reshape(XB, 2 * ny, KY * 2 * XB)
    z_out = np.einsum("qzk,cd->qkcdz", np.stack([zc, -zs], 0), np.eye(CB)).reshape(2 * KZ * CB, CB * nz)
    return bf16(y_in), bf16(z_in), bf16(y_out), bf16(z_out)


@functools.cache
def line_tables(nx):
    xc, xs = angles(nx, KX, True)
    inward = np.stack([np.stack([xc, -xs], 1), np.stack([xs, xc], 1)], 0)
    outward = np.stack([np.stack([xc, -xs], 1), np.stack([xs, xc], 1)], 0)
    blocks = nx // XB

    def order(table):
        return (
            table.reshape(2, blocks, XB, 2 * KX)
            .transpose(1, 0, 2, 3)
            .reshape(nx * 2, 2 * KX)
            .astype(np.float32)
        )

    return order(inward), order(outward)


@functools.cache
def lane_tables(pairs, channels):
    groups = channels // CB
    perm = np.einsum("kl,gh,cd->kgchld", np.eye(pairs), np.eye(groups), np.eye(CB))
    return bf16(perm.reshape(pairs * channels, pairs * channels))


def params(**kw):
    return pltpu.CompilerParams(vmem_limit_bytes=VMEM, **kw)


def exact_dot(a, b, dims):
    return lax.dot_general(a, b, (dims, ((), ())), precision=lax.Precision.HIGHEST, preferred_element_type=F32)


def dot(a, b):
    return jnp.dot(a, b, preferred_element_type=F32)


def split3(v):
    hi = v.astype(BF16)
    rest = v - hi.astype(F32)
    mid = rest.astype(BF16)
    return hi, mid, (rest - mid.astype(F32)).astype(BF16)


def analyse_group(planes, y_in, z_in_ref):
    total = None
    for c in range(0, CB, 2):
        pair = jnp.concatenate([planes(c), planes(c + 1)], axis=1)
        nz = pair.shape[1] // 2
        g = dot(y_in, pair).astype(BF16)
        half = g.shape[0] // 2
        for i in range(2):
            lhs = jnp.concatenate([g[:half, i * nz : (i + 1) * nz], g[half:, i * nz : (i + 1) * nz]], axis=1)
            term = dot(lhs, z_in_ref[c + i])
            total = term if total is None else total + term
    return total


def lines_kernel(f_ref, y_in_ref, z_in_ref, out_ref):
    y_in = y_in_ref[...]
    total = analyse_group(lambda c: f_ref[c].reshape(-1, f_ref.shape[-1]), y_in, z_in_ref)
    out_ref[:, 0] = total.reshape(out_ref.shape[0], 2 * XB, total.shape[1])


def feature_lines(features):
    channels, rows, ny, nz = features.shape
    y_in, z_in, _, _ = plane_tables(ny, nz)
    blocks = rows // XB
    return pl.pallas_call(
        lines_kernel,
        grid=(blocks, channels // CB),
        in_specs=[
            pl.BlockSpec((CB, XB, ny, nz), lambda h, g: (g, h, 0, 0)),
            pl.BlockSpec(y_in.shape, lambda h, g: (0, 0)),
            pl.BlockSpec(z_in.shape, lambda h, g: (0, 0, 0)),
        ],
        out_specs=pl.BlockSpec((KY, 1, 2 * XB, KZ * CB), lambda h, g: (0, h, 0, g)),
        out_shape=jax.ShapeDtypeStruct((KY, blocks, 2 * XB, KZ * channels), F32),
        compiler_params=params(),
        name="feature_lines",
    )(features, jnp.asarray(y_in), jnp.asarray(z_in))


def mix_kernel(scale_ref, lines_ref, w_ref, x_in_ref, x_out_ref, perm_ref, out_ref, spec_ref, rows_ref):
    k = pl.program_id(0)
    pairs = pl.num_programs(0)
    channels = w_ref.shape[-1]
    groups = channels // CB
    lanes = lines_ref.shape[1]
    per_group = lanes // groups

    @pl.when(k == 0)
    def _():
        spec_ref[...] = exact_dot(lines_ref[...].T, x_in_ref[...], ((1,), (0,)))

    v = jnp.concatenate(
        [spec_ref[pl.ds(pl.multiple_of(g * per_group + k * CB, CB), CB), :] for g in range(groups)], axis=0
    )
    reals, imags = [], []
    for a in range(KX):
        vr, vi = v[:, a : a + 1], v[:, KX + a : KX + a + 1]
        wr, wi = w_ref[0, 0, a], w_ref[0, 1, a]
        reals.append(jnp.sum(vr * wr - vi * wi, axis=0, keepdims=True))
        imags.append(jnp.sum(vr * wi + vi * wr, axis=0, keepdims=True))
    rows_ref[k] = jnp.concatenate(reals + imags, axis=0)

    @pl.when(k == pairs - 1)
    def _():
        mixed = jnp.concatenate([rows_ref[i] for i in range(rows_ref.shape[0])], axis=1)
        parts = dot(jnp.concatenate(split3(mixed), axis=0), perm_ref[...])
        n = mixed.shape[0]
        placed = (parts[2 * n :] + parts[n : 2 * n]) + parts[:n]
        out_ref[...] = exact_dot(x_out_ref[...], placed * scale_ref[...], ((1,), (0,)))


def whole(shape):
    return pl.BlockSpec(shape, lambda k: (0,) * len(shape))


def mix_modes(lines, weight, scale, x_in, x_out, perm):
    pairs, _, kx, channels, _ = weight.shape
    lanes = pairs * channels
    return pl.pallas_call(
        mix_kernel,
        grid=(pairs,),
        in_specs=[
            whole(scale.shape),
            whole(lines.shape),
            pl.BlockSpec((1, 2, kx, channels, channels), lambda k: (k, 0, 0, 0, 0)),
            whole(x_in.shape),
            whole(x_out.shape),
            whole(perm.shape),
        ],
        out_specs=[whole(lines.shape), whole((lanes, 2 * kx))],
        out_shape=[jax.ShapeDtypeStruct(lines.shape, F32), jax.ShapeDtypeStruct((lanes, 2 * kx), F32)],
        scratch_shapes=[pltpu.VMEM((pairs, 2 * kx, channels), F32)],
        compiler_params=params(),
        name="mix_modes",
    )(scale, lines, weight, x_in, x_out, perm)


def adjoint_kernel(scale_ref, lines_ref, w_ref, x_in_ref, x_out_ref, perm_ref, out_ref, dspec_ref, cols_ref):
    k = pl.program_id(0)
    pairs = pl.num_programs(0)
    channels = w_ref.shape[-1]
    groups = channels // CB
    lanes = lines_ref.shape[1]
    per_group = lanes // groups

    @pl.when(k == 0)
    def _():
        placed = exact_dot(x_in_ref[...].T, lines_ref[...], ((1,), (0,))) * scale_ref[...]
        n = placed.shape[0]
        parts = lax.dot_general(
            jnp.concatenate(split3(placed), axis=0), perm_ref[...], (((1,), (0,)), ((), ())), preferred_element_type=F32
        )
        rows = (parts[2 * n :] + parts[n : 2 * n]) + parts[:n]
        for i in range(dspec_ref.shape[0]):
            dspec_ref[i] = rows[:, i * channels : (i + 1) * channels]

    d = dspec_ref[k]
    lane = lax.broadcasted_iota(jnp.int32, (channels, 2 * KX), 1)
    cols = jnp.zeros((channels, 2 * KX), F32)
    for a in range(KX):
        dr, di = d[a : a + 1], d[KX + a : KX + a + 1]
        wr, wi = w_ref[0, 0, a], w_ref[0, 1, a]
        cols = jnp.where(lane == a, jnp.sum(dr * wr + di * wi, axis=1, keepdims=True), cols)
        cols = jnp.where(lane == KX + a, jnp.sum(di * wr - dr * wi, axis=1, keepdims=True), cols)
    for g in range(groups):
        cols_ref[pl.ds(pl.multiple_of(g * per_group + k * CB, CB), CB), :] = cols[g * CB : (g + 1) * CB]

    @pl.when(k == pairs - 1)
    def _():
        out_ref[...] = exact_dot(x_out_ref[...], cols_ref[...], ((1,), (1,)))


def adjoint_modes(lines, weight, scale, x_in, x_out, perm_back):
    pairs, _, kx, channels, _ = weight.shape
    lanes = pairs * channels
    return pl.pallas_call(
        adjoint_kernel,
        grid=(pairs,),
        in_specs=[
            whole(scale.shape),
            whole(lines.shape),
            pl.BlockSpec((1, 2, kx, channels, channels), lambda k: (k, 0, 0, 0, 0)),
            whole(x_in.shape),
            whole(x_out.shape),
            whole(perm_back.shape),
        ],
        out_specs=[whole(lines.shape), whole((pairs, 2 * kx, channels))],
        out_shape=[jax.ShapeDtypeStruct(lines.shape, F32), jax.ShapeDtypeStruct((pairs, 2 * kx, channels), F32)],
        scratch_shapes=[pltpu.VMEM((lanes, 2 * kx), F32)],
        compiler_params=params(),
        name="adjoint_modes",
    )(scale, lines, weight, x_in, x_out, perm_back)


def outer_kernel(spec_ref, dspec_ref, out_ref):
    k = pl.program_id(0)
    channels = dspec_ref.shape[-1]
    groups = channels // CB
    per_group = spec_ref.shape[0] // groups
    v = jnp.concatenate(
        [spec_ref[pl.ds(pl.multiple_of(g * per_group + k * CB, CB), CB), :] for g in range(groups)], axis=0
    )
    d = dspec_ref[0]
    for a in range(KX):
        vr, vi = v[:, a : a + 1], v[:, KX + a : KX + a + 1]
        dr, di = d[a : a + 1], d[KX + a : KX + a + 1]
        out_ref[0, 0, a] = vr * dr + vi * di
        out_ref[0, 1, a] = vr * di - vi * dr


def mode_gradient(spec, dspec):
    pairs, twice_kx, channels = dspec.shape
    shape = (pairs, 2, twice_kx // 2, channels, channels)
    return pl.pallas_call(
        outer_kernel,
        grid=(pairs,),
        in_specs=[whole(spec.shape), pl.BlockSpec((1, twice_kx, channels), lambda k: (k, 0, 0))],
        out_specs=pl.BlockSpec((1,) + shape[1:], lambda k: (k, 0, 0, 0, 0)),
        out_shape=jax.ShapeDtypeStruct(shape, F32),
        compiler_params=params(),
        name="mode_gradient",
    )(spec, dspec)


def synthesise(x, lines_ref, y_out_ref, z_out_ref, low_ref, b_ref, space_ref):
    within = lax.rem(x, XB)
    rows = KY * 2 * XB

    @pl.when(within == 0)
    def _():
        block = lines_ref[:, 0].reshape(rows, lines_ref.shape[-1])
        hi = block.astype(BF16)
        low_ref[:rows] = hi
        low_ref[rows:] = (block - hi.astype(F32)).astype(BF16)

    table = y_out_ref[within]
    b_ref[...] = dot(jnp.concatenate([table, table], axis=1), low_ref[...]).astype(BF16)
    ny = table.shape[0] // 2
    lanes = KZ * CB
    for g in range(space_ref.shape[0]):
        lhs = jnp.concatenate([b_ref[:ny, g * lanes : (g + 1) * lanes], b_ref[ny:, g * lanes : (g + 1) * lanes]], axis=1)
        space_ref[g] = dot(lhs, z_out_ref[...])


def channel_mix(kron, cells_ref, y):
    nz = cells_ref.shape[-1]
    tiles = [cells_ref[:, 0, y + t * YB : y + (t + 1) * YB, :].reshape(-1, nz) for t in range(2)]
    return dot(kron, jnp.concatenate(tiles, axis=1))


ROOT = math.sqrt(2.0 / math.pi)
CUBE = 0.044715 * ROOT


def gelu_slope(u):
    square = u * u
    t = jnp.tanh(u * (ROOT + CUBE * square))
    inner = u * (0.5 * ROOT + 1.5 * CUBE * square)
    return (1.0 + t) * (0.5 + (1.0 - t) * inner)


def slope_kernel(
    bias_ref, lines_ref, f_ref, cot_ref, kron_ref, y_in_ref, z_in_ref, y_out_ref, z_out_ref,
    grad_ref, out_ref, low_ref, b_ref, space_ref, keep_ref,
):
    x = pl.program_id(0)
    within = lax.rem(x, XB)
    channels, _, ny, nz = f_ref.shape
    synthesise(x, lines_ref, y_out_ref, z_out_ref, low_ref, b_ref, space_ref)
    for y in range(0, ny, 2 * YB):
        local = channel_mix(kron_ref[...], f_ref, y)
        for o in range(channels):
            g, c = divmod(o, CB)
            for t in range(2):
                first = y + t * YB
                u = (
                    space_ref[g, first : first + YB, c * nz : (c + 1) * nz]
                    + local[o * YB : (o + 1) * YB, t * nz : (t + 1) * nz]
                    + bias_ref[o]
                )
                grad = (gelu_slope(u) * cot_ref[o, 0, first : first + YB, :].astype(F32)).astype(BF16)
                grad_ref[o, 0, first : first + YB, :] = grad
                keep_ref[o, pl.ds(pl.multiple_of(within * ny + first, YB), YB), :] = grad

    @pl.when(within == XB - 1)
    def _():
        y_in = y_in_ref[...]
        lanes = KZ * CB
        for g in range(channels // CB):
            total = analyse_group(lambda c: keep_ref[g * CB + c], y_in, z_in_ref)
            out_ref[:, 0, :, g * lanes : (g + 1) * lanes] = total.reshape(out_ref.shape[0], 2 * XB, lanes)


def cells_specs(channels, ny, nz):
    return pl.BlockSpec((channels, 1, ny, nz), lambda x: (0, x, 0, 0))


def slope(lines, features, cotangent, kron, biases):
    channels, rows, ny, nz = features.shape
    y_in, z_in, y_out, z_out = plane_tables(ny, nz)
    blocks = rows // XB
    lanes = KZ * channels
    line_spec = pl.BlockSpec((KY, 1, 2 * XB, lanes), lambda x: (0, x // XB, 0, 0))
    cells = cells_specs(channels, ny, nz)
    return pl.pallas_call(
        slope_kernel,
        grid=(rows,),
        in_specs=[
            pl.BlockSpec(memory_space=pltpu.SMEM),
            line_spec,
            cells,
            cells,
            whole(kron.shape),
            whole(y_in.shape),
            whole(z_in.shape),
            whole(y_out.shape),
            whole(z_out.shape),
        ],
        out_specs=[cells, line_spec],
        out_shape=[
            jax.ShapeDtypeStruct(features.shape, BF16),
            jax.ShapeDtypeStruct((KY, blocks, 2 * XB, lanes), F32),
        ],
        scratch_shapes=[
            pltpu.VMEM((2 * KY * 2 * XB, lanes), BF16),
            pltpu.VMEM((2 * ny, lanes), BF16),
            pltpu.VMEM((channels // CB, ny, CB * nz), F32),
            pltpu.VMEM((channels, XB * ny, nz), BF16),
        ],
        compiler_params=params(),
        name="slope",
    )(biases, lines, features, cotangent, kron, jnp.asarray(y_in), jnp.asarray(z_in), jnp.asarray(y_out), jnp.asarray(z_out))


def back_kernel(lines_ref, grad_ref, kron_ref, y_out_ref, z_out_ref, out_ref, low_ref, b_ref, space_ref):
    x = pl.program_id(0)
    channels, _, ny, nz = grad_ref.shape
    synthesise(x, lines_ref, y_out_ref, z_out_ref, low_ref, b_ref, space_ref)
    for y in range(0, ny, 2 * YB):
        local = channel_mix(kron_ref[...], grad_ref, y)
        for o in range(channels):
            g, c = divmod(o, CB)
            for t in range(2):
                first = y + t * YB
                u = (
                    space_ref[g, first : first + YB, c * nz : (c + 1) * nz]
                    + local[o * YB : (o + 1) * YB, t * nz : (t + 1) * nz]
                )
                out_ref[o, 0, first : first + YB, :] = u.astype(BF16)


def back(lines, pre_grad, kron):
    channels, rows, ny, nz = pre_grad.shape
    _, _, y_out, z_out = plane_tables(ny, nz)
    lanes = KZ * channels
    cells = cells_specs(channels, ny, nz)
    return pl.pallas_call(
        back_kernel,
        grid=(rows,),
        in_specs=[
            pl.BlockSpec((KY, 1, 2 * XB, lanes), lambda x: (0, x // XB, 0, 0)),
            cells,
            whole(kron.shape),
            whole(y_out.shape),
            whole(z_out.shape),
        ],
        out_specs=cells,
        out_shape=jax.ShapeDtypeStruct(pre_grad.shape, BF16),
        scratch_shapes=[
            pltpu.VMEM((2 * KY * 2 * XB, lanes), BF16),
            pltpu.VMEM((2 * ny, lanes), BF16),
            pltpu.VMEM((channels // CB, ny, CB * nz), F32),
        ],
        compiler_params=params(),
        name="back",
    )(lines, pre_grad, kron, jnp.asarray(y_out), jnp.asarray(z_out))


def cell_sums_kernel(grad_ref, f_ref, out_ref, acc_ref, row_ref):
    x = pl.program_id(0)
    channels, _, ny, nz = f_ref.shape

    def tiles(ref):
        return jnp.concatenate([ref[:, 0, y : y + YB, :].reshape(-1, nz) for y in range(0, ny, YB)], axis=1)

    grads = tiles(grad_ref)
    term = lax.dot_general(grads, tiles(f_ref), (((1,), (1,)), ((), ())), preferred_element_type=F32)
    ones = jnp.ones((grads.shape[1], 128), BF16)
    sums = dot(grads, ones)

    @pl.when(x == 0)
    def _():
        acc_ref[...] = term
        row_ref[...] = sums

    @pl.when(x > 0)
    def _():
        acc_ref[...] += term
        row_ref[...] += sums

    @pl.when(x == pl.num_programs(0) - 1)
    def _():
        n = channels * YB
        same = lax.rem(lax.broadcasted_iota(jnp.int32, (n, n), 0), YB) == lax.rem(
            lax.broadcasted_iota(jnp.int32, (n, n), 1), YB
        )
        picked = jnp.where(same, acc_ref[...], 0.0)
        fold = (
            lax.broadcasted_iota(jnp.int32, (channels, n), 1) // YB
            == lax.broadcasted_iota(jnp.int32, (channels, n), 0)
        ).astype(F32)
        half = exact_dot(fold, picked, ((1,), (0,)))
        out_ref[0] = exact_dot(half, fold, ((1,), (1,)))
        out_ref[1] = exact_dot(fold, row_ref[...], ((1,), (0,)))[:, :channels]


def cell_sums(pre_grad, features):
    channels, rows, ny, nz = features.shape
    cells = cells_specs(channels, ny, nz)
    return pl.pallas_call(
        cell_sums_kernel,
        grid=(rows,),
        in_specs=[cells, cells],
        out_specs=whole((2, channels, channels)),
        out_shape=jax.ShapeDtypeStruct((2, channels, channels), F32),
        scratch_shapes=[pltpu.VMEM((channels * YB, channels * YB), F32), pltpu.VMEM((channels * YB, 128), F32)],
        compiler_params=params(),
        name="cell_sums",
    )(pre_grad, features)


def swap(blocks):
    return lax.all_to_all(blocks, "mp", 0, 0, tiled=True)


def shards(features, cotangent, spectral_weight, pointwise_weight, biases):
    channels, rows, ny, nz = features.shape
    devices = lax.axis_size("mp")
    nx = rows * devices
    pairs = spectral_weight.shape[0]
    groups = channels // CB
    blocks = rows // XB
    cut = KZ // pairs
    cells = nx * ny * nz
    x_in, x_out = (jnp.asarray(t) for t in line_tables(nx))
    perm = jnp.asarray(lane_tables(pairs, channels))
    perm_back = jnp.asarray(lane_tables(pairs, channels).T)
    if cut == 1:
        first_k = 0
    else:
        first_k = lax.rem(lax.axis_index("mp"), cut) * pairs
    ks = jnp.broadcast_to(jnp.arange(pairs)[None, :, None] + first_k, (groups, pairs, CB)).reshape(1, -1)
    scale = jnp.where(ks == 0, 1.0, 2.0).astype(F32) / float(cells)

    def to_owner(lines):
        if cut > 1:
            lines = lines.reshape(KY, blocks, 2 * XB, groups, cut, pairs * CB)
            lines = lines.transpose(0, 4, 1, 2, 3, 5)
        return swap(lines.reshape(devices, blocks, 2 * XB, -1)).reshape(nx * 2, -1)

    def to_cells(lines):
        lines = swap(lines.reshape(devices, blocks, 2 * XB, -1))
        if cut > 1:
            lines = lines.reshape(KY, cut, blocks, 2 * XB, groups, pairs * CB)
            lines = lines.transpose(0, 2, 3, 4, 1, 5)
        return lines.reshape(KY, blocks, 2 * XB, -1)

    eye = jnp.eye(YB, dtype=BF16)
    kron = jnp.kron(pointwise_weight, eye)
    kron_back = jnp.kron(pointwise_weight.T, eye)

    lines = to_owner(feature_lines(features))
    mixed, spec = mix_modes(lines, spectral_weight, scale, x_in, x_out, perm)
    pre_grad, dlines = slope(to_cells(mixed), features, cotangent, kron, biases)
    dmixed, dspec = adjoint_modes(to_owner(dlines), spectral_weight, scale, x_in, x_out, perm_back)
    sums = cell_sums(pre_grad, features)
    sums = jnp.concatenate([sums[0].reshape(-1), sums[1, :, 0], jnp.zeros((channels * 3,), F32)])
    sums = swap(jnp.broadcast_to(sums.reshape(1, -1, 128), (devices, sums.size // 128, 128)))
    total = jnp.sum(sums, axis=0).reshape(-1) * float(cells) ** -0.5
    mix_total = total[: channels * channels].reshape(channels, channels)
    bias_total = total[channels * channels : channels * channels + channels]
    features_grad = back(to_cells(dmixed), pre_grad, kron_back)
    spectral_grad = mode_gradient(spec, dspec)
    return (features_grad, spectral_grad, mix_total, bias_total)


def solution(mesh):
    return jax.shard_map(
        shards,
        mesh=mesh,
        in_specs=(
            P(None, ("groups", "mp"), None, None),
            P(None, ("groups", "mp"), None, None),
            P("mp", None, None, None, None),
            P(),
            P(),
        ),
        out_specs=(
            P(None, ("groups", "mp"), None, None),
            P(("groups", "mp"), None, None, None, None),
            P("groups", None),
            P("groups"),
        ),
        check_vma=False,
    )
```

time: 635 us -> 182 us (0.29)
  matrix products: 359 us -> 0 us
  waiting for transfers between devices: 136 us -> 16 us
  Pallas kernels: 0 us -> 107 us
  blocking collectives: 60.2 us -> 0 us
  starting transfers between devices: 0.74 us -> 27.6 us
  local copies, waits for them, and re-layouts: 44.5 us -> 23.6 us
  between operations: 14.8 us -> 0.72 us
    dot_general x51 -> x0, matrix products: 359 us -> none  [the longest x2 76.5 us: space_plane(): jnp.einsum('kcxy,zk->cxyz', b_imag, z_sin, precision=precise)]
    pallas_call x0 -> x7, Pallas kernels: none -> 107 us  [the longest x1 29.9 us: slope(): pl.pallas_call(slope_kernel, grid=(rows,), in_specs=[pl.BlockSpec(memory_...]
    reduce_scatter x2 -> x0, waiting for transfers between devices: 75.4 us -> none  [to_modes(): lax.psum_scatter(spectrum_lines(partial_value, x_cos_mine, x_sin_mine), '...]
    all_gather x2 -> x0, waiting for transfers between devices: 60.8 us -> none  [to_space(): lax.all_gather(spec, 'mp', axis=0, tiled=True)]
    psum x1 -> x0, blocking collectives: 60.2 us -> none  [shards(): mix_total, bias_total = lax.psum((mix_local, bias_local), 'mp')]
    all_to_all x0 -> x5, starting transfers between devices: none -> 27.6 us  [swap(): return lax.all_to_all(blocks, 'mp', 0, 0, tiled=True)]
    mul x0 -> x2, local copies, waits for them, and re-layouts: none -> 16.8 us  [the longest x1 8.42 us: shards(): kron_back = jnp.kron(pointwise_weight.T, eye)]
    all_to_all x0 -> x5, waiting for transfers between devices: none -> 16 us  [swap(): return lax.all_to_all(blocks, 'mp', 0, 0, tiled=True)]
  transfers between devices with their start and end apart: 4 -> 5, of which waited for: 3 -> 2; matrix products, arithmetic and copies ran while one was open for 8% -> 14% of each run, Pallas kernels for 0% -> 21%
where the time goes in v1:
time: 182 us; the launch traced here: 179 us
  Pallas kernels  107 us (59%)
  starting transfers between devices  27.6 us (15%)
  local copies, waits for them, and re-layouts  23.6 us (13%)
  waiting for transfers between devices  16 us (9%)
  other arithmetic  3.74 us (2%)
    pallas_call x1, Pallas kernels, slope(): pl.pallas_call(slope_kernel, grid=(rows,), in_specs=[pl.BlockSpec(memory_...  29.9 us
    all_to_all x5, starting transfers between devices, swap(): return lax.all_to_all(blocks, 'mp', 0, 0, tiled=True)  27.6 us
    all_to_all x5, waiting for transfers between devices, swap(): return lax.all_to_all(blocks, 'mp', 0, 0, tiled=True)  16 us
    pallas_call x1, Pallas kernels, mix_modes(): pl.pallas_call(mix_kernel, grid=(pairs,), in_specs=[whole(scale.shape), w...  14 us
    pallas_call x1, Pallas kernels, back(): pl.pallas_call(back_kernel, grid=(rows,), in_specs=[pl.BlockSpec((KY, 1,...  13.8 us
    pallas_call x1, Pallas kernels, cell_sums(): pl.pallas_call(cell_sums_kernel, grid=(rows,), in_specs=[cells, cells], o...  13.7 us
    pallas_call x1, Pallas kernels, adjoint_modes(): pl.pallas_call(adjoint_kernel, grid=(pairs,), in_specs=[whole(scale.shape...  13.3 us
    pallas_call x1, Pallas kernels, feature_lines(): pl.pallas_call(lines_kernel, grid=(blocks, channels // CB), in_specs=[pl....  11.8 us
  transfers between devices with their start and end apart: 5, of which 2 were waited for; matrix products, arithmetic and copies ran while one was open for 14% of the time, Pallas kernels for 21%

profile of v1, /device:TPU:0, one launch (start us, length us, event | category | flops | bytes accessed | tf_op | source)
XLA Modules:
  0.0 179.0 jit_solution(14220627411081601974)
XLA Ops:
  0.6 11.8 %feature_lines.1 = f32[16,2,8,512]{3,2,1,0:T(8,128)} custom-call(bf16[32,8,128,128]{3,2,1,0:T(8,128)(2,1)} %f_ref.5, bf16[256,512]{1,0:T(8,128)(2,1)} %constant.31.clone.y_in_ref, bf16[8,256,128]{2,1,0:T(8,128)(2,1)} %constant.32.clone.z_in_ref), custom_call_target="tpu_custom_call" | custom-call | tf_op jit(solution)/shard_map/feature_lines/pallas_call | solution.py:117
  12.4 7.4 %all-to-all-start = ((f32[16,2,8,512]{3,2,1,0:T(8,128)}), f32[16,2,8,512]{3,2,1,0:T(8,128)S(1)}, u32[]{:S(2)}, u32[]{:S(2)}) async-start(f32[16,2,8,512]{3,2,1,0:T(8,128)} %feature_lines.1), calls=%async_computation | async-start | bytes 1048576 | tf_op jit(solution)/shard_map/all_to_all | solution.py:485
  20.5 13.8 %all-to-all-done = f32[16,2,8,512]{3,2,1,0:T(8,128)S(1)} async-done(((f32[16,2,8,512]{3,2,1,0:T(8,128)}), f32[16,2,8,512]{3,2,1,0:T(8,128)S(1)}, u32[]{:S(2)}, u32[]{:S(2)}) %all-to-all-start) | async-done | bytes 524320 | tf_op jit(solution)/shard_map/all_to_all | solution.py:485
  34.3 0.8 copy-done.3
  35.0 14.0 %mix_modes.1 = (f32[256,512]{1,0:T(8,128)}, f32[512,32]{1,0:T(8,128)}) custom-call(f32[1,512]{1,0:T(1,128)} %div.14.scale_ref, f32[256,512]{1,0:T(8,128)} %bitcast.13, f32[16,2,16,32,32]{4,3,2,1,0:T(8,128)} %w_ref.3, f32[256,32]{1,0:T(8,128)} %constant.28.clone.x_in_ref.x_out_ref, f32[256,32]{1,0:T(8,128)} %constant.28.clone.x_in_ref.x_out_ref, ...), custom_call_target="tpu_custom_call" | custom-call | tf_op jit(solution)/shard_map/mix_modes/pallas_call | solution.py:171
  49.0 4.1 %all-to-all-start.1 = ((f32[16,2,8,512]{3,2,1,0:T(8,128)}), f32[16,2,8,512]{3,2,1,0:T(8,128)S(1)}, u32[]{:S(2)}, u32[]{:S(2)}) async-start(f32[16,2,8,512]{3,2,1,0:T(8,128)} %bitcast.15), calls=%async_computation.1 | async-start | bytes 1048576 | tf_op jit(solution)/shard_map/all_to_all | solution.py:485
  53.3 3.7 %broadcast_multiply_fusion = (bf16[32,16,32,16]{3,2,1,0:T(8,128)(2,1)}, bf16[32,16,32,16]{3,2,1,0:T(8,128)(2,1)}) fusion(bf16[32,32]{1,0:T(8,128)(2,1)S(1)} %copy.20, bf16[16,16]{1,0:T(8,128)(2,1)S(1)} %fusion, bf16[32,32]{1,0:T(8,128)(2,1)S(1)} %copy-done.4), kind=kLoop, calls=%fused_computation | loop fusion | flops 524288 | bytes 1053184 | tf_op jit(solution)/shard_map/jit(kron)/mul | solution.py:522
  56.9 8.4 %mul.55.kron_ref = bf16[512,512]{1,0:T(8,128)(2,1)} reshape(bf16[32,16,32,16]{3,2,1,0:T(8,128)(2,1)} %get-tuple-element.19) | data formatting | bytes 1048576 | tf_op jit(solution)/shard_map/jit(kron)/mul | solution.py:521
  65.4 2.3 %all-to-all-done.1.lines_ref = f32[16,2,8,512]{3,2,1,0:T(8,128)S(1)} async-done(((f32[16,2,8,512]{3,2,1,0:T(8,128)}), f32[16,2,8,512]{3,2,1,0:T(8,128)S(1)}, u32[]{:S(2)}, u32[]{:S(2)}) %all-to-all-start.1) | async-done | bytes 524320 | tf_op jit(solution)/shard_map/all_to_all | solution.py:485
  67.6 0.8 copy-done.1
  68.4 29.9 %slope.1 = (bf16[32,8,128,128]{3,2,1,0:T(8,128)(2,1)}, f32[16,2,8,512]{3,2,1,0:T(8,128)}) custom-call(f32[32]{0:T(128)} %bias_ref.1, f32[16,2,8,512]{3,2,1,0:T(8,128)} %copy-done.1, bf16[32,8,128,128]{3,2,1,0:T(8,128)(2,1)} %f_ref.5, bf16[32,8,128,128]{3,2,1,0:T(8,128)(2,1)} %cot_ref.1, bf16[512,512]{1,0:T(8,128)(2,1)} %mul.55.kron_ref, ...), custom_call_target="tpu_custom_call" | custom-call | tf_op jit(solution)/shard_map/slope/pallas_call | solution.py:357
  98.3 4.1 %all-to-all-start.2 = ((f32[16,2,8,512]{3,2,1,0:T(8,128)}), f32[16,2,8,512]{3,2,1,0:T(8,128)S(1)}, u32[]{:S(2)}, u32[]{:S(2)}) async-start(f32[16,2,8,512]{3,2,1,0:T(8,128)} %get-tuple-element.11), calls=%async_computation.2 | async-start | bytes 1048576 | tf_op jit(solution)/shard_map/all_to_all | solution.py:485
  102.4 13.7 %cell_sums.1 = f32[2,32,32]{2,1,0:T(8,128)} custom-call(bf16[32,8,128,128]{3,2,1,0:T(8,128)(2,1)} %get-tuple-element.13.grad_ref, bf16[32,8,128,128]{3,2,1,0:T(8,128)(2,1)} %f_ref.5), custom_call_target="tpu_custom_call" | custom-call | tf_op jit(solution)/shard_map/cell_sums/pallas_call | solution.py:472
  116.2 0.7 slice.21
  117.0 0.8 slice_reduce_fusion
  117.9 0.7 broadcast_in_dim.37
  118.6 6.0 %all-to-all-start.4 = ((f32[16,9,128]{2,1,0:T(8,128)}), f32[16,9,128]{2,1,0:T(8,128)S(1)}, u32[]{:S(2)}, u32[]{:S(2)}) async-start(f32[16,9,128]{2,1,0:T(8,128)} %broadcast_in_dim.37), calls=%async_computation.4 | async-start | bytes 262144 | tf_op jit(solution)/shard_map/all_to_all | solution.py:485
  124.6 13.3 %adjoint_modes.1 = (f32[256,512]{1,0:T(8,128)}, f32[16,32,32]{2,1,0:T(8,128)}) custom-call(f32[1,512]{1,0:T(1,128)} %div.14.scale_ref, f32[256,512]{1,0:T(8,128)} %bitcast.12, f32[16,2,16,32,32]{4,3,2,1,0:T(8,128)} %w_ref.3, f32[256,32]{1,0:T(8,128)} %constant.28.clone.x_in_ref.x_out_ref, f32[256,32]{1,0:T(8,128)} %constant.28.clone.x_in_ref.x_out_ref, ...), custom_call_target="tpu_custom_call" | custom-call | tf_op jit(solution)/shard_map/adjoint_modes/pallas_call | solution.py:228
  138.0 6.0 %all-to-all-start.3 = ((f32[16,2,8,512]{3,2,1,0:T(8,128)}), f32[16,2,8,512]{3,2,1,0:T(8,128)S(1)}, u32[]{:S(2)}, u32[]{:S(2)}) async-start(f32[16,2,8,512]{3,2,1,0:T(8,128)} %bitcast.14), calls=%async_computation.3 | async-start | bytes 1048576 | tf_op jit(solution)/shard_map/all_to_all | solution.py:485
  144.0 8.4 %mul.58.kron_ref = bf16[512,512]{1,0:T(8,128)(2,1)} reshape(bf16[32,16,32,16]{3,2,1,0:T(8,128)(2,1)} %get-tuple-element.18) | data formatting | bytes 1048576 | tf_op jit(solution)/shard_map/jit(kron)/mul | solution.py:522
  152.9 0.7 slice.19
  153.6 10.8 %mode_gradient.1 = f32[16,2,16,32,32]{4,3,2,1,0:T(8,128)} custom-call(f32[512,32]{1,0:T(8,128)} %get-tuple-element.14.spec_ref, f32[16,32,32]{2,1,0:T(8,128)} %get-tuple-element.15.dspec_ref), custom_call_target="tpu_custom_call" | custom-call | tf_op jit(solution)/shard_map/mode_gradient/pallas_call | solution.py:266
  164.4 0.8 copy-done
  165.3 13.8 %back.1 = bf16[32,8,128,128]{3,2,1,0:T(8,128)(2,1)} custom-call(f32[16,2,8,512]{3,2,1,0:T(8,128)} %copy-done, bf16[32,8,128,128]{3,2,1,0:T(8,128)(2,1)} %get-tuple-element.13.grad_ref, bf16[512,512]{1,0:T(8,128)(2,1)} %mul.58.kron_ref, bf16[4,256,128]{2,1,0:T(8,128)(2,1)} %constant.33.clone.y_out_ref, bf16[256,1024]{1,0:T(8,128)(2,1)} %constant.34.clone.z_out_ref), custom_call_target="tpu_custom_call" | custom-call | tf_op jit(solution)/shard_map/back/pallas_call | solution.py:409
  (21 shorter events, 1.5 us)
Async XLA Ops:
  12.4 21.9 %all-to-all-start = ((f32[16,2,8,512]{3,2,1,0:T(8,128)}), f32[16,2,8,512]{3,2,1,0:T(8,128)S(1)}, u32[]{:S(2)}, u32[]{:S(2)}) async-start(f32[16,2,8,512]{3,2,1,0:T(8,128)} %feature_lines.1), calls=%async_computation | async-start | bytes 1048576 | tf_op jit(solution)/shard_map/all_to_all | solution.py:485
  34.3 0.8 copy-start.3
  35.0 18.1 %copy-start.4 = (bf16[32,32]{1,0:T(8,128)(2,1)S(1)}, bf16[32,32]{1,0:T(8,128)(2,1)}, u32[]{:S(2)}) copy-start(bf16[32,32]{1,0:T(8,128)(2,1)} %param.16) | copy-start | bytes 6148
  49.0 18.6 %all-to-all-start.1 = ((f32[16,2,8,512]{3,2,1,0:T(8,128)}), f32[16,2,8,512]{3,2,1,0:T(8,128)S(1)}, u32[]{:S(2)}, u32[]{:S(2)}) async-start(f32[16,2,8,512]{3,2,1,0:T(8,128)} %bitcast.15), calls=%async_computation.1 | async-start | bytes 1048576 | tf_op jit(solution)/shard_map/all_to_all | solution.py:485
  67.6 0.8 copy-start.1
  98.3 19.6 %all-to-all-start.2 = ((f32[16,2,8,512]{3,2,1,0:T(8,128)}), f32[16,2,8,512]{3,2,1,0:T(8,128)S(1)}, u32[]{:S(2)}, u32[]{:S(2)}) async-start(f32[16,2,8,512]{3,2,1,0:T(8,128)} %get-tuple-element.11), calls=%async_computation.2 | async-start | bytes 1048576 | tf_op jit(solution)/shard_map/all_to_all | solution.py:485
  117.9 6.7 %copy-start.2 = (f32[16,2,8,512]{3,2,1,0:T(8,128)}, f32[16,2,8,512]{3,2,1,0:T(8,128)S(1)}, u32[]{:S(2)}) copy-start(f32[16,2,8,512]{3,2,1,0:T(8,128)S(1)} %all-to-all-done.2) | copy-start | bytes 1572868
  118.6 19.4 %all-to-all-start.4 = ((f32[16,9,128]{2,1,0:T(8,128)}), f32[16,9,128]{2,1,0:T(8,128)S(1)}, u32[]{:S(2)}, u32[]{:S(2)}) async-start(f32[16,9,128]{2,1,0:T(8,128)} %broadcast_in_dim.37), calls=%async_computation.4 | async-start | bytes 262144 | tf_op jit(solution)/shard_map/all_to_all | solution.py:485
  138.0 26.5 %all-to-all-start.3 = ((f32[16,2,8,512]{3,2,1,0:T(8,128)}), f32[16,2,8,512]{3,2,1,0:T(8,128)S(1)}, u32[]{:S(2)}, u32[]{:S(2)}) async-start(f32[16,2,8,512]{3,2,1,0:T(8,128)} %bitcast.14), calls=%async_computation.3 | async-start | bytes 1048576 | tf_op jit(solution)/shard_map/all_to_all | solution.py:485
  164.4 0.8 copy-start

commit v2 on v1

v2 whole, which is shorter than its diff:
```python
import functools
import math

import jax
import jax.numpy as jnp
import ml_dtypes
import numpy as np
from jax import lax
from jax.experimental import pallas as pl
from jax.experimental.pallas import tpu as pltpu
from jax.sharding import PartitionSpec as P

KX = 16
KY = 16
KZ = 16
XB = 4
CB = 8
YB = 16
MIB = 1 << 20

F32 = jnp.float32
BF16 = jnp.bfloat16


def angles(length, modes, signed):
    freqs = np.arange(modes) - (modes // 2 if signed else 0)
    theta = (np.arange(length)[:, None] * freqs[None, :] % length) * (2.0 * math.pi / length)
    return np.cos(theta), np.sin(theta)


def bf16(table):
    return np.asarray(table, np.float32).astype(ml_dtypes.bfloat16)


@functools.cache
def plane_tables(ny, nz):
    yc, ys = angles(ny, KY, True)
    zc, zs = angles(nz, KZ, False)
    eye_x = np.eye(XB)
    rows = np.stack([np.stack([yc, -ys], 0), np.stack([-ys, -yc], 0)], 0)
    y_in = np.einsum("mryj,xw->mjrxwy", rows, eye_x).reshape(2 * KY * 2 * XB, XB * ny)
    z_in = np.einsum("mzk,cd->cmzkd", np.stack([zc, zs], 0), np.eye(CB)).reshape(CB, 2 * nz, KZ * CB)
    mix = np.stack([np.stack([yc, -ys], 0), np.stack([ys, yc], 0)], 0)
    y_out = np.einsum("qryj,xw->xqyjrw", mix, eye_x).reshape(XB, 2 * ny, KY * 2 * XB)
    z_out = np.einsum("qzk,cd->qkcdz", np.stack([zc, -zs], 0), np.eye(CB)).reshape(2 * KZ * CB, CB * nz)
    return bf16(y_in), bf16(z_in), bf16(y_out), bf16(z_out)


@functools.cache
def line_tables(nx):
    xc, xs = angles(nx, KX, True)
    inward = np.stack([np.stack([xc, -xs], 1), np.stack([xs, xc], 1)], 0)
    outward = np.stack([np.stack([xc, -xs], 1), np.stack([xs, xc], 1)], 0)
    blocks = nx // XB

    def order(table):
        return (
            table.reshape(2, blocks, XB, 2 * KX)
            .transpose(1, 0, 2, 3)
            .reshape(nx * 2, 2 * KX)
            .astype(np.float32)
        )

    return order(inward), order(outward)


@functools.cache
def lane_tables(pairs, channels):
    groups = channels // CB
    perm = np.einsum("kl,gh,cd->kgchld", np.eye(pairs), np.eye(groups), np.eye(CB))
    return bf16(perm.reshape(pairs * channels, pairs * channels))


def params(mib):
    return pltpu.CompilerParams(vmem_limit_bytes=mib * MIB)


def exact_dot(a, b, dims):
    return lax.dot_general(a, b, (dims, ((), ())), precision=lax.Precision.HIGHEST, preferred_element_type=F32)


def dot(a, b):
    return jnp.dot(a, b, preferred_element_type=F32)


def split3(v):
    hi = v.astype(BF16)
    rest = v - hi.astype(F32)
    mid = rest.astype(BF16)
    return hi, mid, (rest - mid.astype(F32)).astype(BF16)


def analyse_y(planes, first, count, y_in, g_ref):
    rows = y_in.shape[0] // 2
    for c in range(first, first + count, 2):
        pair = jnp.concatenate([planes(c), planes(c + 1)], axis=1)
        nz = pair.shape[1] // 2
        g = dot(y_in, pair).astype(BF16)
        for i in range(2):
            group, of_group = divmod(c + i, CB)
            for m in range(2):
                g_ref[group * rows : (group + 1) * rows, (2 * of_group + m) * nz : (2 * of_group + m + 1) * nz] = g[
                    m * rows : (m + 1) * rows, i * nz : (i + 1) * nz
                ]


def analyse_z(z_in_ref, g_ref):
    return dot(g_ref[...], z_in_ref[...].reshape(g_ref.shape[1], -1))


def put_lines(out_ref, h, first_group, total):
    rows, lanes = KY * 2 * XB, total.shape[1]
    for g in range(total.shape[0] // rows):
        first = (first_group + g) * lanes
        out_ref[:, h, :, first : first + lanes] = total[g * rows : (g + 1) * rows].reshape(KY, 2 * XB, lanes)


def in_hbm():
    return pl.BlockSpec(memory_space=pltpu.HBM)


def in_vmem():
    return pl.BlockSpec(memory_space=pltpu.VMEM)


DEPTH = 3
PER_COPY = 4
PER_DOT = 16


def lines_kernel(f_hbm, y_in_hbm, z_in_hbm, out_ref, f_ref, g_ref, y_in_ref, z_in_ref, sem, table_sem):
    channels, rows, ny, nz = f_ref.shape
    copies = [
        pltpu.make_async_copy(f_hbm.at[pl.ds(c, PER_COPY)], f_ref.at[pl.ds(c, PER_COPY)], sem.at[c // PER_COPY])
        for c in range(0, channels, PER_COPY)
    ]
    tables = [
        pltpu.make_async_copy(y_in_hbm, y_in_ref, table_sem.at[0]),
        pltpu.make_async_copy(z_in_hbm, z_in_ref, table_sem.at[1]),
    ]
    tables[0].start()
    for copy in copies[:DEPTH]:
        copy.start()
    tables[1].start()
    tables[0].wait()
    y_in = y_in_ref[...]
    for first in range(0, channels, PER_DOT):
        for c in range(0, PER_DOT, PER_COPY):
            n = (first + c) // PER_COPY
            copies[n].wait()
            if n + DEPTH < len(copies):
                copies[n + DEPTH].start()
            for h in range(rows // XB):
                analyse_y(
                    lambda i: f_ref[first + i, h * XB : (h + 1) * XB].reshape(XB * ny, nz), c, PER_COPY, y_in, g_ref.at[h]
                )
        if first == 0:
            tables[1].wait()
        for h in range(rows // XB):
            put_lines(out_ref, h, first // CB, analyse_z(z_in_ref, g_ref.at[h]))


def feature_lines(features):
    channels, rows, ny, nz = features.shape
    y_in, z_in, _, _ = plane_tables(ny, nz)
    blocks = rows // XB
    return pl.pallas_call(
        lines_kernel,
        in_specs=[in_hbm()] * 3,
        out_specs=in_vmem(),
        out_shape=jax.ShapeDtypeStruct((KY, blocks, 2 * XB, KZ * channels), F32),
        scratch_shapes=[
            pltpu.VMEM(features.shape, BF16),
            pltpu.VMEM((blocks, PER_DOT // CB * KY * 2 * XB, CB * 2 * nz), BF16),
            pltpu.VMEM(y_in.shape, BF16),
            pltpu.VMEM(z_in.shape, BF16),
            pltpu.SemaphoreType.DMA((channels // PER_COPY,)),
            pltpu.SemaphoreType.DMA((2,)),
        ],
        compiler_params=params(60),
        name="feature_lines",
    )(features, jnp.asarray(y_in), jnp.asarray(z_in))


WEIGHT_DEPTH = 16


def columns(spec_ref, k, pairs, channels):
    groups = channels // CB
    per_group = pairs * CB
    return jnp.concatenate(
        [spec_ref[pl.ds(pl.multiple_of(g * per_group + k * CB, CB), CB), :] for g in range(groups)], axis=0
    )


def weight_copies(w_hbm, w_ref, sem):
    pairs = w_ref.shape[0]

    def copy(k):
        return pltpu.make_async_copy(w_hbm.at[k], w_ref.at[k], sem.at[k])

    for k in range(min(WEIGHT_DEPTH, pairs)):
        copy(k).start()

    def arrive(k):
        copy(k).wait()

        @pl.when(k + WEIGHT_DEPTH < pairs)
        def _():
            copy(k + WEIGHT_DEPTH).start()

    return arrive


def mix_kernel(scale_ref, lines_ref, w_hbm, x_in_ref, x_out_ref, perm_ref, out_ref, spec_ref, rows_ref, w_ref, sem):
    pairs, _, _, channels, _ = w_ref.shape
    arrive = weight_copies(w_hbm, w_ref, sem)
    spec_ref[...] = exact_dot(lines_ref[...].reshape(x_in_ref.shape[0], -1).T, x_in_ref[...], ((1,), (0,)))

    def step(k, carry):
        arrive(k)
        v = columns(spec_ref, k, pairs, channels)
        reals, imags = [], []
        for a in range(KX):
            vr, vi = v[:, a : a + 1], v[:, KX + a : KX + a + 1]
            wr, wi = w_ref[k, 0, a], w_ref[k, 1, a]
            reals.append(jnp.sum(vr * wr - vi * wi, axis=0, keepdims=True))
            imags.append(jnp.sum(vr * wi + vi * wr, axis=0, keepdims=True))
        rows_ref[k] = jnp.concatenate(reals + imags, axis=0)
        return carry

    lax.fori_loop(0, pairs, step, 0)
    mixed = jnp.concatenate([rows_ref[i] for i in range(pairs)], axis=1)
    parts = dot(jnp.concatenate(split3(mixed), axis=0), perm_ref[...])
    n = mixed.shape[0]
    placed = (parts[2 * n :] + parts[n : 2 * n]) + parts[:n]
    out_ref[...] = exact_dot(x_out_ref[...], placed * scale_ref[...], ((1,), (0,))).reshape(out_ref.shape)


def whole(shape):
    return pl.BlockSpec(shape, lambda k: (0,) * len(shape))


def mix_modes(lines, weight, scale, x_in, x_out, perm):
    pairs, _, kx, channels, _ = weight.shape
    lanes = pairs * channels
    return pl.pallas_call(
        mix_kernel,
        in_specs=[in_vmem(), in_vmem(), in_hbm(), in_vmem(), in_vmem(), in_vmem()],
        out_specs=[in_vmem(), in_vmem()],
        out_shape=[jax.ShapeDtypeStruct(lines.shape, F32), jax.ShapeDtypeStruct((lanes, 2 * kx), F32)],
        scratch_shapes=[
            pltpu.VMEM((pairs, 2 * kx, channels), F32),
            pltpu.VMEM(weight.shape, F32),
            pltpu.SemaphoreType.DMA((pairs,)),
        ],
        compiler_params=params(53),
        name="mix_modes",
    )(scale, lines, weight, x_in, x_out, perm)


def adjoint_kernel(scale_ref, lines_ref, w_hbm, x_in_ref, x_out_ref, perm_ref, out_ref, dspec_ref, cols_ref, w_ref, sem):
    pairs, _, _, channels, _ = w_ref.shape
    arrive = weight_copies(w_hbm, w_ref, sem)
    placed = exact_dot(x_in_ref[...].T, lines_ref[...].reshape(x_in_ref.shape[0], -1), ((1,), (0,))) * scale_ref[...]
    n = placed.shape[0]
    parts = dot(jnp.concatenate(split3(placed), axis=0), perm_ref[...])
    rows = (parts[2 * n :] + parts[n : 2 * n]) + parts[:n]
    for i in range(pairs):
        dspec_ref[i] = rows[:, i * channels : (i + 1) * channels]
    lane = lax.broadcasted_iota(jnp.int32, (channels, 2 * KX), 1)

    def step(k, carry):
        arrive(k)
        d = dspec_ref[k]
        cols = jnp.zeros((channels, 2 * KX), F32)
        for a in range(KX):
            dr, di = d[a : a + 1], d[KX + a : KX + a + 1]
            wr, wi = w_ref[k, 0, a], w_ref[k, 1, a]
            cols = jnp.where(lane == a, jnp.sum(dr * wr + di * wi, axis=1, keepdims=True), cols)
            cols = jnp.where(lane == KX + a, jnp.sum(di * wr - dr * wi, axis=1, keepdims=True), cols)
        for g in range(channels // CB):
            cols_ref[pl.ds(pl.multiple_of(g * pairs * CB + k * CB, CB), CB), :] = cols[g * CB : (g + 1) * CB]
        return carry

    lax.fori_loop(0, pairs, step, 0)
    out_ref[...] = exact_dot(x_out_ref[...], cols_ref[...], ((1,), (1,))).reshape(out_ref.shape)


def adjoint_modes(lines, weight, scale, x_in, x_out, perm_back):
    pairs, _, kx, channels, _ = weight.shape
    lanes = pairs * channels
    return pl.pallas_call(
        adjoint_kernel,
        in_specs=[in_vmem(), in_vmem(), in_hbm(), in_vmem(), in_vmem(), in_vmem()],
        out_specs=[in_vmem(), in_vmem()],
        out_shape=[jax.ShapeDtypeStruct(lines.shape, F32), jax.ShapeDtypeStruct((pairs, 2 * kx, channels), F32)],
        scratch_shapes=[
            pltpu.VMEM((lanes, 2 * kx), F32),
            pltpu.VMEM(weight.shape, F32),
            pltpu.SemaphoreType.DMA((pairs,)),
        ],
        compiler_params=params(53),
        name="adjoint_modes",
    )(scale, lines, weight, x_in, x_out, perm_back)


PER_STEP = 4


def outer_kernel(spec_ref, dspec_ref, out_ref):
    channels = dspec_ref.shape[-1]
    pairs = spec_ref.shape[0] // channels
    for i in range(PER_STEP):
        v = columns(spec_ref, pl.program_id(0) * PER_STEP + i, pairs, channels)
        d = dspec_ref[i]
        for a in range(KX):
            vr, vi = v[:, a : a + 1], v[:, KX + a : KX + a + 1]
            dr, di = d[a : a + 1], d[KX + a : KX + a + 1]
            out_ref[i, 0, a] = vr * dr + vi * di
            out_ref[i, 1, a] = vr * di - vi * dr


def mode_gradient(spec, dspec):
    pairs, twice_kx, channels = dspec.shape
    shape = (pairs, 2, twice_kx // 2, channels, channels)
    return pl.pallas_call(
        outer_kernel,
        grid=(pairs // PER_STEP,),
        in_specs=[whole(spec.shape), pl.BlockSpec((PER_STEP, twice_kx, channels), lambda k: (k, 0, 0))],
        out_specs=pl.BlockSpec((PER_STEP,) + shape[1:], lambda k: (k, 0, 0, 0, 0)),
        out_shape=jax.ShapeDtypeStruct(shape, F32),
        compiler_params=params(24),
        name="mode_gradient",
    )(spec, dspec)


def spread(w, by_column, out_ref):
    n = out_ref.shape[0]
    fold = (
        lax.broadcasted_iota(jnp.int32, (n, w.shape[0]), 0) // YB
        == lax.broadcasted_iota(jnp.int32, (n, w.shape[0]), 1)
    ).astype(F32).astype(BF16)
    wide = lax.dot_general(fold, w, (((1,), (1 if by_column else 0,)), ((), ())), preferred_element_type=F32)
    full = lax.dot_general(wide.astype(BF16), fold, (((1,), (1,)), ((), ())), preferred_element_type=F32)
    same = lax.rem(lax.broadcasted_iota(jnp.int32, (n, n), 0), YB) == lax.rem(
        lax.broadcasted_iota(jnp.int32, (n, n), 1), YB
    )
    out_ref[...] = jnp.where(same, full, 0.0).astype(BF16)


def synthesise_y(lines_ref, bias, y_out_ref, low_ref, b_ref):
    rows = KY * 2 * XB
    lanes = KZ * CB
    ny = b_ref.shape[2]
    tables = y_out_ref[...].reshape(-1, rows)
    tables = jnp.concatenate([tables, tables], axis=1)
    for h in range(lines_ref.shape[1]):
        block = lines_ref[:, h].reshape(rows, lines_ref.shape[-1])
        if bias is not None:
            row = lax.broadcasted_iota(jnp.int32, (rows, 1), 0) // XB
            block = block + jnp.where(row == KY // 2 * 2, bias, 0.0)
        hi = block.astype(BF16)
        low_ref[:rows] = hi
        low_ref[rows:] = (block - hi.astype(F32)).astype(BF16)
        b = dot(tables, low_ref[...]).astype(BF16)
        for x in range(XB):
            for part in range(2):
                first = (2 * x + part) * ny
                for g in range(b_ref.shape[1]):
                    b_ref[h * XB + x, g, :, part * lanes : (part + 1) * lanes] = b[
                        first : first + ny, g * lanes : (g + 1) * lanes
                    ]


def channel_mix(kron, cells_ref, x, y):
    nz = cells_ref.shape[-1]
    tiles = [cells_ref[:, x, y + t * YB : y + (t + 1) * YB, :].reshape(-1, nz) for t in range(2)]
    return dot(kron, jnp.concatenate(tiles, axis=1))


def store_mix(kron_ref, cells_ref, out_ref):
    channels, rows, ny, nz = cells_ref.shape
    for x in range(rows):
        for y in range(0, ny, 2 * YB):
            local = channel_mix(kron_ref[...], cells_ref, x, y).astype(BF16)
            for t in range(2):
                out_ref[:, x, y + t * YB : y + (t + 1) * YB, :] = local[:, t * nz : (t + 1) * nz].reshape(
                    channels, YB, nz
                )


def local_kernel(by_column, cells_ref, w_ref, out_ref, kron_ref):
    @pl.when(pl.program_id(0) == 0)
    def _():
        spread(w_ref[...], by_column, kron_ref)

    store_mix(kron_ref, cells_ref, out_ref)


def local_branch(features, weight, by_column):
    channels, rows, ny, nz = features.shape
    cells = pl.BlockSpec((channels, 2, ny, nz), lambda x: (0, x, 0, 0))
    return pl.pallas_call(
        functools.partial(local_kernel, by_column),
        grid=(rows // 2,),
        in_specs=[cells, whole(weight.shape)],
        out_specs=cells,
        out_shape=jax.ShapeDtypeStruct(features.shape, BF16),
        scratch_shapes=[pltpu.VMEM((channels * YB, channels * YB), BF16)],
        compiler_params=params(53),
        cost_estimate=pl.CostEstimate(flops=2 * features.size * channels, bytes_accessed=4 * features.size, transcendentals=0),
        name="local_branch",
    )(features, weight)


ROOT = math.sqrt(2.0 / math.pi)
CUBE = 0.044715 * ROOT


def gelu_slope(u):
    square = u * u
    t = jnp.tanh(u * (ROOT + CUBE * square))
    inner = u * (0.5 * ROOT + 1.5 * CUBE * square)
    return (1.0 + t) * (0.5 + (1.0 - t) * inner)


def row_copy(src, dst, sem):
    return lambda x: pltpu.make_async_copy(src.at[:, x], dst.at[:, x], sem.at[x])


def each_row(rows, act):
    def step(x, carry):
        act(x)
        return carry

    lax.fori_loop(0, rows, step, 0)


def rows_in_turn(rows, z_out_ref, b_ref, even_ref, odd_ref, arrive, use, leave):
    groups = b_ref.shape[1]

    def synthesise_z(x, g, space_ref):
        space_ref[g] = dot(b_ref[x, g], z_out_ref[...])

    for g in range(groups):
        synthesise_z(0, g, even_ref)

    def pair(i, carry):
        for n, here, there in ((0, even_ref, odd_ref), (1, odd_ref, even_ref)):
            x = 2 * i + n
            arrive(x)
            for g in range(groups):
                synthesise_z(jnp.minimum(x + 1, rows - 1), g, there)
                use(x, g, here)
            leave(x)
        return carry

    return pair


def slope_kernel(
    bias_ref, lines_ref, local_hbm, cot_hbm, y_in_ref, z_in_ref, y_out_ref, z_out_ref, grad_hbm, out_ref,
    local_ref, cot_ref, grad_ref, low_ref, b_ref, even_ref, odd_ref, g_ref, local_sem, cot_sem, grad_sem,
):
    channels, rows, ny, nz = local_ref.shape
    local_copy = row_copy(local_hbm, local_ref, local_sem)
    cot_copy = row_copy(cot_hbm, cot_ref, cot_sem)
    grad_copy = row_copy(grad_ref, grad_hbm, grad_sem)

    def begin(x):
        local_copy(x).start()
        cot_copy(x).start()

    each_row(2, begin)
    synthesise_y(lines_ref, bias_ref[...], y_out_ref, low_ref, b_ref)

    def arrive(x):
        local_copy(x).wait()
        cot_copy(x).wait()

        @pl.when(x + 2 < rows)
        def _():
            begin(x + 2)

    def use(x, g, space_ref):
        for c in range(CB):
            o = g * CB + c
            for y in range(0, ny, YB):
                at = slice(y, y + YB)
                u = space_ref[g, at, c * nz : (c + 1) * nz] + local_ref[o, x, at, :].astype(F32)
                grad_ref[o, x, at, :] = (gelu_slope(u) * cot_ref[o, x, at, :].astype(F32)).astype(BF16)

    pair = rows_in_turn(rows, z_out_ref, b_ref, even_ref, odd_ref, arrive, use, lambda x: grad_copy(x).start())

    def block(h):
        lax.fori_loop(h * XB // 2, (h + 1) * XB // 2, pair, 0)
        analyse_y(
            lambda c: grad_ref[c, pl.ds(h * XB, XB)].reshape(XB * ny, nz), 0, channels, y_in_ref[...], g_ref
        )
        total = analyse_z(z_in_ref, g_ref)
        put_lines(out_ref, h, 0, total)

    each_row(rows // XB, block)
    each_row(rows, lambda x: grad_copy(x).wait())


def space_scratch(rows, channels, ny, nz):
    groups = channels // CB
    return [
        pltpu.VMEM((2 * KY * 2 * XB, KZ * channels), BF16),
        pltpu.VMEM((rows, groups, ny, 2 * KZ * CB), BF16),
        pltpu.VMEM((groups, ny, CB * nz), F32),
        pltpu.VMEM((groups, ny, CB * nz), F32),
    ]


def slope(lines, local, cotangent, biases):
    channels, rows, ny, nz = local.shape
    y_in, z_in, y_out, z_out = plane_tables(ny, nz)
    lanes = KZ * channels
    bias_lanes = jnp.where(jnp.arange(KZ)[None, :, None] == 0, biases.reshape(-1, 1, CB), 0.0).reshape(1, lanes)
    return pl.pallas_call(
        slope_kernel,
        in_specs=[in_vmem(), in_vmem(), in_hbm(), in_hbm()] + [in_vmem()] * 4,
        out_specs=[in_hbm(), in_vmem()],
        out_shape=[
            jax.ShapeDtypeStruct(local.shape, BF16),
            jax.ShapeDtypeStruct((KY, rows // XB, 2 * XB, lanes), F32),
        ],
        scratch_shapes=[pltpu.VMEM(local.shape, BF16)] * 3
        + space_scratch(rows, channels, ny, nz)
        + [pltpu.VMEM((channels // CB * KY * 2 * XB, CB * 2 * nz), BF16)]
        + [pltpu.SemaphoreType.DMA((rows,))] * 3,
        compiler_params=params(44),
        name="slope",
    )(bias_lanes, lines, local, cotangent, jnp.asarray(y_in), jnp.asarray(z_in), jnp.asarray(y_out), jnp.asarray(z_out))


def back_kernel(
    lines_ref, local_hbm, y_out_ref, z_out_ref, out_hbm,
    local_ref, out_ref, low_ref, b_ref, even_ref, odd_ref, local_sem, out_sem,
):
    channels, rows, ny, nz = local_ref.shape
    local_copy = row_copy(local_hbm, local_ref, local_sem)
    out_copy = row_copy(out_ref, out_hbm, out_sem)
    each_row(3, lambda x: local_copy(x).start())
    synthesise_y(lines_ref, None, y_out_ref, low_ref, b_ref)

    def arrive(x):
        local_copy(x).wait()

        @pl.when(x + 3 < rows)
        def _():
            local_copy(x + 3).start()

    def use(x, g, space_ref):
        for c in range(CB):
            o = g * CB + c
            for y in range(0, ny, YB):
                at = slice(y, y + YB)
                u = space_ref[g, at, c * nz : (c + 1) * nz] + local_ref[o, x, at, :].astype(F32)
                out_ref[o, x, at, :] = u.astype(BF16)

    pair = rows_in_turn(rows, z_out_ref, b_ref, even_ref, odd_ref, arrive, use, lambda x: out_copy(x).start())
    lax.fori_loop(0, rows // 2, pair, 0)
    each_row(rows, lambda x: out_copy(x).wait())


def back(lines, local):
    channels, rows, ny, nz = local.shape
    _, _, y_out, z_out = plane_tables(ny, nz)
    return pl.pallas_call(
        back_kernel,
        in_specs=[in_vmem(), in_hbm(), in_vmem(), in_vmem()],
        out_specs=in_hbm(),
        out_shape=jax.ShapeDtypeStruct(local.shape, BF16),
        scratch_shapes=[pltpu.VMEM(local.shape, BF16)] * 2
        + space_scratch(rows, channels, ny, nz)
        + [pltpu.SemaphoreType.DMA((rows,))] * 2,
        compiler_params=params(53),
        name="back",
    )(lines, local, jnp.asarray(y_out), jnp.asarray(z_out))


def cell_sums_kernel(grad_ref, f_ref, dlines_ref, sums_ref, acc_ref):
    step = pl.program_id(0)
    channels, rows, ny, nz = f_ref.shape
    lanes = KZ * CB

    @pl.when(step == 0)
    def _():
        acc_ref[...] = jnp.zeros_like(acc_ref)

    def tiles(ref):
        return jnp.concatenate(
            [ref[:, x, y : y + YB, :].reshape(-1, nz) for x in range(rows) for y in range(0, ny, YB)], axis=1
        )

    acc_ref[...] += lax.dot_general(tiles(grad_ref), tiles(f_ref), (((1,), (1,)), ((), ())), preferred_element_type=F32)

    @pl.when(step == pl.num_programs(0) - 1)
    def _():
        n = channels * YB
        same = lax.rem(lax.broadcasted_iota(jnp.int32, (n, n), 0), YB) == lax.rem(
            lax.broadcasted_iota(jnp.int32, (n, n), 1), YB
        )
        picked = jnp.where(same, acc_ref[...], 0.0)
        fold = (
            lax.broadcasted_iota(jnp.int32, (channels, n), 1) // YB
            == lax.broadcasted_iota(jnp.int32, (channels, n), 0)
        ).astype(F32)
        half = exact_dot(fold, picked, ((1,), (0,)))
        mixing = exact_dot(half, fold, ((1,), (1,)))
        zero = dlines_ref[KY // 2].reshape(-1, KZ * channels)
        real = lax.rem(lax.broadcasted_iota(jnp.int32, (zero.shape[0], 1), 0), 2 * XB) < XB
        line = jnp.sum(jnp.where(real, zero, 0.0), axis=0, keepdims=True)
        lane = lax.broadcasted_iota(jnp.int32, (channels, KZ * channels), 1)
        channel = lax.broadcasted_iota(jnp.int32, (channels, KZ * channels), 0)
        pick = (lane == channel // CB * lanes + lax.rem(channel, CB)).astype(F32)
        biases = exact_dot(jnp.broadcast_to(line, (8, line.shape[1])), pick, ((1,), (1,)))
        packed = jnp.concatenate(
            [
                jnp.concatenate([mixing[r : r + 8] for r in range(0, channels, 8)], axis=1),
                jnp.concatenate([biases] * (channels // 8), axis=1),
            ],
            axis=0,
        )
        sums_ref[...] = jnp.broadcast_to(packed[None], sums_ref.shape)


def cell_sums(pre_grad, features, dlines, devices):
    channels, rows, ny, nz = features.shape
    cells = pl.BlockSpec((channels, 2, ny, nz), lambda x: (0, x, 0, 0))
    tile = channels * YB
    return pl.pallas_call(
        cell_sums_kernel,
        grid=(rows // 2,),
        in_specs=[cells, cells, whole(dlines.shape)],
        out_specs=whole((devices, 16, channels * channels // 8)),
        out_shape=jax.ShapeDtypeStruct((devices, 16, channels * channels // 8), F32),
        scratch_shapes=[pltpu.VMEM((tile, tile), F32)],
        compiler_params=params(53),
        name="cell_sums",
    )(pre_grad, features, dlines)


def swap(blocks):
    return lax.all_to_all(blocks, "mp", 0, 0, tiled=True)


def shards(features, cotangent, spectral_weight, pointwise_weight, biases):
    channels, rows, ny, nz = features.shape
    devices = lax.axis_size("mp")
    nx = rows * devices
    pairs = spectral_weight.shape[0]
    groups = channels // CB
    blocks = rows // XB
    cut = KZ // pairs
    cells = nx * ny * nz
    x_in, x_out = (jnp.asarray(t) for t in line_tables(nx))
    perm = jnp.asarray(lane_tables(pairs, channels))
    perm_back = jnp.asarray(lane_tables(pairs, channels).T)
    if cut == 1:
        first_k = 0
    else:
        first_k = lax.rem(lax.axis_index("mp"), cut) * pairs
    ks = jnp.broadcast_to(jnp.arange(pairs)[None, :, None] + first_k, (groups, pairs, CB)).reshape(1, -1)
    scale = jnp.where(ks == 0, 1.0, 2.0).astype(F32) / float(cells)

    def to_owner(lines):
        if cut > 1:
            lines = lines.reshape(KY, blocks, 2 * XB, groups, cut, pairs * CB)
            lines = lines.transpose(0, 4, 1, 2, 3, 5)
        return swap(lines.reshape(devices, blocks, 2 * XB, -1))

    def to_cells(lines):
        lines = swap(lines.reshape(devices, blocks, 2 * XB, -1))
        if cut > 1:
            lines = lines.reshape(KY, cut, blocks, 2 * XB, groups, pairs * CB)
            lines = lines.transpose(0, 2, 3, 4, 1, 5)
        return lines.reshape(KY, blocks, 2 * XB, -1)

    lines = to_owner(feature_lines(features))
    mixed, spec = mix_modes(lines, spectral_weight, scale, x_in, x_out, perm)
    pre_grad, dlines = slope(to_cells(mixed), local_branch(features, pointwise_weight, False), cotangent, biases)
    sums = cell_sums(pre_grad, features, dlines, devices)
    dlines, _ = lax.optimization_barrier((to_owner(dlines), sums))
    dmixed, dspec = adjoint_modes(dlines, spectral_weight, scale, x_in, x_out, perm_back)
    back_lines = to_cells(dmixed)
    spectral_grad = mode_gradient(spec, dspec)
    late_grad, _ = lax.optimization_barrier((pre_grad, dspec))
    local_back = local_branch(late_grad, pointwise_weight, True)
    total = jnp.sum(swap(sums), axis=0) * float(cells) ** -0.5
    mix_total = total[:8].reshape(8, channels // 8, channels).transpose(1, 0, 2).reshape(channels, channels)
    bias_total = total[8, :channels]
    features_grad = back(back_lines, local_back)
    return (features_grad, spectral_grad, mix_total, bias_total)


def solution(mesh):
    return jax.shard_map(
        shards,
        mesh=mesh,
        in_specs=(
            P(None, ("groups", "mp"), None, None),
            P(None, ("groups", "mp"), None, None),
            P("mp", None, None, None, None),
            P(),
            P(),
        ),
        out_specs=(
            P(None, ("groups", "mp"), None, None),
            P(("groups", "mp"), None, None, None, None),
            P("groups", None),
            P("groups"),
        ),
        check_vma=False,
    )
```

time: 182 us -> 138 us (0.76); the launches traced: 179 us -> 137 us
  Pallas kernels: 107 us -> 85.5 us
  local copies, waits for them, and re-layouts: 23.6 us -> 2.31 us
  waiting for transfers between devices: 16 us -> 23.3 us
  other arithmetic: 3.74 us -> 0.11 us
  starting transfers between devices: 27.6 us -> 25.1 us
    pallas_call x7 -> x9, Pallas kernels: 107 us -> 85.5 us  [the longest x2 19.6 us: local_branch(): pl.pallas_call(functools.partial(local_kernel, by_column), grid=(rows //...]
    mul x2 -> x0, local copies, waits for them, and re-layouts: 16.8 us -> none  [the longest x1 8.42 us: shards(): kron_back = jnp.kron(pointwise_weight.T, eye)]
    all_to_all x5, waiting for transfers between devices: 16 us -> 23.3 us  [swap(): return lax.all_to_all(blocks, 'mp', 0, 0, tiled=True)]
    mul x2 -> x1, other arithmetic: 3.7 us -> 0.01 us  [shards(): total = jnp.sum(swap(sums), axis=0) * float(cells) ** (-0.5)]
    slice x5 -> x1, local copies, waits for them, and re-layouts: 2.74 us -> 0.01 us  [shards(): total[:8].reshape(8, channels // 8, channels).transpose(1, 0, 2)]
    all_to_all x5, starting transfers between devices: 27.6 us -> 25.1 us  [swap(): return lax.all_to_all(blocks, 'mp', 0, 0, tiled=True)]
  transfers between devices with their start and end apart: 5 -> 5, of which waited for: 2 -> 4; matrix products, arithmetic and copies ran while one was open for 14% -> 1% of each run, Pallas kernels for 21% -> 31%
where the time goes in v2:
time: 138 us; the launch traced here: 137 us
  Pallas kernels  85.5 us (62%)
  starting transfers between devices  25.1 us (18%)
  waiting for transfers between devices  23.3 us (17%)
  local copies, waits for them, and re-layouts  2.31 us (2%)
    all_to_all x5, starting transfers between devices, swap(): return lax.all_to_all(blocks, 'mp', 0, 0, tiled=True)  25.1 us
    all_to_all x5, waiting for transfers between devices, swap(): return lax.all_to_all(blocks, 'mp', 0, 0, tiled=True)  23.3 us
    pallas_call x2, Pallas kernels, local_branch(): pl.pallas_call(functools.partial(local_kernel, by_column), grid=(rows //...  19.6 us
    pallas_call x1, Pallas kernels, slope(): pl.pallas_call(slope_kernel, in_specs=[in_vmem(), in_vmem(), in_hbm(), in...  18.8 us
    pallas_call x1, Pallas kernels, cell_sums(): pl.pallas_call(cell_sums_kernel, grid=(rows // 2,), in_specs=[cells, cell...  10.4 us
    pallas_call x1, Pallas kernels, back(): pl.pallas_call(back_kernel, in_specs=[in_vmem(), in_hbm(), in_vmem(), in_...  8.71 us
    pallas_call x1, Pallas kernels, mix_modes(): pl.pallas_call(mix_kernel, in_specs=[in_vmem(), in_vmem(), in_hbm(), in_v...  8.62 us
    pallas_call x1, Pallas kernels, adjoint_modes(): pl.pallas_call(adjoint_kernel, in_specs=[in_vmem(), in_vmem(), in_hbm(),...  7.31 us
  transfers between devices with their start and end apart: 5, of which 4 were waited for; matrix products, arithmetic and copies ran while one was open for 1% of the time, Pallas kernels for 31%

profile of v2, /device:TPU:0, one launch (start us, length us, event | category | flops | bytes accessed | tf_op | source)
XLA Modules:
  0.0 137.4 jit_solution(5168923750274213734)
XLA Ops:
  0.7 7.1 %feature_lines.1 = f32[16,2,8,512]{3,2,1,0:T(8,128)} custom-call(bf16[32,8,128,128]{3,2,1,0:T(8,128)(2,1)} %f_ref.1, bf16[256,512]{1,0:T(8,128)(2,1)} %constant.31.clone.y_in_hbm.y_in_ref, bf16[8,256,128]{2,1,0:T(8,128)(2,1)} %constant.32.clone.z_in_hbm.z_in_ref), custom_call_target="tpu_custom_call" | custom-call | tf_op jit(solution)/shard_map/feature_lines/pallas_call | solution.py:167
  7.7 7.4 %all-to-all-start = ((f32[16,2,8,512]{3,2,1,0:T(8,128)}), f32[16,2,8,512]{3,2,1,0:T(8,128)S(1)}, u32[]{:S(2)}, u32[]{:S(2)}) async-start(f32[16,2,8,512]{3,2,1,0:T(8,128)} %feature_lines.1), calls=%async_computation | async-start | bytes 1048576 | tf_op jit(solution)/shard_map/all_to_all | solution.py:649
  15.2 0.1 div.14.scale_ref
  15.3 14.4 %all-to-all-done.lines_ref = f32[16,2,8,512]{3,2,1,0:T(8,128)S(1)} async-done(((f32[16,2,8,512]{3,2,1,0:T(8,128)}), f32[16,2,8,512]{3,2,1,0:T(8,128)S(1)}, u32[]{:S(2)}, u32[]{:S(2)}) %all-to-all-start) | async-done | bytes 524320 | tf_op jit(solution)/shard_map/all_to_all | solution.py:649
  29.6 0.8 copy-done.7
  30.4 8.6 %mix_modes.1 = (f32[16,2,8,512]{3,2,1,0:T(8,128)}, f32[512,32]{1,0:T(8,128)S(1)}) custom-call(f32[1,512]{1,0:T(1,128)S(1)} %div.14.scale_ref, f32[16,2,8,512]{3,2,1,0:T(8,128)} %copy-done.7, f32[16,2,16,32,32]{4,3,2,1,0:T(8,128)} %w_hbm.3, f32[256,32]{1,0:T(8,128)S(1)} %copy-done, f32[256,32]{1,0:T(8,128)S(1)} %copy-done, ...), custom_call_target="tpu_custom_call" | custom-call | tf_op jit(solution)/shard_map/mix_modes/pallas_call | solution.py:247
  39.0 4.1 %all-to-all-start.1 = ((f32[16,2,8,512]{3,2,1,0:T(8,128)}), f32[16,2,8,512]{3,2,1,0:T(8,128)S(1)}, u32[]{:S(2)}, u32[]{:S(2)}) async-start(f32[16,2,8,512]{3,2,1,0:T(8,128)} %get-tuple-element.12), calls=%async_computation.1 | async-start | bytes 1048576 | tf_op jit(solution)/shard_map/all_to_all | solution.py:649
  43.2 0.1 broadcast_in_dim.43
  43.3 0.1 select_n.31.bias_ref
  43.5 9.9 %local_branch.2.local_hbm = bf16[32,8,128,128]{3,2,1,0:T(8,128)(2,1)} custom-call(bf16[32,8,128,128]{3,2,1,0:T(8,128)(2,1)} %f_ref.1, bf16[32,32]{1,0:T(8,128)(2,1)S(1)} %copy-done.5), custom_call_target="tpu_custom_call" | custom-call | flops 268435456 | bytes 16777216 | tf_op jit(solution)/shard_map/local_branch/pallas_call | solution.py:404
  53.4 4.3 %all-to-all-done.1.lines_ref = f32[16,2,8,512]{3,2,1,0:T(8,128)S(1)} async-done(((f32[16,2,8,512]{3,2,1,0:T(8,128)}), f32[16,2,8,512]{3,2,1,0:T(8,128)S(1)}, u32[]{:S(2)}, u32[]{:S(2)}) %all-to-all-start.1) | async-done | bytes 524320 | tf_op jit(solution)/shard_map/all_to_all | solution.py:649
  57.6 18.8 %slope.1 = (bf16[32,8,128,128]{3,2,1,0:T(8,128)(2,1)}, f32[16,2,8,512]{3,2,1,0:T(8,128)}) custom-call(f32[1,512]{1,0:T(1,128)S(1)} %select_n.31.bias_ref, f32[16,2,8,512]{3,2,1,0:T(8,128)S(1)} %all-to-all-done.1.lines_ref, bf16[32,8,128,128]{3,2,1,0:T(8,128)(2,1)} %local_branch.2.local_hbm, bf16[32,8,128,128]{3,2,1,0:T(8,128)(2,1)} %cot_hbm.1, ...), custom_call_target="tpu_custom_call" | custom-call | tf_op jit(solution)/shard_map/slope/pallas_call | solution.py:523
  76.4 4.1 %all-to-all-start.2 = ((f32[16,2,8,512]{3,2,1,0:T(8,128)}), f32[16,2,8,512]{3,2,1,0:T(8,128)S(1)}, u32[]{:S(2)}, u32[]{:S(2)}) async-start(f32[16,2,8,512]{3,2,1,0:T(8,128)} %get-tuple-element.13.dlines_ref), calls=%async_computation.2 | async-start | bytes 1048576 | tf_op jit(solution)/shard_map/all_to_all | solution.py:649
  80.6 10.4 %cell_sums.1 = f32[16,16,128]{2,1,0:T(8,128)} custom-call(bf16[32,8,128,128]{3,2,1,0:T(8,128)(2,1)} %get-tuple-element.18.grad_ref.cells_ref, bf16[32,8,128,128]{3,2,1,0:T(8,128)(2,1)} %f_ref.1, f32[16,2,8,512]{3,2,1,0:T(8,128)} %get-tuple-element.13.dlines_ref), custom_call_target="tpu_custom_call" | custom-call | tf_op jit(solution)/shard_map/cell_sums/pallas_call | solution.py:636
  90.9 4.1 %all-to-all-done.2.lines_ref = f32[16,2,8,512]{3,2,1,0:T(8,128)S(1)} async-done(((f32[16,2,8,512]{3,2,1,0:T(8,128)}), f32[16,2,8,512]{3,2,1,0:T(8,128)S(1)}, u32[]{:S(2)}, u32[]{:S(2)}) %all-to-all-start.2) | async-done | bytes 524320 | tf_op jit(solution)/shard_map/all_to_all | solution.py:649
  95.0 4.1 %all-to-all-start.4 = ((f32[16,16,128]{2,1,0:T(8,128)}), f32[16,16,128]{2,1,0:T(8,128)S(1)}, u32[]{:S(2)}, u32[]{:S(2)}) async-start(f32[16,16,128]{2,1,0:T(8,128)} %cell_sums.1), calls=%async_computation.4 | async-start | bytes 262144 | tf_op jit(solution)/shard_map/all_to_all | solution.py:649
  99.1 7.3 %adjoint_modes.1 = (f32[16,2,8,512]{3,2,1,0:T(8,128)}, f32[16,32,32]{2,1,0:T(8,128)S(1)}) custom-call(f32[1,512]{1,0:T(1,128)S(1)} %div.14.scale_ref, f32[16,2,8,512]{3,2,1,0:T(8,128)} %copy-done.6, f32[16,2,16,32,32]{4,3,2,1,0:T(8,128)} %w_hbm.3, f32[256,32]{1,0:T(8,128)S(1)} %copy-done, f32[256,32]{1,0:T(8,128)S(1)} %copy-done, ...), custom_call_target="tpu_custom_call" | custom-call | tf_op jit(solution)/shard_map/adjoint_modes/pallas_call | solution.py:293
  106.5 0.6 all-to-all-done.4
  107.1 5.4 %all-to-all-start.3 = ((f32[16,2,8,512]{3,2,1,0:T(8,128)}), f32[16,2,8,512]{3,2,1,0:T(8,128)S(1)}, u32[]{:S(2)}, u32[]{:S(2)}) async-start(f32[16,2,8,512]{3,2,1,0:T(8,128)} %get-tuple-element.16), calls=%async_computation.3 | async-start | bytes 1048576 | tf_op jit(solution)/shard_map/all_to_all | solution.py:649
  112.6 0.6 copy.20
  113.2 0.5 slice_bitcast_fusion
  113.8 5.1 %mode_gradient.1 = f32[16,2,16,32,32]{4,3,2,1,0:T(8,128)} custom-call(f32[512,32]{1,0:T(8,128)S(1)} %get-tuple-element.19.spec_ref, f32[16,32,32]{2,1,0:T(8,128)S(1)} %get-tuple-element.17.dspec_ref), custom_call_target="tpu_custom_call" | custom-call | tf_op jit(solution)/shard_map/mode_gradient/pallas_call | solution.py:327
  118.8 9.7 %local_branch.3.local_hbm = bf16[32,8,128,128]{3,2,1,0:T(8,128)(2,1)} custom-call(bf16[32,8,128,128]{3,2,1,0:T(8,128)(2,1)} %get-tuple-element.18.grad_ref.cells_ref, bf16[32,32]{1,0:T(8,128)(2,1)S(1)} %copy-done.5), custom_call_target="tpu_custom_call" | custom-call | flops 268435456 | bytes 16777216 | tf_op jit(solution)/shard_map/local_branch/pallas_call | solution.py:404
  128.6 8.7 %back.1 = bf16[32,8,128,128]{3,2,1,0:T(8,128)(2,1)} custom-call(f32[16,2,8,512]{3,2,1,0:T(8,128)S(1)} %all-to-all-done.3.lines_ref, bf16[32,8,128,128]{3,2,1,0:T(8,128)(2,1)} %local_branch.3.local_hbm, bf16[4,256,128]{2,1,0:T(8,128)(2,1)S(1)} %copy-done.3, bf16[256,1024]{1,0:T(8,128)(2,1)} %constant.34.clone.z_out_ref), custom_call_target="tpu_custom_call" | custom-call | tf_op jit(solution)/shard_map/back/pallas_call | solution.py:573
  (25 shorter events, 0.2 us)
Async XLA Ops:
  0.6 29.8 %copy-start = (f32[256,32]{1,0:T(8,128)S(1)}, f32[256,32]{1,0:T(8,128)}, u32[]{:S(2)}) copy-start(f32[256,32]{1,0:T(8,128)} %constant.28.clone.x_in_ref.x_out_ref) | copy-start | bytes 98308
  0.6 42.5 %copy-start.8 = (f32[32]{0:T(128)S(1)}, f32[32]{0:T(128)}, u32[]{:S(2)}) copy-start(f32[32]{0:T(128)} %param.17) | copy-start | bytes 388
  7.7 35.7 %copy-start.5 = (bf16[32,32]{1,0:T(8,128)(2,1)S(1)}, bf16[32,32]{1,0:T(8,128)(2,1)}, u32[]{:S(2)}) copy-start(bf16[32,32]{1,0:T(8,128)(2,1)} %w_ref.3) | copy-start | bytes 6148
  7.7 21.9 %all-to-all-start = ((f32[16,2,8,512]{3,2,1,0:T(8,128)}), f32[16,2,8,512]{3,2,1,0:T(8,128)S(1)}, u32[]{:S(2)}, u32[]{:S(2)}) async-start(f32[16,2,8,512]{3,2,1,0:T(8,128)} %feature_lines.1), calls=%async_computation | async-start | bytes 1048576 | tf_op jit(solution)/shard_map/all_to_all | solution.py:649
  29.6 0.8 copy-start.7
  39.0 18.6 %all-to-all-start.1 = ((f32[16,2,8,512]{3,2,1,0:T(8,128)}), f32[16,2,8,512]{3,2,1,0:T(8,128)S(1)}, u32[]{:S(2)}, u32[]{:S(2)}) async-start(f32[16,2,8,512]{3,2,1,0:T(8,128)} %get-tuple-element.12), calls=%async_computation.1 | async-start | bytes 1048576 | tf_op jit(solution)/shard_map/all_to_all | solution.py:649
  43.4 14.2 %copy-start.1 = (bf16[256,1024]{1,0:T(8,128)(2,1)S(1)}, bf16[256,1024]{1,0:T(8,128)(2,1)}, u32[]{:S(2)}) copy-start(bf16[256,1024]{1,0:T(8,128)(2,1)} %constant.34.clone.z_out_ref) | copy-start | bytes 1572868
  43.5 14.2 %copy-start.2 = (bf16[8,256,128]{2,1,0:T(8,128)(2,1)S(1)}, bf16[8,256,128]{2,1,0:T(8,128)(2,1)}, u32[]{:S(2)}) copy-start(bf16[8,256,128]{2,1,0:T(8,128)(2,1)} %constant.32.clone.z_in_hbm.z_in_ref) | copy-start | bytes 1572868
  43.5 14.2 %copy-start.3 = (bf16[4,256,128]{2,1,0:T(8,128)(2,1)S(1)}, bf16[4,256,128]{2,1,0:T(8,128)(2,1)}, u32[]{:S(2)}) copy-start(bf16[4,256,128]{2,1,0:T(8,128)(2,1)} %constant.33.clone.y_out_ref) | copy-start | bytes 786436
  43.5 14.2 %copy-start.4 = (bf16[256,512]{1,0:T(8,128)(2,1)S(1)}, bf16[256,512]{1,0:T(8,128)(2,1)}, u32[]{:S(2)}) copy-start(bf16[256,512]{1,0:T(8,128)(2,1)} %constant.31.clone.y_in_hbm.y_in_ref) | copy-start | bytes 786436
  76.4 18.6 %all-to-all-start.2 = ((f32[16,2,8,512]{3,2,1,0:T(8,128)}), f32[16,2,8,512]{3,2,1,0:T(8,128)S(1)}, u32[]{:S(2)}, u32[]{:S(2)}) async-start(f32[16,2,8,512]{3,2,1,0:T(8,128)} %get-tuple-element.13.dlines_ref), calls=%async_computation.2 | async-start | bytes 1048576 | tf_op jit(solution)/shard_map/all_to_all | solution.py:649
  95.0 4.1 %copy-start.6 = (f32[16,2,8,512]{3,2,1,0:T(8,128)}, f32[16,2,8,512]{3,2,1,0:T(8,128)S(1)}, u32[]{:S(2)}) copy-start(f32[16,2,8,512]{3,2,1,0:T(8,128)S(1)} %all-to-all-done.2.lines_ref) | copy-start | bytes 1572868
  95.0 12.0 %all-to-all-start.4 = ((f32[16,16,128]{2,1,0:T(8,128)}), f32[16,16,128]{2,1,0:T(8,128)S(1)}, u32[]{:S(2)}, u32[]{:S(2)}) async-start(f32[16,16,128]{2,1,0:T(8,128)} %cell_sums.1), calls=%async_computation.4 | async-start | bytes 262144 | tf_op jit(solution)/shard_map/all_to_all | solution.py:649
  107.1 21.5 %all-to-all-start.3 = ((f32[16,2,8,512]{3,2,1,0:T(8,128)}), f32[16,2,8,512]{3,2,1,0:T(8,128)S(1)}, u32[]{:S(2)}, u32[]{:S(2)}) async-start(f32[16,2,8,512]{3,2,1,0:T(8,128)} %get-tuple-element.16), calls=%async_computation.3 | async-start | bytes 1048576 | tf_op jit(solution)/shard_map/all_to_all | solution.py:649

commit v3 on v2

--- a/solution.py
+++ b/solution.py
@@ -62,13 +62,6 @@
         )
 
     return order(inward), order(outward)
-
-
-@functools.cache
-def lane_tables(pairs, channels):
-    groups = channels // CB
-    perm = np.einsum("kl,gh,cd->kgchld", np.eye(pairs), np.eye(groups), np.eye(CB))
-    return bf16(perm.reshape(pairs * channels, pairs * channels))
 
 
 def params(mib):
@@ -182,7 +175,49 @@
     )(features, jnp.asarray(y_in), jnp.asarray(z_in))
 
 
-WEIGHT_DEPTH = 16
+def quad_of(channels):
+    return 128 // channels
+
+
+def chosen(shape, rule):
+    row = lax.broadcasted_iota(jnp.int32, (shape[0], 1), 0)
+    column = lax.broadcasted_iota(jnp.int32, (1, shape[1]), 1)
+    return jnp.where(rule(row, column), 1.0, 0.0).astype(BF16)
+
+
+def lane_order(lane, pairs, channels):
+    per_group = pairs * CB
+    return lax.rem(lane, per_group) // CB * channels + lane // per_group * CB + lax.rem(lane, CB)
+
+
+def quad_columns(table, channels):
+    quad = quad_of(channels)
+    return table.reshape(-1, 2, KX // quad, quad).transpose(0, 3, 1, 2).reshape(table.shape)
+
+
+def pack_kernel(w_ref, out_ref):
+    pairs, _, kx, channels, _ = w_ref.shape
+    quad = quad_of(channels)
+    for k in range(pairs):
+        for part in range(2):
+            for t in range(kx // quad):
+                out_ref[k, part, t] = jnp.concatenate([w_ref[k, part, t * quad + q] for q in range(quad)], axis=1)
+
+
+def pack_weights(weight):
+    pairs, _, kx, channels, _ = weight.shape
+    quad = quad_of(channels)
+    shape = (pairs, 2, kx // quad, channels, quad * channels)
+    return pl.pallas_call(
+        pack_kernel,
+        grid=(pairs // PER_STEP,),
+        in_specs=[pl.BlockSpec((PER_STEP,) + weight.shape[1:], lambda k: (k, 0, 0, 0, 0))],
+        out_specs=pl.BlockSpec((PER_STEP,) + shape[1:], lambda k: (k, 0, 0, 0, 0)),
+        out_shape=jax.ShapeDtypeStruct(shape, F32),
+        compiler_params=params(53),
+        cost_estimate=pl.CostEstimate(flops=0, bytes_accessed=8 * weight.size * quad, transcendentals=0),
+        name="pack_weights",
+    )(weight)
 
 
 def columns(spec_ref, k, pairs, channels):
@@ -193,45 +228,39 @@
     )
 
 
-def weight_copies(w_hbm, w_ref, sem):
-    pairs = w_ref.shape[0]
-
-    def copy(k):
-        return pltpu.make_async_copy(w_hbm.at[k], w_ref.at[k], sem.at[k])
-
-    for k in range(min(WEIGHT_DEPTH, pairs)):
-        copy(k).start()
-
-    def arrive(k):
-        copy(k).wait()
-
-        @pl.when(k + WEIGHT_DEPTH < pairs)
-        def _():
-            copy(k + WEIGHT_DEPTH).start()
-
-    return arrive
-
-
-def mix_kernel(scale_ref, lines_ref, w_hbm, x_in_ref, x_out_ref, perm_ref, out_ref, spec_ref, rows_ref, w_ref, sem):
-    pairs, _, _, channels, _ = w_ref.shape
-    arrive = weight_copies(w_hbm, w_ref, sem)
-    spec_ref[...] = exact_dot(lines_ref[...].reshape(x_in_ref.shape[0], -1).T, x_in_ref[...], ((1,), (0,)))
+def mix_kernel(
+    scale_ref, lines_ref, w_hbm, x_in_ref, x_out_ref, out_ref, spec_ref, w_ref, wide_ref, rows_ref, sem
+):
+    pairs, _, turns, channels, lanes = w_ref.shape
+    copy = pltpu.make_async_copy(w_hbm, w_ref, sem)
+    copy.start()
+    spec = exact_dot(lines_ref[...].reshape(x_in_ref.shape[0], -1).T, x_in_ref[...], ((1,), (0,)))
+    spec_ref[...] = spec
+    over = chosen((6 * KX, 2 * KX * channels), lambda row, lane: lax.rem(row, 2 * KX) == lane // channels)
+    wide_ref[...] = dot(jnp.concatenate(split3(spec), axis=1), over)
+    copy.wait()
 
     def step(k, carry):
-        arrive(k)
-        v = columns(spec_ref, k, pairs, channels)
+        v = columns(wide_ref, k, pairs, channels)
         reals, imags = [], []
-        for a in range(KX):
-            vr, vi = v[:, a : a + 1], v[:, KX + a : KX + a + 1]
-            wr, wi = w_ref[k, 0, a], w_ref[k, 1, a]
+        for t in range(turns):
+            vr, vi = v[:, t * lanes : (t + 1) * lanes], v[:, (turns + t) * lanes : (turns + t + 1) * lanes]
+            wr, wi = w_ref[k, 0, t], w_ref[k, 1, t]
             reals.append(jnp.sum(vr * wr - vi * wi, axis=0, keepdims=True))
             imags.append(jnp.sum(vr * wi + vi * wr, axis=0, keepdims=True))
         rows_ref[k] = jnp.concatenate(reals + imags, axis=0)
         return carry
 
-    lax.fori_loop(0, pairs, step, 0)
-    mixed = jnp.concatenate([rows_ref[i] for i in range(pairs)], axis=1)
-    parts = dot(jnp.concatenate(split3(mixed), axis=0), perm_ref[...])
+    lax.fori_loop(0, pairs, step, 0, unroll=2)
+    mixed = jnp.concatenate(
+        [
+            jnp.concatenate([rows_ref[k, :, q * channels : (q + 1) * channels] for k in range(pairs)], axis=1)
+            for q in range(lanes // channels)
+        ],
+        axis=0,
+    )
+    order = chosen((mixed.shape[1],) * 2, lambda row, lane: row == lane_order(lane, pairs, channels))
+    parts = dot(jnp.concatenate(split3(mixed), axis=0), order)
     n = mixed.shape[0]
     placed = (parts[2 * n :] + parts[n : 2 * n]) + parts[:n]
     out_ref[...] = exact_dot(x_out_ref[...], placed * scale_ref[...], ((1,), (0,))).reshape(out_ref.shape)
@@ -241,68 +270,103 @@
     return pl.BlockSpec(shape, lambda k: (0,) * len(shape))
 
 
-def mix_modes(lines, weight, scale, x_in, x_out, perm):
-    pairs, _, kx, channels, _ = weight.shape
+def mix_modes(lines, packed, scale, x_in, x_out):
+    pairs, _, turns, channels, wide = packed.shape
     lanes = pairs * channels
     return pl.pallas_call(
         mix_kernel,
-        in_specs=[in_vmem(), in_vmem(), in_hbm(), in_vmem(), in_vmem(), in_vmem()],
+        in_specs=[in_vmem(), in_vmem(), in_hbm()] + [in_vmem()] * 2,
         out_specs=[in_vmem(), in_vmem()],
-        out_shape=[jax.ShapeDtypeStruct(lines.shape, F32), jax.ShapeDtypeStruct((lanes, 2 * kx), F32)],
+        out_shape=[jax.ShapeDtypeStruct(lines.shape, F32), jax.ShapeDtypeStruct((lanes, 2 * KX), F32)],
         scratch_shapes=[
-            pltpu.VMEM((pairs, 2 * kx, channels), F32),
-            pltpu.VMEM(weight.shape, F32),
-            pltpu.SemaphoreType.DMA((pairs,)),
+            pltpu.VMEM(packed.shape, F32),
+            pltpu.VMEM((lanes, 2 * turns * wide), F32),
+            pltpu.VMEM((pairs, 2 * turns, wide), F32),
+            pltpu.SemaphoreType.DMA,
         ],
         compiler_params=params(53),
         name="mix_modes",
-    )(scale, lines, weight, x_in, x_out, perm)
-
-
-def adjoint_kernel(scale_ref, lines_ref, w_hbm, x_in_ref, x_out_ref, perm_ref, out_ref, dspec_ref, cols_ref, w_ref, sem):
-    pairs, _, _, channels, _ = w_ref.shape
-    arrive = weight_copies(w_hbm, w_ref, sem)
+    )(scale, lines, packed, jnp.asarray(x_in), jnp.asarray(quad_columns(x_out, channels)))
+
+
+def adjoint_kernel(
+    scale_ref, lines_ref, w_hbm, x_in_ref, x_out_ref, sums_ref, out_ref, dspec_ref,
+    w_ref, rows_ref, prod_ref, sem,
+):
+    pairs, _, turns, channels, lanes = w_ref.shape
+    copy = pltpu.make_async_copy(w_hbm, w_ref, sem)
+    copy.start()
     placed = exact_dot(x_in_ref[...].T, lines_ref[...].reshape(x_in_ref.shape[0], -1), ((1,), (0,))) * scale_ref[...]
     n = placed.shape[0]
-    parts = dot(jnp.concatenate(split3(placed), axis=0), perm_ref[...])
+    order = chosen((placed.shape[1],) * 2, lambda row, lane: lane_order(row, pairs, channels) == lane)
+    parts = dot(jnp.concatenate(split3(placed), axis=0), order)
     rows = (parts[2 * n :] + parts[n : 2 * n]) + parts[:n]
-    for i in range(pairs):
-        dspec_ref[i] = rows[:, i * channels : (i + 1) * channels]
-    lane = lax.broadcasted_iota(jnp.int32, (channels, 2 * KX), 1)
+    per = 2 * turns
+    for k in range(pairs):
+        mine = rows[:, k * channels : (k + 1) * channels]
+        dspec_ref[k] = mine
+        rows_ref[k] = jnp.concatenate([mine[q * per : (q + 1) * per] for q in range(lanes // channels)], axis=1)
+    copy.wait()
+    half = per * lanes
 
     def step(k, carry):
-        arrive(k)
-        d = dspec_ref[k]
-        cols = jnp.zeros((channels, 2 * KX), F32)
-        for a in range(KX):
-            dr, di = d[a : a + 1], d[KX + a : KX + a + 1]
-            wr, wi = w_ref[k, 0, a], w_ref[k, 1, a]
-            cols = jnp.where(lane == a, jnp.sum(dr * wr + di * wi, axis=1, keepdims=True), cols)
-            cols = jnp.where(lane == KX + a, jnp.sum(di * wr - dr * wi, axis=1, keepdims=True), cols)
-        for g in range(channels // CB):
-            cols_ref[pl.ds(pl.multiple_of(g * pairs * CB + k * CB, CB), CB), :] = cols[g * CB : (g + 1) * CB]
+        d = rows_ref[k]
+        at = pl.ds(pl.multiple_of(k * channels, channels), channels)
+        for t in range(turns):
+            dr, di = d[t : t + 1], d[turns + t : turns + t + 1]
+            wr, wi = w_ref[k, 0, t], w_ref[k, 1, t]
+            for part, value in enumerate((dr * wr + di * wi, di * wr - dr * wi)):
+                first = (part * turns + t) * lanes
+                hi = value.astype(BF16)
+                prod_ref[at, first : first + lanes] = hi
+                prod_ref[at, half + first : half + first + lanes] = (value - hi.astype(F32)).astype(BF16)
         return carry
 
-    lax.fori_loop(0, pairs, step, 0)
-    out_ref[...] = exact_dot(x_out_ref[...], cols_ref[...], ((1,), (1,))).reshape(out_ref.shape)
-
-
-def adjoint_modes(lines, weight, scale, x_in, x_out, perm_back):
-    pairs, _, kx, channels, _ = weight.shape
-    lanes = pairs * channels
+    lax.fori_loop(0, pairs, step, 0, unroll=2)
+    fold = chosen(
+        (2 * half, 2 * KX),
+        lambda row, lane: lax.rem(row, half) // channels == lax.rem(lane, per) * (lanes // channels) + lane // per,
+    )
+    sums = dot(prod_ref[...], fold)
+    cols = jnp.concatenate(
+        [
+            sums[k * channels + g * CB : k * channels + (g + 1) * CB]
+            for g in range(channels // CB)
+            for k in range(pairs)
+        ],
+        axis=0,
+    )
+    lines = exact_dot(x_out_ref[...], cols, ((1,), (1,)))
+    out_ref[:, :, :, : lines.shape[1]] = lines.reshape(lines_ref.shape)
+    out_ref[:, :, :, lines.shape[1] :] = jnp.broadcast_to(sums_ref[...][None], out_ref.shape[:1] + sums_ref.shape)
+
+
+def adjoint_modes(lines, packed, scale, x_in, x_out, sums):
+    pairs, _, turns, channels, wide = packed.shape
     return pl.pallas_call(
         adjoint_kernel,
-        in_specs=[in_vmem(), in_vmem(), in_hbm(), in_vmem(), in_vmem(), in_vmem()],
+        in_specs=[in_vmem(), in_vmem(), in_hbm()] + [in_vmem()] * 3,
         out_specs=[in_vmem(), in_vmem()],
-        out_shape=[jax.ShapeDtypeStruct(lines.shape, F32), jax.ShapeDtypeStruct((pairs, 2 * kx, channels), F32)],
+        out_shape=[
+            jax.ShapeDtypeStruct(lines.shape[:3] + (lines.shape[3] + sums.shape[2],), F32),
+            jax.ShapeDtypeStruct((pairs, 2 * KX, channels), F32),
+        ],
         scratch_shapes=[
-            pltpu.VMEM((lanes, 2 * kx), F32),
-            pltpu.VMEM(weight.shape, F32),
-            pltpu.SemaphoreType.DMA((pairs,)),
+            pltpu.VMEM(packed.shape, F32),
+            pltpu.VMEM((pairs, 2 * turns, wide), F32),
+            pltpu.VMEM((pairs * channels, 4 * turns * wide), BF16),
+            pltpu.SemaphoreType.DMA,
         ],
         compiler_params=params(53),
         name="adjoint_modes",
-    )(scale, lines, weight, x_in, x_out, perm_back)
+    )(
+        scale,
+        lines,
+        packed,
+        jnp.asarray(quad_columns(x_in, channels)),
+        jnp.asarray(quad_columns(x_out, channels)),
+        sums,
+    )
 
 
 PER_STEP = 4
@@ -311,12 +375,16 @@
 def outer_kernel(spec_ref, dspec_ref, out_ref):
     channels = dspec_ref.shape[-1]
     pairs = spec_ref.shape[0] // channels
+    quad = quad_of(channels)
+    per = 2 * KX // quad
     for i in range(PER_STEP):
         v = columns(spec_ref, pl.program_id(0) * PER_STEP + i, pairs, channels)
         d = dspec_ref[i]
         for a in range(KX):
             vr, vi = v[:, a : a + 1], v[:, KX + a : KX + a + 1]
-            dr, di = d[a : a + 1], d[KX + a : KX + a + 1]
+            t, q = divmod(a, quad)
+            dr = d[q * per + t : q * per + t + 1]
+            di = d[q * per + per // 2 + t : q * per + per // 2 + t + 1]
             out_ref[i, 0, a] = vr * dr + vi * di
             out_ref[i, 1, a] = vr * di - vi * dr
 
@@ -356,7 +424,7 @@
     tables = y_out_ref[...].reshape(-1, rows)
     tables = jnp.concatenate([tables, tables], axis=1)
     for h in range(lines_ref.shape[1]):
-        block = lines_ref[:, h].reshape(rows, lines_ref.shape[-1])
+        block = lines_ref[:, h, :, : low_ref.shape[1]].reshape(rows, low_ref.shape[1])
         if bias is not None:
             row = lax.broadcasted_iota(jnp.int32, (rows, 1), 0) // XB
             block = block + jnp.where(row == KY // 2 * 2, bias, 0.0)
@@ -440,23 +508,31 @@
 def rows_in_turn(rows, z_out_ref, b_ref, even_ref, odd_ref, arrive, use, leave):
     groups = b_ref.shape[1]
 
-    def synthesise_z(x, g, space_ref):
-        space_ref[g] = dot(b_ref[x, g], z_out_ref[...])
+    lanes = even_ref.shape[2] // CB * PER_USE
+
+    def synthesise_z(x, g, c, space_ref):
+        at = slice(c // PER_USE * lanes, (c // PER_USE + 1) * lanes)
+        space_ref[g, :, at] = dot(b_ref[x, g], z_out_ref[:, at])
 
     for g in range(groups):
-        synthesise_z(0, g, even_ref)
+        for c in range(0, CB, PER_USE):
+            synthesise_z(0, g, c, even_ref)
 
     def pair(i, carry):
         for n, here, there in ((0, even_ref, odd_ref), (1, odd_ref, even_ref)):
             x = 2 * i + n
             arrive(x)
             for g in range(groups):
-                synthesise_z(jnp.minimum(x + 1, rows - 1), g, there)
-                use(x, g, here)
+                for c in range(0, CB, PER_USE):
+                    synthesise_z(jnp.minimum(x + 1, rows - 1), g, c, there)
+                    use(x, g, c, here)
             leave(x)
         return carry
 
     return pair
+
+
+PER_USE = 8
 
 
 def slope_kernel(
@@ -483,8 +559,8 @@
         def _():
             begin(x + 2)
 
-    def use(x, g, space_ref):
-        for c in range(CB):
+    def use(x, g, first, space_ref):
+        for c in range(first, first + PER_USE):
             o = g * CB + c
             for y in range(0, ny, YB):
                 at = slice(y, y + YB)
@@ -538,7 +614,7 @@
 
 
 def back_kernel(
-    lines_ref, local_hbm, y_out_ref, z_out_ref, out_hbm,
+    factor, lines_ref, sums_ref, local_hbm, y_out_ref, z_out_ref, out_hbm, mix_ref, bias_ref,
     local_ref, out_ref, low_ref, b_ref, even_ref, odd_ref, local_sem, out_sem,
 ):
     channels, rows, ny, nz = local_ref.shape
@@ -546,6 +622,11 @@
     out_copy = row_copy(out_ref, out_hbm, out_sem)
     each_row(3, lambda x: local_copy(x).start())
     synthesise_y(lines_ref, None, y_out_ref, low_ref, b_ref)
+    wide = channels * channels // 8
+    total = jnp.sum(sums_ref[...], axis=0) * factor
+    mixing, biases = total[0, :, :wide], total[-1, :, total.shape[2] - wide :]
+    mix_ref[...] = jnp.concatenate([mixing[:, c : c + channels] for c in range(0, wide, channels)], axis=0)
+    bias_ref[...] = biases[:1, :channels]
 
     def arrive(x):
         local_copy(x).wait()
@@ -554,8 +635,8 @@
         def _():
             local_copy(x + 3).start()
 
-    def use(x, g, space_ref):
-        for c in range(CB):
+    def use(x, g, first, space_ref):
+        for c in range(first, first + PER_USE):
             o = g * CB + c
             for y in range(0, ny, YB):
                 at = slice(y, y + YB)
@@ -567,20 +648,24 @@
     each_row(rows, lambda x: out_copy(x).wait())
 
 
-def back(lines, local):
+def back(lines, sums, local, factor):
     channels, rows, ny, nz = local.shape
     _, _, y_out, z_out = plane_tables(ny, nz)
     return pl.pallas_call(
-        back_kernel,
-        in_specs=[in_vmem(), in_hbm(), in_vmem(), in_vmem()],
-        out_specs=in_hbm(),
-        out_shape=jax.ShapeDtypeStruct(local.shape, BF16),
+        functools.partial(back_kernel, factor),
+        in_specs=[in_vmem(), in_vmem(), in_hbm(), in_vmem(), in_vmem()],
+        out_specs=[in_hbm(), in_vmem(), in_vmem()],
+        out_shape=[
+            jax.ShapeDtypeStruct(local.shape, BF16),
+            jax.ShapeDtypeStruct((channels, channels), F32),
+            jax.ShapeDtypeStruct((1, channels), F32),
+        ],
         scratch_shapes=[pltpu.VMEM(local.shape, BF16)] * 2
         + space_scratch(rows, channels, ny, nz)
         + [pltpu.SemaphoreType.DMA((rows,))] * 2,
         compiler_params=params(53),
         name="back",
-    )(lines, local, jnp.asarray(y_out), jnp.asarray(z_out))
+    )(lines, sums, local, jnp.asarray(y_out), jnp.asarray(z_out))
 
 
 def cell_sums_kernel(grad_ref, f_ref, dlines_ref, sums_ref, acc_ref):
@@ -619,26 +704,29 @@
         channel = lax.broadcasted_iota(jnp.int32, (channels, KZ * channels), 0)
         pick = (lane == channel // CB * lanes + lax.rem(channel, CB)).astype(F32)
         biases = exact_dot(jnp.broadcast_to(line, (8, line.shape[1])), pick, ((1,), (1,)))
-        packed = jnp.concatenate(
-            [
-                jnp.concatenate([mixing[r : r + 8] for r in range(0, channels, 8)], axis=1),
-                jnp.concatenate([biases] * (channels // 8), axis=1),
-            ],
-            axis=0,
-        )
-        sums_ref[...] = jnp.broadcast_to(packed[None], sums_ref.shape)
-
-
-def cell_sums(pre_grad, features, dlines, devices):
+        packed = [
+            jnp.concatenate([mixing[r : r + 8] for r in range(0, channels, 8)], axis=1),
+            jnp.concatenate([biases] * (channels // 8), axis=1),
+        ]
+        if sums_ref.shape[0] == 1:
+            sums_ref[0] = jnp.concatenate(packed, axis=1)
+        else:
+            for h in range(sums_ref.shape[0]):
+                sums_ref[h] = packed[min(h, 1)]
+
+
+def cell_sums(pre_grad, features, dlines):
     channels, rows, ny, nz = features.shape
     cells = pl.BlockSpec((channels, 2, ny, nz), lambda x: (0, x, 0, 0))
     tile = channels * YB
+    blocks = rows // XB
+    shape = (blocks, 8, channels * channels // 8 * (2 if blocks == 1 else 1))
     return pl.pallas_call(
         cell_sums_kernel,
         grid=(rows // 2,),
         in_specs=[cells, cells, whole(dlines.shape)],
-        out_specs=whole((devices, 16, channels * channels // 8)),
-        out_shape=jax.ShapeDtypeStruct((devices, 16, channels * channels // 8), F32),
+        out_specs=whole(shape),
+        out_shape=jax.ShapeDtypeStruct(shape, F32),
         scratch_shapes=[pltpu.VMEM((tile, tile), F32)],
         compiler_params=params(53),
         name="cell_sums",
@@ -658,9 +746,7 @@
     blocks = rows // XB
     cut = KZ // pairs
     cells = nx * ny * nz
-    x_in, x_out = (jnp.asarray(t) for t in line_tables(nx))
-    perm = jnp.asarray(lane_tables(pairs, channels))
-    perm_back = jnp.asarray(lane_tables(pairs, channels).T)
+    x_in, x_out = line_tables(nx)
     if cut == 1:
         first_k = 0
     else:
@@ -675,27 +761,28 @@
         return swap(lines.reshape(devices, blocks, 2 * XB, -1))
 
     def to_cells(lines):
-        lines = swap(lines.reshape(devices, blocks, 2 * XB, -1))
+        lines = swap(lines)
+        own = pairs * channels
+        extra = lines[..., own:]
         if cut > 1:
-            lines = lines.reshape(KY, cut, blocks, 2 * XB, groups, pairs * CB)
-            lines = lines.transpose(0, 2, 3, 4, 1, 5)
-        return lines.reshape(KY, blocks, 2 * XB, -1)
+            lines = lines[..., :own].reshape(KY, cut, blocks, 2 * XB, groups, pairs * CB)
+            lines = lines.transpose(0, 2, 3, 4, 1, 5).reshape(KY, blocks, 2 * XB, -1)
+        return lines, extra
 
     lines = to_owner(feature_lines(features))
-    mixed, spec = mix_modes(lines, spectral_weight, scale, x_in, x_out, perm)
-    pre_grad, dlines = slope(to_cells(mixed), local_branch(features, pointwise_weight, False), cotangent, biases)
-    sums = cell_sums(pre_grad, features, dlines, devices)
-    dlines, _ = lax.optimization_barrier((to_owner(dlines), sums))
-    dmixed, dspec = adjoint_modes(dlines, spectral_weight, scale, x_in, x_out, perm_back)
-    back_lines = to_cells(dmixed)
+    packed = pack_weights(spectral_weight)
+    lines, packed = lax.optimization_barrier((lines, packed))
+    mixed, spec = mix_modes(lines, packed, scale, x_in, x_out)
+    pre_grad, dlines = slope(to_cells(mixed)[0], local_branch(features, pointwise_weight, False), cotangent, biases)
+    sums = cell_sums(pre_grad, features, dlines)
+    dlines = to_owner(dlines)
+    dmixed, dspec = adjoint_modes(dlines, packed, scale, x_in, x_out, sums)
+    back_lines, sums = to_cells(dmixed)
     spectral_grad = mode_gradient(spec, dspec)
     late_grad, _ = lax.optimization_barrier((pre_grad, dspec))
     local_back = local_branch(late_grad, pointwise_weight, True)
-    total = jnp.sum(swap(sums), axis=0) * float(cells) ** -0.5
-    mix_total = total[:8].reshape(8, channels // 8, channels).transpose(1, 0, 2).reshape(channels, channels)
-    bias_total = total[8, :channels]
-    features_grad = back(back_lines, local_back)
-    return (features_grad, spectral_grad, mix_total, bias_total)
+    features_grad, mix_total, bias_total = back(back_lines, sums, local_back, float(cells) ** -0.5)
+    return (features_grad, spectral_grad, mix_total, bias_total[0])
 
 
 def solution(mesh):

time: 138 us -> 129 us (0.935)
  starting transfers between devices: 25.1 us -> 19.7 us
  waiting for transfers between devices: 23.3 us -> 19.2 us
    all_to_all x5 -> x4, starting transfers between devices: 25.1 us -> 19.7 us  [swap(): return lax.all_to_all(blocks, 'mp', 0, 0, tiled=True)]
    all_to_all x5 -> x4, waiting for transfers between devices: 23.3 us -> 19.2 us  [swap(): return lax.all_to_all(blocks, 'mp', 0, 0, tiled=True)]
    pallas_call x3 -> x4, Pallas kernels: 24.6 us -> 26.3 us  [the longest x1 9.32 us: back(): pl.pallas_call(functools.partial(back_kernel, factor), in_specs=[in_vmem(...]
  transfers between devices with their start and end apart: 5 -> 4, of which waited for: 4 -> 4; matrix products, arithmetic and copies ran while one was open for 1% -> 0% of each run, Pallas kernels for 31% -> 31%
where the time goes in v3:
time: 129 us
  Pallas kernels  86.5 us (67%)
  starting transfers between devices  19.7 us (15%)
  waiting for transfers between devices  19.2 us (15%)
  local copies, waits for them, and re-layouts  2.03 us (2%)
    all_to_all x4, starting transfers between devices, swap(): return lax.all_to_all(blocks, 'mp', 0, 0, tiled=True)  19.7 us
    pallas_call x2, Pallas kernels, local_branch(): pl.pallas_call(functools.partial(local_kernel, by_column), grid=(rows //...  19.6 us
    all_to_all x4, waiting for transfers between devices, swap(): return lax.all_to_all(blocks, 'mp', 0, 0, tiled=True)  19.2 us
    pallas_call x1, Pallas kernels, slope(): pl.pallas_call(slope_kernel, in_specs=[in_vmem(), in_vmem(), in_hbm(), in...  18.8 us
    pallas_call x1, Pallas kernels, cell_sums(): pl.pallas_call(cell_sums_kernel, grid=(rows // 2,), in_specs=[cells, cell...  9.67 us
    pallas_call x1, Pallas kernels, back(): pl.pallas_call(functools.partial(back_kernel, factor), in_specs=[in_vmem(...  9.32 us
    pallas_call x1, Pallas kernels, feature_lines(): pl.pallas_call(lines_kernel, in_specs=[in_hbm()] * 3, out_specs=in_vmem()...  7.08 us
    pallas_call x1, Pallas kernels, pack_weights(): pl.pallas_call(pack_kernel, grid=(pairs // PER_STEP,), in_specs=[pl.Block...  6.06 us
  transfers between devices with their start and end apart: 4, of which 4 were waited for; matrix products, arithmetic and copies ran while one was open for 0% of the time, Pallas kernels for 31%

profile of v3, /device:TPU:0, one launch (start us, length us, event | category | flops | bytes accessed | tf_op | source)
XLA Modules:
  0.0 128.5 jit_solution(12823174730509844588)
XLA Ops:
  0.7 7.1 %feature_lines.1 = f32[16,2,8,512]{3,2,1,0:T(8,128)} custom-call(bf16[32,8,128,128]{3,2,1,0:T(8,128)(2,1)} %f_ref.1, bf16[256,512]{1,0:T(8,128)(2,1)} %constant.24.clone.y_in_hbm.y_in_ref, bf16[8,256,128]{2,1,0:T(8,128)(2,1)} %constant.25.clone.z_in_hbm.z_in_ref), custom_call_target="tpu_custom_call" | custom-call | tf_op jit(solution)/shard_map/feature_lines/pallas_call | solution.py:160
  7.8 7.4 %all-to-all-start = ((f32[16,2,8,512]{3,2,1,0:T(8,128)}), f32[16,2,8,512]{3,2,1,0:T(8,128)S(1)}, u32[]{:S(2)}, u32[]{:S(2)}) async-start(f32[16,2,8,512]{3,2,1,0:T(8,128)} %feature_lines.1), calls=%async_computation | async-start | bytes 1048576 | tf_op jit(solution)/shard_map/all_to_all | solution.py:737
  15.2 0.1 div.14.scale_ref
  15.3 6.1 %pack_weights.1.w_hbm = f32[16,2,4,32,128]{4,3,2,1,0:T(8,128)} custom-call(f32[16,2,16,32,32]{4,3,2,1,0:T(8,128)} %w_ref.3), custom_call_target="tpu_custom_call" | custom-call | bytes 16777216 | tf_op jit(solution)/shard_map/pack_weights/pallas_call | solution.py:211
  21.3 8.3 %all-to-all-done.lines_ref = f32[16,2,8,512]{3,2,1,0:T(8,128)S(1)} async-done(((f32[16,2,8,512]{3,2,1,0:T(8,128)}), f32[16,2,8,512]{3,2,1,0:T(8,128)S(1)}, u32[]{:S(2)}, u32[]{:S(2)}) %all-to-all-start) | async-done | bytes 524320 | tf_op jit(solution)/shard_map/all_to_all | solution.py:737
  29.6 0.8 copy-done.8
  30.4 5.7 %mix_modes.1 = (f32[16,2,8,512]{3,2,1,0:T(8,128)}, f32[512,32]{1,0:T(8,128)S(1)}) custom-call(f32[1,512]{1,0:T(1,128)S(1)} %div.14.scale_ref, f32[16,2,8,512]{3,2,1,0:T(8,128)} %copy-done.8, f32[16,2,4,32,128]{4,3,2,1,0:T(8,128)} %pack_weights.1.w_hbm, f32[256,32]{1,0:T(8,128)S(1)} %copy-done.5, f32[256,32]{1,0:T(8,128)S(1)} %copy-done.2), custom_call_target="tpu_custom_call" | custom-call | tf_op jit(solution)/shard_map/mix_modes/pallas_call | solution.py:276
  36.1 4.1 %all-to-all-start.1 = ((f32[16,2,8,512]{3,2,1,0:T(8,128)}), f32[16,2,8,512]{3,2,1,0:T(8,128)S(1)}, u32[]{:S(2)}, u32[]{:S(2)}) async-start(f32[16,2,8,512]{3,2,1,0:T(8,128)} %get-tuple-element.18), calls=%async_computation.1 | async-start | bytes 1048576 | tf_op jit(solution)/shard_map/all_to_all | solution.py:737
  40.3 0.1 broadcast_in_dim.43
  40.4 0.1 broadcast_select_fusion
  40.4 0.1 select_n.31.bias_ref
  40.6 9.9 %local_branch.2.local_hbm = bf16[32,8,128,128]{3,2,1,0:T(8,128)(2,1)} custom-call(bf16[32,8,128,128]{3,2,1,0:T(8,128)(2,1)} %f_ref.1, bf16[32,32]{1,0:T(8,128)(2,1)S(1)} %copy-done.6), custom_call_target="tpu_custom_call" | custom-call | flops 268435456 | bytes 16777216 | tf_op jit(solution)/shard_map/local_branch/pallas_call | solution.py:472
  50.4 4.3 %all-to-all-done.1.lines_ref = f32[16,2,8,512]{3,2,1,0:T(8,128)S(1)} async-done(((f32[16,2,8,512]{3,2,1,0:T(8,128)}), f32[16,2,8,512]{3,2,1,0:T(8,128)S(1)}, u32[]{:S(2)}, u32[]{:S(2)}) %all-to-all-start.1) | async-done | bytes 524320 | tf_op jit(solution)/shard_map/all_to_all | solution.py:737
  54.7 18.8 %slope.1 = (bf16[32,8,128,128]{3,2,1,0:T(8,128)(2,1)}, f32[16,2,8,512]{3,2,1,0:T(8,128)}) custom-call(f32[1,512]{1,0:T(1,128)S(1)} %select_n.31.bias_ref, f32[16,2,8,512]{3,2,1,0:T(8,128)S(1)} %all-to-all-done.1.lines_ref, bf16[32,8,128,128]{3,2,1,0:T(8,128)(2,1)} %local_branch.2.local_hbm, bf16[32,8,128,128]{3,2,1,0:T(8,128)(2,1)} %cot_hbm.1, ...), custom_call_target="tpu_custom_call" | custom-call | tf_op jit(solution)/shard_map/slope/pallas_call | solution.py:599
  73.5 4.1 %all-to-all-start.2 = ((f32[16,2,8,512]{3,2,1,0:T(8,128)}), f32[16,2,8,512]{3,2,1,0:T(8,128)S(1)}, u32[]{:S(2)}, u32[]{:S(2)}) async-start(f32[16,2,8,512]{3,2,1,0:T(8,128)} %get-tuple-element.19.dlines_ref), calls=%async_computation.2 | async-start | bytes 1048576 | tf_op jit(solution)/shard_map/all_to_all | solution.py:737
  77.6 9.7 %cell_sums.1.sums_ref = f32[2,8,128]{2,1,0:T(8,128)S(1)} custom-call(bf16[32,8,128,128]{3,2,1,0:T(8,128)(2,1)} %get-tuple-element.23.grad_ref.cells_ref, bf16[32,8,128,128]{3,2,1,0:T(8,128)(2,1)} %f_ref.1, f32[16,2,8,512]{3,2,1,0:T(8,128)} %get-tuple-element.19.dlines_ref), custom_call_target="tpu_custom_call" | custom-call | tf_op jit(solution)/shard_map/cell_sums/pallas_call | solution.py:724
  87.3 4.8 %all-to-all-done.2.lines_ref = f32[16,2,8,512]{3,2,1,0:T(8,128)S(1)} async-done(((f32[16,2,8,512]{3,2,1,0:T(8,128)}), f32[16,2,8,512]{3,2,1,0:T(8,128)S(1)}, u32[]{:S(2)}, u32[]{:S(2)}) %all-to-all-start.2) | async-done | bytes 524320 | tf_op jit(solution)/shard_map/all_to_all | solution.py:737
  92.1 5.2 %adjoint_modes.1 = (f32[16,2,8,640]{3,2,1,0:T(8,128)}, f32[16,32,32]{2,1,0:T(8,128)S(1)}) custom-call(f32[1,512]{1,0:T(1,128)S(1)} %div.14.scale_ref, f32[16,2,8,512]{3,2,1,0:T(8,128)S(1)} %all-to-all-done.2.lines_ref, f32[16,2,4,32,128]{4,3,2,1,0:T(8,128)} %pack_weights.1.w_hbm, f32[256,32]{1,0:T(8,128)S(1)} %copy-done.2, f32[256,32]{1,0:T(8,128)S(1)} %copy-done.2, ...), custom_call_target="tpu_custom_call" | custom-call | tf_op jit(solution)/shard_map/adjoint_modes/pallas_call | solution.py:346
  97.4 4.1 %all-to-all-start.3 = ((f32[16,2,8,640]{3,2,1,0:T(8,128)}), f32[16,2,8,640]{3,2,1,0:T(8,128)S(1)}, u32[]{:S(2)}, u32[]{:S(2)}) async-start(f32[16,2,8,640]{3,2,1,0:T(8,128)} %get-tuple-element.21), calls=%async_computation.3 | async-start | bytes 1310720 | tf_op jit(solution)/shard_map/all_to_all | solution.py:737
  101.5 5.1 %mode_gradient.1 = f32[16,2,16,32,32]{4,3,2,1,0:T(8,128)} custom-call(f32[512,32]{1,0:T(8,128)S(1)} %get-tuple-element.25.spec_ref, f32[16,32,32]{2,1,0:T(8,128)S(1)} %get-tuple-element.22.dspec_ref), custom_call_target="tpu_custom_call" | custom-call | tf_op jit(solution)/shard_map/mode_gradient/pallas_call | solution.py:395
  106.6 9.7 %local_branch.3.local_hbm = bf16[32,8,128,128]{3,2,1,0:T(8,128)(2,1)} custom-call(bf16[32,8,128,128]{3,2,1,0:T(8,128)(2,1)} %get-tuple-element.23.grad_ref.cells_ref, bf16[32,32]{1,0:T(8,128)(2,1)S(1)} %copy-done.6), custom_call_target="tpu_custom_call" | custom-call | flops 268435456 | bytes 16777216 | tf_op jit(solution)/shard_map/local_branch/pallas_call | solution.py:472
  116.3 1.8 %all-to-all-done.3.lines_ref = f32[16,2,8,640]{3,2,1,0:T(8,128)S(1)} async-done(((f32[16,2,8,640]{3,2,1,0:T(8,128)}), f32[16,2,8,640]{3,2,1,0:T(8,128)S(1)}, u32[]{:S(2)}, u32[]{:S(2)}) %all-to-all-start.3) | async-done | bytes 655392 | tf_op jit(solution)/shard_map/all_to_all | solution.py:737
  118.1 0.9 copy-done.7
  119.0 9.3 %back.1 = (bf16[32,8,128,128]{3,2,1,0:T(8,128)(2,1)}, f32[32,32]{1,0:T(8,128)}, f32[1,32]{1,0:T(1,128)}) custom-call(f32[16,2,8,640]{3,2,1,0:T(8,128)} %copy-done.7, f32[16,2,8,128]{3,2,1,0:T(8,128)S(1)} %slice.4.sums_ref, bf16[32,8,128,128]{3,2,1,0:T(8,128)(2,1)} %local_branch.3.local_hbm, bf16[4,256,128]{2,1,0:T(8,128)(2,1)S(1)} %copy-done.3, ...), custom_call_target="tpu_custom_call" | custom-call | tf_op jit(solution)/shard_map/back/pallas_call | solution.py:654
  (21 shorter events, 0.1 us)
Async XLA Ops:
  0.6 29.8 %copy-start.2 = (f32[256,32]{1,0:T(8,128)S(1)}, f32[256,32]{1,0:T(8,128)}, u32[]{:S(2)}) copy-start(f32[256,32]{1,0:T(8,128)} %constant.27.clone.x_out_ref.x_in_ref) | copy-start | bytes 98308
  0.6 29.8 %copy-start.5 = (f32[256,32]{1,0:T(8,128)S(1)}, f32[256,32]{1,0:T(8,128)}, u32[]{:S(2)}) copy-start(f32[256,32]{1,0:T(8,128)} %constant.26.clone.x_in_ref) | copy-start | bytes 98308
  7.7 32.5 %copy-start.9 = (f32[32]{0:T(128)S(1)}, f32[32]{0:T(128)}, u32[]{:S(2)}) copy-start(f32[32]{0:T(128)} %param.17) | copy-start | bytes 388
  7.8 32.8 %copy-start.6 = (bf16[32,32]{1,0:T(8,128)(2,1)S(1)}, bf16[32,32]{1,0:T(8,128)(2,1)}, u32[]{:S(2)}) copy-start(bf16[32,32]{1,0:T(8,128)(2,1)} %w_ref.5) | copy-start | bytes 6148
  7.8 21.9 %all-to-all-start = ((f32[16,2,8,512]{3,2,1,0:T(8,128)}), f32[16,2,8,512]{3,2,1,0:T(8,128)S(1)}, u32[]{:S(2)}, u32[]{:S(2)}) async-start(f32[16,2,8,512]{3,2,1,0:T(8,128)} %feature_lines.1), calls=%async_computation | async-start | bytes 1048576 | tf_op jit(solution)/shard_map/all_to_all | solution.py:737
  29.6 0.8 copy-start.8
  36.1 18.6 %all-to-all-start.1 = ((f32[16,2,8,512]{3,2,1,0:T(8,128)}), f32[16,2,8,512]{3,2,1,0:T(8,128)S(1)}, u32[]{:S(2)}, u32[]{:S(2)}) async-start(f32[16,2,8,512]{3,2,1,0:T(8,128)} %get-tuple-element.18), calls=%async_computation.1 | async-start | bytes 1048576 | tf_op jit(solution)/shard_map/all_to_all | solution.py:737
  40.5 14.2 %copy-start = (bf16[256,1024]{1,0:T(8,128)(2,1)S(1)}, bf16[256,1024]{1,0:T(8,128)(2,1)}, u32[]{:S(2)}) copy-start(bf16[256,1024]{1,0:T(8,128)(2,1)} %constant.29.clone.z_out_ref) | copy-start | bytes 1572868
  40.5 14.2 %copy-start.1 = (bf16[8,256,128]{2,1,0:T(8,128)(2,1)S(1)}, bf16[8,256,128]{2,1,0:T(8,128)(2,1)}, u32[]{:S(2)}) copy-start(bf16[8,256,128]{2,1,0:T(8,128)(2,1)} %constant.25.clone.z_in_hbm.z_in_ref) | copy-start | bytes 1572868
  40.6 14.2 %copy-start.3 = (bf16[4,256,128]{2,1,0:T(8,128)(2,1)S(1)}, bf16[4,256,128]{2,1,0:T(8,128)(2,1)}, u32[]{:S(2)}) copy-start(bf16[4,256,128]{2,1,0:T(8,128)(2,1)} %constant.28.clone.y_out_ref) | copy-start | bytes 786436
  40.6 14.2 %copy-start.4 = (bf16[256,512]{1,0:T(8,128)(2,1)S(1)}, bf16[256,512]{1,0:T(8,128)(2,1)}, u32[]{:S(2)}) copy-start(bf16[256,512]{1,0:T(8,128)(2,1)} %constant.24.clone.y_in_hbm.y_in_ref) | copy-start | bytes 786436
  73.5 18.6 %all-to-all-start.2 = ((f32[16,2,8,512]{3,2,1,0:T(8,128)}), f32[16,2,8,512]{3,2,1,0:T(8,128)S(1)}, u32[]{:S(2)}, u32[]{:S(2)}) async-start(f32[16,2,8,512]{3,2,1,0:T(8,128)} %get-tuple-element.19.dlines_ref), calls=%async_computation.2 | async-start | bytes 1048576 | tf_op jit(solution)/shard_map/all_to_all | solution.py:737
  97.4 20.7 %all-to-all-start.3 = ((f32[16,2,8,640]{3,2,1,0:T(8,128)}), f32[16,2,8,640]{3,2,1,0:T(8,128)S(1)}, u32[]{:S(2)}, u32[]{:S(2)}) async-start(f32[16,2,8,640]{3,2,1,0:T(8,128)} %get-tuple-element.21), calls=%async_computation.3 | async-start | bytes 1310720 | tf_op jit(solution)/shard_map/all_to_all | solution.py:737
  118.1 0.9 copy-start.7

commit v4 on v3

--- a/solution.py
+++ b/solution.py
@@ -116,8 +116,8 @@
     return pl.BlockSpec(memory_space=pltpu.VMEM)
 
 
-DEPTH = 3
-PER_COPY = 4
+DEPTH = 2
+PER_COPY = 8
 PER_DOT = 16
 
 
@@ -614,16 +614,21 @@
 
 
 def back_kernel(
-    factor, lines_ref, sums_ref, local_hbm, y_out_ref, z_out_ref, out_hbm, mix_ref, bias_ref,
-    local_ref, out_ref, low_ref, b_ref, even_ref, odd_ref, local_sem, out_sem,
+    factor, apart, lines_ref, *refs
 ):
+    sums_ref, refs = (refs[0], refs[1:]) if apart else (None, refs)
+    (
+        local_hbm, y_out_ref, z_out_ref, out_hbm, mix_ref, bias_ref,
+        local_ref, out_ref, low_ref, b_ref, even_ref, odd_ref, local_sem, out_sem,
+    ) = refs
     channels, rows, ny, nz = local_ref.shape
     local_copy = row_copy(local_hbm, local_ref, local_sem)
     out_copy = row_copy(out_ref, out_hbm, out_sem)
     each_row(3, lambda x: local_copy(x).start())
     synthesise_y(lines_ref, None, y_out_ref, low_ref, b_ref)
     wide = channels * channels // 8
-    total = jnp.sum(sums_ref[...], axis=0) * factor
+    shared = sums_ref[...] if apart else lines_ref[:, :, :, low_ref.shape[1] :]
+    total = jnp.sum(shared, axis=0) * factor
     mixing, biases = total[0, :, :wide], total[-1, :, total.shape[2] - wide :]
     mix_ref[...] = jnp.concatenate([mixing[:, c : c + channels] for c in range(0, wide, channels)], axis=0)
     bias_ref[...] = biases[:1, :channels]
@@ -649,11 +654,12 @@
 
 
 def back(lines, sums, local, factor):
+    apart = sums is not None
     channels, rows, ny, nz = local.shape
     _, _, y_out, z_out = plane_tables(ny, nz)
     return pl.pallas_call(
-        functools.partial(back_kernel, factor),
-        in_specs=[in_vmem(), in_vmem(), in_hbm(), in_vmem(), in_vmem()],
+        functools.partial(back_kernel, factor, apart),
+        in_specs=[in_vmem()] * (1 + apart) + [in_hbm(), in_vmem(), in_vmem()],
         out_specs=[in_hbm(), in_vmem(), in_vmem()],
         out_shape=[
             jax.ShapeDtypeStruct(local.shape, BF16),
@@ -663,9 +669,9 @@
         scratch_shapes=[pltpu.VMEM(local.shape, BF16)] * 2
         + space_scratch(rows, channels, ny, nz)
         + [pltpu.SemaphoreType.DMA((rows,))] * 2,
-        compiler_params=params(53),
+        compiler_params=params(46),
         name="back",
-    )(lines, sums, local, jnp.asarray(y_out), jnp.asarray(z_out))
+    )(lines, *([sums] if apart else []), local, jnp.asarray(y_out), jnp.asarray(z_out))
 
 
 def cell_sums_kernel(grad_ref, f_ref, dlines_ref, sums_ref, acc_ref):
@@ -763,8 +769,9 @@
     def to_cells(lines):
         lines = swap(lines)
         own = pairs * channels
-        extra = lines[..., own:]
+        extra = None
         if cut > 1:
+            extra = lines[..., own:]
             lines = lines[..., :own].reshape(KY, cut, blocks, 2 * XB, groups, pairs * CB)
             lines = lines.transpose(0, 2, 3, 4, 1, 5).reshape(KY, blocks, 2 * XB, -1)
         return lines, extra

time: 129 us -> 127 us (0.984)
  Pallas kernels: 86.5 us -> 85.1 us
  transfers between devices with their start and end apart: 4 -> 4, of which waited for: 4 -> 4; matrix products, arithmetic and copies ran while one was open for 0% -> 0% of each run, Pallas kernels for 31% -> 32%
where the time goes in v4:
time: 127 us; the launch traced here: 126 us
  Pallas kernels  85.1 us (67%)
  starting transfers between devices  19.8 us (16%)
  waiting for transfers between devices  19.1 us (15%)
    all_to_all x4, starting transfers between devices, swap(): return lax.all_to_all(blocks, 'mp', 0, 0, tiled=True)  19.8 us
    pallas_call x2, Pallas kernels, local_branch(): pl.pallas_call(functools.partial(local_kernel, by_column), grid=(rows //...  19.6 us
    all_to_all x4, waiting for transfers between devices, swap(): return lax.all_to_all(blocks, 'mp', 0, 0, tiled=True)  19.1 us
    pallas_call x1, Pallas kernels, slope(): pl.pallas_call(slope_kernel, in_specs=[in_vmem(), in_vmem(), in_hbm(), in...  18.9 us
    pallas_call x1, Pallas kernels, cell_sums(): pl.pallas_call(cell_sums_kernel, grid=(rows // 2,), in_specs=[cells, cell...  9.67 us
    pallas_call x1, Pallas kernels, back(): pl.pallas_call(functools.partial(back_kernel, factor, apart), in_specs=[i...  8.22 us
    pallas_call x1, Pallas kernels, feature_lines(): pl.pallas_call(lines_kernel, in_specs=[in_hbm()] * 3, out_specs=in_vmem()...  6.67 us
    pallas_call x1, Pallas kernels, pack_weights(): pl.pallas_call(pack_kernel, grid=(pairs // PER_STEP,), in_specs=[pl.Block...  6.06 us
  transfers between devices with their start and end apart: 4, of which 4 were waited for; matrix products, arithmetic and copies ran while one was open for 0% of the time, Pallas kernels for 32%

profile of v4, /device:TPU:0, one launch (start us, length us, event | category | flops | bytes accessed | tf_op | source)
XLA Modules:
  0.0 126.2 jit_solution(9789115296782982024)
XLA Ops:
  0.6 0.0 copy-start.5
  0.7 6.7 %feature_lines.1 = f32[16,2,8,512]{3,2,1,0:T(8,128)} custom-call(bf16[32,8,128,128]{3,2,1,0:T(8,128)(2,1)} %f_ref.1, bf16[256,512]{1,0:T(8,128)(2,1)} %constant.24.clone.y_in_hbm.y_in_ref, bf16[8,256,128]{2,1,0:T(8,128)(2,1)} %constant.25.clone.z_in_hbm.z_in_ref), custom_call_target="tpu_custom_call" | custom-call | tf_op jit(solution)/shard_map/feature_lines/pallas_call | solution.py:160
  7.4 7.4 %all-to-all-start = ((f32[16,2,8,512]{3,2,1,0:T(8,128)}), f32[16,2,8,512]{3,2,1,0:T(8,128)S(1)}, u32[]{:S(2)}, u32[]{:S(2)}) async-start(f32[16,2,8,512]{3,2,1,0:T(8,128)} %feature_lines.1), calls=%async_computation | async-start | bytes 1048576 | tf_op jit(solution)/shard_map/all_to_all | solution.py:743
  14.8 0.1 div.14.scale_ref
  14.9 6.1 %pack_weights.1.w_hbm = f32[16,2,4,32,128]{4,3,2,1,0:T(8,128)} custom-call(f32[16,2,16,32,32]{4,3,2,1,0:T(8,128)} %w_ref.3), custom_call_target="tpu_custom_call" | custom-call | bytes 16777216 | tf_op jit(solution)/shard_map/pack_weights/pallas_call | solution.py:211
  20.9 8.3 %all-to-all-done.lines_ref = f32[16,2,8,512]{3,2,1,0:T(8,128)S(1)} async-done(((f32[16,2,8,512]{3,2,1,0:T(8,128)}), f32[16,2,8,512]{3,2,1,0:T(8,128)S(1)}, u32[]{:S(2)}, u32[]{:S(2)}) %all-to-all-start) | async-done | bytes 524320 | tf_op jit(solution)/shard_map/all_to_all | solution.py:743
  29.2 0.8 copy-done.7
  30.0 5.7 %mix_modes.1 = (f32[16,2,8,512]{3,2,1,0:T(8,128)}, f32[512,32]{1,0:T(8,128)S(1)}) custom-call(f32[1,512]{1,0:T(1,128)S(1)} %div.14.scale_ref, f32[16,2,8,512]{3,2,1,0:T(8,128)} %copy-done.7, f32[16,2,4,32,128]{4,3,2,1,0:T(8,128)} %pack_weights.1.w_hbm, f32[256,32]{1,0:T(8,128)S(1)} %copy-done.5, f32[256,32]{1,0:T(8,128)S(1)} %copy-done.2), custom_call_target="tpu_custom_call" | custom-call | tf_op jit(solution)/shard_map/mix_modes/pallas_call | solution.py:276
  35.7 4.1 %all-to-all-start.1 = ((f32[16,2,8,512]{3,2,1,0:T(8,128)}), f32[16,2,8,512]{3,2,1,0:T(8,128)S(1)}, u32[]{:S(2)}, u32[]{:S(2)}) async-start(f32[16,2,8,512]{3,2,1,0:T(8,128)} %get-tuple-element.18), calls=%async_computation.1 | async-start | bytes 1048576 | tf_op jit(solution)/shard_map/all_to_all | solution.py:743
  39.9 0.1 broadcast_in_dim.43
  40.0 0.1 broadcast_select_fusion
  40.0 0.1 select_n.31.bias_ref
  40.2 9.9 %local_branch.2.local_hbm = bf16[32,8,128,128]{3,2,1,0:T(8,128)(2,1)} custom-call(bf16[32,8,128,128]{3,2,1,0:T(8,128)(2,1)} %f_ref.1, bf16[32,32]{1,0:T(8,128)(2,1)S(1)} %copy-done.6), custom_call_target="tpu_custom_call" | custom-call | flops 268435456 | bytes 16777216 | tf_op jit(solution)/shard_map/local_branch/pallas_call | solution.py:472
  50.0 4.3 %all-to-all-done.1.lines_ref = f32[16,2,8,512]{3,2,1,0:T(8,128)S(1)} async-done(((f32[16,2,8,512]{3,2,1,0:T(8,128)}), f32[16,2,8,512]{3,2,1,0:T(8,128)S(1)}, u32[]{:S(2)}, u32[]{:S(2)}) %all-to-all-start.1) | async-done | bytes 524320 | tf_op jit(solution)/shard_map/all_to_all | solution.py:743
  54.3 18.9 %slope.1 = (bf16[32,8,128,128]{3,2,1,0:T(8,128)(2,1)}, f32[16,2,8,512]{3,2,1,0:T(8,128)}) custom-call(f32[1,512]{1,0:T(1,128)S(1)} %select_n.31.bias_ref, f32[16,2,8,512]{3,2,1,0:T(8,128)S(1)} %all-to-all-done.1.lines_ref, bf16[32,8,128,128]{3,2,1,0:T(8,128)(2,1)} %local_branch.2.local_hbm, bf16[32,8,128,128]{3,2,1,0:T(8,128)(2,1)} %cot_hbm.1, ...), custom_call_target="tpu_custom_call" | custom-call | tf_op jit(solution)/shard_map/slope/pallas_call | solution.py:599
  73.2 4.1 %all-to-all-start.2 = ((f32[16,2,8,512]{3,2,1,0:T(8,128)}), f32[16,2,8,512]{3,2,1,0:T(8,128)S(1)}, u32[]{:S(2)}, u32[]{:S(2)}) async-start(f32[16,2,8,512]{3,2,1,0:T(8,128)} %get-tuple-element.19.dlines_ref), calls=%async_computation.2 | async-start | bytes 1048576 | tf_op jit(solution)/shard_map/all_to_all | solution.py:743
  77.3 9.7 %cell_sums.1.sums_ref = f32[2,8,128]{2,1,0:T(8,128)S(1)} custom-call(bf16[32,8,128,128]{3,2,1,0:T(8,128)(2,1)} %get-tuple-element.23.grad_ref.cells_ref, bf16[32,8,128,128]{3,2,1,0:T(8,128)(2,1)} %f_ref.1, f32[16,2,8,512]{3,2,1,0:T(8,128)} %get-tuple-element.19.dlines_ref), custom_call_target="tpu_custom_call" | custom-call | tf_op jit(solution)/shard_map/cell_sums/pallas_call | solution.py:730
  87.0 4.8 %all-to-all-done.2.lines_ref = f32[16,2,8,512]{3,2,1,0:T(8,128)S(1)} async-done(((f32[16,2,8,512]{3,2,1,0:T(8,128)}), f32[16,2,8,512]{3,2,1,0:T(8,128)S(1)}, u32[]{:S(2)}, u32[]{:S(2)}) %all-to-all-start.2) | async-done | bytes 524320 | tf_op jit(solution)/shard_map/all_to_all | solution.py:743
  91.8 5.2 %adjoint_modes.1 = (f32[16,2,8,640]{3,2,1,0:T(8,128)}, f32[16,32,32]{2,1,0:T(8,128)S(1)}) custom-call(f32[1,512]{1,0:T(1,128)S(1)} %div.14.scale_ref, f32[16,2,8,512]{3,2,1,0:T(8,128)S(1)} %all-to-all-done.2.lines_ref, f32[16,2,4,32,128]{4,3,2,1,0:T(8,128)} %pack_weights.1.w_hbm, f32[256,32]{1,0:T(8,128)S(1)} %copy-done.2, f32[256,32]{1,0:T(8,128)S(1)} %copy-done.2, ...), custom_call_target="tpu_custom_call" | custom-call | tf_op jit(solution)/shard_map/adjoint_modes/pallas_call | solution.py:346
  97.0 4.1 %all-to-all-start.3 = ((f32[16,2,8,640]{3,2,1,0:T(8,128)}), f32[16,2,8,640]{3,2,1,0:T(8,128)S(1)}, u32[]{:S(2)}, u32[]{:S(2)}) async-start(f32[16,2,8,640]{3,2,1,0:T(8,128)} %get-tuple-element.21), calls=%async_computation.3 | async-start | bytes 1310720 | tf_op jit(solution)/shard_map/all_to_all | solution.py:743
  101.2 5.1 %mode_gradient.1 = f32[16,2,16,32,32]{4,3,2,1,0:T(8,128)} custom-call(f32[512,32]{1,0:T(8,128)S(1)} %get-tuple-element.25.spec_ref, f32[16,32,32]{2,1,0:T(8,128)S(1)} %get-tuple-element.22.dspec_ref), custom_call_target="tpu_custom_call" | custom-call | tf_op jit(solution)/shard_map/mode_gradient/pallas_call | solution.py:395
  106.2 9.7 %local_branch.3.refs_0_ = bf16[32,8,128,128]{3,2,1,0:T(8,128)(2,1)} custom-call(bf16[32,8,128,128]{3,2,1,0:T(8,128)(2,1)} %get-tuple-element.23.grad_ref.cells_ref, bf16[32,32]{1,0:T(8,128)(2,1)S(1)} %copy-done.6), custom_call_target="tpu_custom_call" | custom-call | flops 268435456 | bytes 16777216 | tf_op jit(solution)/shard_map/local_branch/pallas_call | solution.py:472
  116.0 1.8 %all-to-all-done.3.lines_ref = f32[16,2,8,640]{3,2,1,0:T(8,128)S(1)} async-done(((f32[16,2,8,640]{3,2,1,0:T(8,128)}), f32[16,2,8,640]{3,2,1,0:T(8,128)S(1)}, u32[]{:S(2)}, u32[]{:S(2)}) %all-to-all-start.3) | async-done | bytes 655392 | tf_op jit(solution)/shard_map/all_to_all | solution.py:743
  117.7 8.2 %back.1 = (bf16[32,8,128,128]{3,2,1,0:T(8,128)(2,1)}, f32[32,32]{1,0:T(8,128)}, f32[1,32]{1,0:T(1,128)}) custom-call(f32[16,2,8,640]{3,2,1,0:T(8,128)S(1)} %all-to-all-done.3.lines_ref, bf16[32,8,128,128]{3,2,1,0:T(8,128)(2,1)} %local_branch.3.refs_0_, bf16[4,256,128]{2,1,0:T(8,128)(2,1)S(1)} %copy-done.3, bf16[256,1024]{1,0:T(8,128)(2,1)S(1)} %copy-done), custom_call_target="tpu_custom_call" | custom-call | tf_op jit(solution)/shard_map/back/pallas_call | solution.py:660
  (18 shorter events, 0.1 us)
Async XLA Ops:
  0.6 29.4 %copy-start.2 = (f32[256,32]{1,0:T(8,128)S(1)}, f32[256,32]{1,0:T(8,128)}, u32[]{:S(2)}) copy-start(f32[256,32]{1,0:T(8,128)} %constant.27.clone.x_out_ref.x_in_ref) | copy-start | bytes 98308
  0.6 29.4 %copy-start.5 = (f32[256,32]{1,0:T(8,128)S(1)}, f32[256,32]{1,0:T(8,128)}, u32[]{:S(2)}) copy-start(f32[256,32]{1,0:T(8,128)} %constant.26.clone.x_in_ref) | copy-start | bytes 98308
  7.3 32.5 %copy-start.8 = (f32[32]{0:T(128)S(1)}, f32[32]{0:T(128)}, u32[]{:S(2)}) copy-start(f32[32]{0:T(128)} %param.17) | copy-start | bytes 388
  7.3 32.8 %copy-start.6 = (bf16[32,32]{1,0:T(8,128)(2,1)S(1)}, bf16[32,32]{1,0:T(8,128)(2,1)}, u32[]{:S(2)}) copy-start(bf16[32,32]{1,0:T(8,128)(2,1)} %w_ref.5) | copy-start | bytes 6148
  7.4 21.9 %all-to-all-start = ((f32[16,2,8,512]{3,2,1,0:T(8,128)}), f32[16,2,8,512]{3,2,1,0:T(8,128)S(1)}, u32[]{:S(2)}, u32[]{:S(2)}) async-start(f32[16,2,8,512]{3,2,1,0:T(8,128)} %feature_lines.1), calls=%async_computation | async-start | bytes 1048576 | tf_op jit(solution)/shard_map/all_to_all | solution.py:743
  29.2 0.8 copy-start.7
  35.7 18.6 %all-to-all-start.1 = ((f32[16,2,8,512]{3,2,1,0:T(8,128)}), f32[16,2,8,512]{3,2,1,0:T(8,128)S(1)}, u32[]{:S(2)}, u32[]{:S(2)}) async-start(f32[16,2,8,512]{3,2,1,0:T(8,128)} %get-tuple-element.18), calls=%async_computation.1 | async-start | bytes 1048576 | tf_op jit(solution)/shard_map/all_to_all | solution.py:743
  40.1 14.2 %copy-start = (bf16[256,1024]{1,0:T(8,128)(2,1)S(1)}, bf16[256,1024]{1,0:T(8,128)(2,1)}, u32[]{:S(2)}) copy-start(bf16[256,1024]{1,0:T(8,128)(2,1)} %constant.29.clone.z_out_ref.refs_2_) | copy-start | bytes 1572868
  40.1 14.2 %copy-start.1 = (bf16[8,256,128]{2,1,0:T(8,128)(2,1)S(1)}, bf16[8,256,128]{2,1,0:T(8,128)(2,1)}, u32[]{:S(2)}) copy-start(bf16[8,256,128]{2,1,0:T(8,128)(2,1)} %constant.25.clone.z_in_hbm.z_in_ref) | copy-start | bytes 1572868
  40.2 14.2 %copy-start.3 = (bf16[4,256,128]{2,1,0:T(8,128)(2,1)S(1)}, bf16[4,256,128]{2,1,0:T(8,128)(2,1)}, u32[]{:S(2)}) copy-start(bf16[4,256,128]{2,1,0:T(8,128)(2,1)} %constant.28.clone.y_out_ref.refs_1_) | copy-start | bytes 786436
  40.2 14.2 %copy-start.4 = (bf16[256,512]{1,0:T(8,128)(2,1)S(1)}, bf16[256,512]{1,0:T(8,128)(2,1)}, u32[]{:S(2)}) copy-start(bf16[256,512]{1,0:T(8,128)(2,1)} %constant.24.clone.y_in_hbm.y_in_ref) | copy-start | bytes 786436
  73.2 18.6 %all-to-all-start.2 = ((f32[16,2,8,512]{3,2,1,0:T(8,128)}), f32[16,2,8,512]{3,2,1,0:T(8,128)S(1)}, u32[]{:S(2)}, u32[]{:S(2)}) async-start(f32[16,2,8,512]{3,2,1,0:T(8,128)} %get-tuple-element.19.dlines_ref), calls=%async_computation.2 | async-start | bytes 1048576 | tf_op jit(solution)/shard_map/all_to_all | solution.py:743
  97.0 20.7 %all-to-all-start.3 = ((f32[16,2,8,640]{3,2,1,0:T(8,128)}), f32[16,2,8,640]{3,2,1,0:T(8,128)S(1)}, u32[]{:S(2)}, u32[]{:S(2)}) async-start(f32[16,2,8,640]{3,2,1,0:T(8,128)} %get-tuple-element.21), calls=%async_computation.3 | async-start | bytes 1310720 | tf_op jit(solution)/shard_map/all_to_all | solution.py:743

commit v5 on v4

--- a/solution.py
+++ b/solution.py
@@ -284,7 +284,7 @@
             pltpu.VMEM((pairs, 2 * turns, wide), F32),
             pltpu.SemaphoreType.DMA,
         ],
-        compiler_params=params(53),
+        compiler_params=params(46),
         name="mix_modes",
     )(scale, lines, packed, jnp.asarray(x_in), jnp.asarray(quad_columns(x_out, channels)))
 

time: 127 us -> 126 us (level)
  Pallas kernels: 85.1 us -> 83.2 us
    pallas_call x1, Pallas kernels: 5.68 us -> 3.79 us  [mix_modes(): pl.pallas_call(mix_kernel, in_specs=[in_vmem(), in_vmem(), in_hbm()] + [i...]
where the time goes in v5:
time: 126 us; the launch traced here: 125 us
  Pallas kernels  83.2 us (66%)
  starting transfers between devices  19.8 us (16%)
  waiting for transfers between devices  19.1 us (15%)
  local copies, waits for them, and re-layouts  1.91 us (2%)
    all_to_all x4, starting transfers between devices, swap(): return lax.all_to_all(blocks, 'mp', 0, 0, tiled=True)  19.8 us
    pallas_call x2, Pallas kernels, local_branch(): pl.pallas_call(functools.partial(local_kernel, by_column), grid=(rows //...  19.6 us
    all_to_all x4, waiting for transfers between devices, swap(): return lax.all_to_all(blocks, 'mp', 0, 0, tiled=True)  19.1 us
    pallas_call x1, Pallas kernels, slope(): pl.pallas_call(slope_kernel, in_specs=[in_vmem(), in_vmem(), in_hbm(), in...  18.8 us
    pallas_call x1, Pallas kernels, cell_sums(): pl.pallas_call(cell_sums_kernel, grid=(rows // 2,), in_specs=[cells, cell...  9.67 us
    pallas_call x1, Pallas kernels, back(): pl.pallas_call(functools.partial(back_kernel, factor, apart), in_specs=[i...  8.22 us
    pallas_call x1, Pallas kernels, feature_lines(): pl.pallas_call(lines_kernel, in_specs=[in_hbm()] * 3, out_specs=in_vmem()...  6.67 us
    pallas_call x1, Pallas kernels, pack_weights(): pl.pallas_call(pack_kernel, grid=(pairs // PER_STEP,), in_specs=[pl.Block...  6.06 us
  transfers between devices with their start and end apart: 4, of which 4 were waited for; matrix products, arithmetic and copies ran while one was open for 0% of the time, Pallas kernels for 32%

profile of v5, /device:TPU:0, one launch (start us, length us, event | category | flops | bytes accessed | tf_op | source)
XLA Modules:
  0.0 125.1 jit_solution(13003583244341406492)
XLA Ops:
  0.6 0.0 copy-start.3
  0.7 6.7 %feature_lines.1 = f32[16,2,8,512]{3,2,1,0:T(8,128)} custom-call(bf16[32,8,128,128]{3,2,1,0:T(8,128)(2,1)} %f_ref.1, bf16[256,512]{1,0:T(8,128)(2,1)} %constant.24.clone.y_in_hbm.y_in_ref, bf16[8,256,128]{2,1,0:T(8,128)(2,1)} %constant.25.clone.z_in_hbm.z_in_ref), custom_call_target="tpu_custom_call" | custom-call | tf_op jit(solution)/shard_map/feature_lines/pallas_call | solution.py:160
  7.4 7.4 %all-to-all-start = ((f32[16,2,8,512]{3,2,1,0:T(8,128)}), f32[16,2,8,512]{3,2,1,0:T(8,128)S(1)}, u32[]{:S(2)}, u32[]{:S(2)}) async-start(f32[16,2,8,512]{3,2,1,0:T(8,128)} %feature_lines.1), calls=%async_computation | async-start | bytes 1048576 | tf_op jit(solution)/shard_map/all_to_all | solution.py:743
  14.8 0.1 div.14.scale_ref
  14.9 6.1 %pack_weights.1.w_hbm = f32[16,2,4,32,128]{4,3,2,1,0:T(8,128)} custom-call(f32[16,2,16,32,32]{4,3,2,1,0:T(8,128)} %w_ref.3), custom_call_target="tpu_custom_call" | custom-call | bytes 16777216 | tf_op jit(solution)/shard_map/pack_weights/pallas_call | solution.py:211
  20.9 8.3 %all-to-all-done.lines_ref = f32[16,2,8,512]{3,2,1,0:T(8,128)S(1)} async-done(((f32[16,2,8,512]{3,2,1,0:T(8,128)}), f32[16,2,8,512]{3,2,1,0:T(8,128)S(1)}, u32[]{:S(2)}, u32[]{:S(2)}) %all-to-all-start) | async-done | bytes 524320 | tf_op jit(solution)/shard_map/all_to_all | solution.py:743
  29.2 1.6 %copy-done = f32[16,2,4,32,128]{4,3,2,1,0:T(8,128)S(1)} copy-done((f32[16,2,4,32,128]{4,3,2,1,0:T(8,128)S(1)}, f32[16,2,4,32,128]{4,3,2,1,0:T(8,128)}, u32[]{:S(2)}) %copy-start) | copy-done | bytes 2097176
  30.8 3.8 %mix_modes.1 = (f32[16,2,8,512]{3,2,1,0:T(8,128)}, f32[512,32]{1,0:T(8,128)S(1)}) custom-call(f32[1,512]{1,0:T(1,128)S(1)} %div.14.scale_ref, f32[16,2,8,512]{3,2,1,0:T(8,128)S(1)} %all-to-all-done.lines_ref, f32[16,2,4,32,128]{4,3,2,1,0:T(8,128)S(1)} %copy-done, f32[256,32]{1,0:T(8,128)S(1)} %copy-done.6, f32[256,32]{1,0:T(8,128)S(1)} %copy-done.3), custom_call_target="tpu_custom_call" | custom-call | tf_op jit(solution)/shard_map/mix_modes/pallas_call | solution.py:276
  34.6 4.1 %all-to-all-start.1 = ((f32[16,2,8,512]{3,2,1,0:T(8,128)}), f32[16,2,8,512]{3,2,1,0:T(8,128)S(1)}, u32[]{:S(2)}, u32[]{:S(2)}) async-start(f32[16,2,8,512]{3,2,1,0:T(8,128)} %get-tuple-element.18), calls=%async_computation.1 | async-start | bytes 1048576 | tf_op jit(solution)/shard_map/all_to_all | solution.py:743
  38.8 0.1 broadcast_in_dim.43
  38.9 0.1 broadcast_select_fusion
  38.9 0.1 select_n.31.bias_ref
  39.1 9.9 %local_branch.2.local_hbm = bf16[32,8,128,128]{3,2,1,0:T(8,128)(2,1)} custom-call(bf16[32,8,128,128]{3,2,1,0:T(8,128)(2,1)} %f_ref.1, bf16[32,32]{1,0:T(8,128)(2,1)S(1)} %copy-done.7), custom_call_target="tpu_custom_call" | custom-call | flops 268435456 | bytes 16777216 | tf_op jit(solution)/shard_map/local_branch/pallas_call | solution.py:472
  48.9 4.3 %all-to-all-done.1.lines_ref = f32[16,2,8,512]{3,2,1,0:T(8,128)S(1)} async-done(((f32[16,2,8,512]{3,2,1,0:T(8,128)}), f32[16,2,8,512]{3,2,1,0:T(8,128)S(1)}, u32[]{:S(2)}, u32[]{:S(2)}) %all-to-all-start.1) | async-done | bytes 524320 | tf_op jit(solution)/shard_map/all_to_all | solution.py:743
  53.2 18.8 %slope.1 = (bf16[32,8,128,128]{3,2,1,0:T(8,128)(2,1)}, f32[16,2,8,512]{3,2,1,0:T(8,128)}) custom-call(f32[1,512]{1,0:T(1,128)S(1)} %select_n.31.bias_ref, f32[16,2,8,512]{3,2,1,0:T(8,128)S(1)} %all-to-all-done.1.lines_ref, bf16[32,8,128,128]{3,2,1,0:T(8,128)(2,1)} %local_branch.2.local_hbm, bf16[32,8,128,128]{3,2,1,0:T(8,128)(2,1)} %cot_hbm.1, ...), custom_call_target="tpu_custom_call" | custom-call | tf_op jit(solution)/shard_map/slope/pallas_call | solution.py:599
  72.1 4.2 %all-to-all-start.2 = ((f32[16,2,8,512]{3,2,1,0:T(8,128)}), f32[16,2,8,512]{3,2,1,0:T(8,128)S(1)}, u32[]{:S(2)}, u32[]{:S(2)}) async-start(f32[16,2,8,512]{3,2,1,0:T(8,128)} %get-tuple-element.19.dlines_ref), calls=%async_computation.2 | async-start | bytes 1048576 | tf_op jit(solution)/shard_map/all_to_all | solution.py:743
  76.2 9.7 %cell_sums.1.sums_ref = f32[2,8,128]{2,1,0:T(8,128)S(1)} custom-call(bf16[32,8,128,128]{3,2,1,0:T(8,128)(2,1)} %get-tuple-element.23.grad_ref.cells_ref, bf16[32,8,128,128]{3,2,1,0:T(8,128)(2,1)} %f_ref.1, f32[16,2,8,512]{3,2,1,0:T(8,128)} %get-tuple-element.19.dlines_ref), custom_call_target="tpu_custom_call" | custom-call | tf_op jit(solution)/shard_map/cell_sums/pallas_call | solution.py:730
  85.9 4.8 %all-to-all-done.2.lines_ref = f32[16,2,8,512]{3,2,1,0:T(8,128)S(1)} async-done(((f32[16,2,8,512]{3,2,1,0:T(8,128)}), f32[16,2,8,512]{3,2,1,0:T(8,128)S(1)}, u32[]{:S(2)}, u32[]{:S(2)}) %all-to-all-start.2) | async-done | bytes 524320 | tf_op jit(solution)/shard_map/all_to_all | solution.py:743
  90.7 5.2 %adjoint_modes.1 = (f32[16,2,8,640]{3,2,1,0:T(8,128)}, f32[16,32,32]{2,1,0:T(8,128)S(1)}) custom-call(f32[1,512]{1,0:T(1,128)S(1)} %div.14.scale_ref, f32[16,2,8,512]{3,2,1,0:T(8,128)S(1)} %all-to-all-done.2.lines_ref, f32[16,2,4,32,128]{4,3,2,1,0:T(8,128)} %pack_weights.1.w_hbm, f32[256,32]{1,0:T(8,128)S(1)} %copy-done.3, f32[256,32]{1,0:T(8,128)S(1)} %copy-done.3, ...), custom_call_target="tpu_custom_call" | custom-call | tf_op jit(solution)/shard_map/adjoint_modes/pallas_call | solution.py:346
  96.0 4.1 %all-to-all-start.3 = ((f32[16,2,8,640]{3,2,1,0:T(8,128)}), f32[16,2,8,640]{3,2,1,0:T(8,128)S(1)}, u32[]{:S(2)}, u32[]{:S(2)}) async-start(f32[16,2,8,640]{3,2,1,0:T(8,128)} %get-tuple-element.21), calls=%async_computation.3 | async-start | bytes 1310720 | tf_op jit(solution)/shard_map/all_to_all | solution.py:743
  100.1 5.1 %mode_gradient.1 = f32[16,2,16,32,32]{4,3,2,1,0:T(8,128)} custom-call(f32[512,32]{1,0:T(8,128)S(1)} %get-tuple-element.25.spec_ref, f32[16,32,32]{2,1,0:T(8,128)S(1)} %get-tuple-element.22.dspec_ref), custom_call_target="tpu_custom_call" | custom-call | tf_op jit(solution)/shard_map/mode_gradient/pallas_call | solution.py:395
  105.2 9.7 %local_branch.3.refs_0_ = bf16[32,8,128,128]{3,2,1,0:T(8,128)(2,1)} custom-call(bf16[32,8,128,128]{3,2,1,0:T(8,128)(2,1)} %get-tuple-element.23.grad_ref.cells_ref, bf16[32,32]{1,0:T(8,128)(2,1)S(1)} %copy-done.7), custom_call_target="tpu_custom_call" | custom-call | flops 268435456 | bytes 16777216 | tf_op jit(solution)/shard_map/local_branch/pallas_call | solution.py:472
  114.9 1.8 %all-to-all-done.3.lines_ref = f32[16,2,8,640]{3,2,1,0:T(8,128)S(1)} async-done(((f32[16,2,8,640]{3,2,1,0:T(8,128)}), f32[16,2,8,640]{3,2,1,0:T(8,128)S(1)}, u32[]{:S(2)}, u32[]{:S(2)}) %all-to-all-start.3) | async-done | bytes 655392 | tf_op jit(solution)/shard_map/all_to_all | solution.py:743
  116.7 8.2 %back.1 = (bf16[32,8,128,128]{3,2,1,0:T(8,128)(2,1)}, f32[32,32]{1,0:T(8,128)}, f32[1,32]{1,0:T(1,128)}) custom-call(f32[16,2,8,640]{3,2,1,0:T(8,128)S(1)} %all-to-all-done.3.lines_ref, bf16[32,8,128,128]{3,2,1,0:T(8,128)(2,1)} %local_branch.3.refs_0_, bf16[4,256,128]{2,1,0:T(8,128)(2,1)S(1)} %copy-done.4, bf16[256,1024]{1,0:T(8,128)(2,1)S(1)} %copy-done.1), custom_call_target="tpu_custom_call" | custom-call | tf_op jit(solution)/shard_map/back/pallas_call | solution.py:660
  (18 shorter events, 0.1 us)
Async XLA Ops:
  0.6 28.6 %copy-start.3 = (f32[256,32]{1,0:T(8,128)S(1)}, f32[256,32]{1,0:T(8,128)}, u32[]{:S(2)}) copy-start(f32[256,32]{1,0:T(8,128)} %constant.27.clone.x_out_ref.x_in_ref) | copy-start | bytes 98308
  0.6 28.6 %copy-start.6 = (f32[256,32]{1,0:T(8,128)S(1)}, f32[256,32]{1,0:T(8,128)}, u32[]{:S(2)}) copy-start(f32[256,32]{1,0:T(8,128)} %constant.26.clone.x_in_ref) | copy-start | bytes 98308
  7.3 31.4 %copy-start.8 = (f32[32]{0:T(128)S(1)}, f32[32]{0:T(128)}, u32[]{:S(2)}) copy-start(f32[32]{0:T(128)} %param.17) | copy-start | bytes 388
  7.3 31.7 %copy-start.7 = (bf16[32,32]{1,0:T(8,128)(2,1)S(1)}, bf16[32,32]{1,0:T(8,128)(2,1)}, u32[]{:S(2)}) copy-start(bf16[32,32]{1,0:T(8,128)(2,1)} %w_ref.5) | copy-start | bytes 6148
  7.4 21.9 %all-to-all-start = ((f32[16,2,8,512]{3,2,1,0:T(8,128)}), f32[16,2,8,512]{3,2,1,0:T(8,128)S(1)}, u32[]{:S(2)}, u32[]{:S(2)}) async-start(f32[16,2,8,512]{3,2,1,0:T(8,128)} %feature_lines.1), calls=%async_computation | async-start | bytes 1048576 | tf_op jit(solution)/shard_map/all_to_all | solution.py:743
  29.2 1.6 %copy-start = (f32[16,2,4,32,128]{4,3,2,1,0:T(8,128)S(1)}, f32[16,2,4,32,128]{4,3,2,1,0:T(8,128)}, u32[]{:S(2)}) copy-start(f32[16,2,4,32,128]{4,3,2,1,0:T(8,128)} %pack_weights.1.w_hbm) | copy-start | bytes 6291460
  34.6 18.6 %all-to-all-start.1 = ((f32[16,2,8,512]{3,2,1,0:T(8,128)}), f32[16,2,8,512]{3,2,1,0:T(8,128)S(1)}, u32[]{:S(2)}, u32[]{:S(2)}) async-start(f32[16,2,8,512]{3,2,1,0:T(8,128)} %get-tuple-element.18), calls=%async_computation.1 | async-start | bytes 1048576 | tf_op jit(solution)/shard_map/all_to_all | solution.py:743
  39.0 14.2 %copy-start.1 = (bf16[256,1024]{1,0:T(8,128)(2,1)S(1)}, bf16[256,1024]{1,0:T(8,128)(2,1)}, u32[]{:S(2)}) copy-start(bf16[256,1024]{1,0:T(8,128)(2,1)} %constant.29.clone.z_out_ref.refs_2_) | copy-start | bytes 1572868
  39.0 14.2 %copy-start.2 = (bf16[8,256,128]{2,1,0:T(8,128)(2,1)S(1)}, bf16[8,256,128]{2,1,0:T(8,128)(2,1)}, u32[]{:S(2)}) copy-start(bf16[8,256,128]{2,1,0:T(8,128)(2,1)} %constant.25.clone.z_in_hbm.z_in_ref) | copy-start | bytes 1572868
  39.1 14.2 %copy-start.4 = (bf16[4,256,128]{2,1,0:T(8,128)(2,1)S(1)}, bf16[4,256,128]{2,1,0:T(8,128)(2,1)}, u32[]{:S(2)}) copy-start(bf16[4,256,128]{2,1,0:T(8,128)(2,1)} %constant.28.clone.y_out_ref.refs_1_) | copy-start | bytes 786436
  39.1 14.2 %copy-start.5 = (bf16[256,512]{1,0:T(8,128)(2,1)S(1)}, bf16[256,512]{1,0:T(8,128)(2,1)}, u32[]{:S(2)}) copy-start(bf16[256,512]{1,0:T(8,128)(2,1)} %constant.24.clone.y_in_hbm.y_in_ref) | copy-start | bytes 786436
  72.1 18.6 %all-to-all-start.2 = ((f32[16,2,8,512]{3,2,1,0:T(8,128)}), f32[16,2,8,512]{3,2,1,0:T(8,128)S(1)}, u32[]{:S(2)}, u32[]{:S(2)}) async-start(f32[16,2,8,512]{3,2,1,0:T(8,128)} %get-tuple-element.19.dlines_ref), calls=%async_computation.2 | async-start | bytes 1048576 | tf_op jit(solution)/shard_map/all_to_all | solution.py:743
  96.0 20.7 %all-to-all-start.3 = ((f32[16,2,8,640]{3,2,1,0:T(8,128)}), f32[16,2,8,640]{3,2,1,0:T(8,128)S(1)}, u32[]{:S(2)}, u32[]{:S(2)}) async-start(f32[16,2,8,640]{3,2,1,0:T(8,128)} %get-tuple-element.21), calls=%async_computation.3 | async-start | bytes 1310720 | tf_op jit(solution)/shard_map/all_to_all | solution.py:743
